TPU v7x, 32 devices: a whole 2x2x4 slice. The times are simulated.
32 devices in a mesh: batch: 4 (over x, core), seq: 8 (over z, y).
Axes of the slice: x: 2, y: 2, z: 4, core: 2. Of those that a mesh axis runs over, the one named last changes fastest.
Arguments:
- block_in: bfloat16 [8, 2048, 1536], P('batch', 'seq'), may hold values from -6 to 6
- lengths: int32 [8], replicated, may hold values from 512 to 2048, as said below
- norm_gain: bfloat16 [1536], P(('batch', 'seq')), may hold values from 0.5 to 1.5
- in_weight: bfloat16 [1536, 6448], P(('batch', 'seq')), may hold values from -0.15625 to 0.15625
- conv_weight: bfloat16 [4, 3328], P(None, ('batch', 'seq')), may hold values from -3 to 3
- conv_bias: bfloat16 [3328], P(('batch', 'seq')), may hold values from -3 to 3
- step_bias: float32 [48], replicated, may hold values from -8 to -3
- decay_log: float32 [48], replicated, may hold values from 0 to 2.77
- skip_gain: float32 [48], replicated, may hold values from 0.5 to 1.5
- out_gain: bfloat16 [3072], P(('batch', 'seq')), may hold values from 0.5 to 1.5
- out_weight: bfloat16 [3072, 1536], P(('batch', 'seq')), may hold values from -0.109375 to 0.109375
- grad_out: bfloat16 [8, 2048, 1536], P('batch', 'seq'), may hold values from -6 to 6
Outputs:
- block_out: bfloat16 [8, 2048, 1536], P('batch', 'seq')
- grad_in: bfloat16 [8, 2048, 1536], P('batch', 'seq')
- grad_norm_gain: float32 [1536], P(('batch', 'seq'))
- grad_in_weight: float32 [1536, 6448], P(('batch', 'seq'))
- grad_conv_weight: float32 [4, 3328], P(None, ('batch', 'seq'))
- grad_conv_bias: float32 [3328], P(('batch', 'seq'))
- grad_step_bias: float32 [48], replicated
- grad_decay_log: float32 [48], replicated
- grad_skip_gain: float32 [48], replicated
- grad_out_gain: float32 [3072], P(('batch', 'seq'))
- grad_out_weight: float32 [3072, 1536], P(('batch', 'seq'))
- rms_stats: float32 [3], replicated
Inputs may be any that keep to these rules, and one draw needn't show every extreme that they name: `lengths`: among the 2 slots of each batch index, one drawn from the seed has length 2048.
All inputs are finite; a program needn't handle non-finite values.
Results may differ from a plain program's by a relative error of at most 0.0064.
Values may be sent and summed in bfloat16 or wider, within the bound.
No kernel may reach another device: no remote copies, remote signals or barrier semaphores. Data moves between devices by JAX's collectives and lax.ppermute only.
A program may use at most 256 MiB of HBM per device.

v0:
```python
import jax
import jax.numpy as jnp
from jax import lax
from jax.sharding import PartitionSpec as P

H = 48
P_SIZE = 64
NS = 128
CONV = 4
SPAN = 256
E = 3072
CH = 3328


EPSILON = 1e-05
PRECISE = lax.Precision.HIGHEST


def shifted(block, axis, distance):
    devices = range(lax.axis_size(axis))
    route = [(i - distance, i) for i in devices if i - distance in devices]
    return lax.ppermute(block, axis, route)


def pre_norm(residual, gain_vec):
    inv_scale = lax.rsqrt(jnp.mean(residual * residual, axis=-1, keepdims=True) + EPSILON)
    return residual * inv_scale * gain_vec


def gate_norm(ssm_out, gate_in, gain_vec):
    gated_out = ssm_out * jax.nn.silu(gate_in)
    inv_scale = lax.rsqrt(jnp.mean(gated_out * gated_out, axis=-1, keepdims=True) + EPSILON)
    return gated_out * inv_scale * gain_vec


def conv_apply(padded, weight, bias_vec, row_count):
    running = bias_vec
    for offset in range(CONV):
        running = running + weight[offset] * padded[..., offset : offset + row_count, :]
    return jax.nn.silu(running)


def conv_local(prev_rows, conv_in, weight, bias_vec):
    padded = jnp.concatenate([prev_rows, conv_in], axis=1)
    return conv_apply(padded, weight, bias_vec, conv_in.shape[1])


def unpack_slot(conv_out, step_raw, step_bias, decay_log):
    row_count = conv_out.shape[0]
    heads_in = conv_out[:, :E].reshape(row_count, H, P_SIZE)
    write_vec = conv_out[:, E : E + NS]
    read_vec = conv_out[:, E + NS :]
    step_size = jax.nn.softplus(step_raw + step_bias)
    log_decay = -step_size * jnp.exp(decay_log)
    return (heads_in, write_vec, read_vec, step_size, log_decay)


def intra_part(heads_in, write_vec, read_vec, step_size, log_decay):
    row_count = heads_in.shape[0]
    cumulative = jnp.cumsum(log_decay, axis=0)
    causal = jnp.arange(row_count)[:, None] >= jnp.arange(row_count)[None, :]
    differ = cumulative[:, None, :] - cumulative[None, :, :]
    segment = jnp.exp(jnp.where(causal[:, :, None], differ, -jnp.inf))
    intersection = jnp.dot(read_vec, write_vec.T, precision=PRECISE)
    mixing = segment * intersection[:, :, None] * step_size[None, :, :]
    inner_out = jnp.einsum("tsh,shp->thp", mixing, heads_in, precision=PRECISE)
    tail_weight = jnp.exp(cumulative[-1][None, :] - cumulative) * step_size
    fresh_state = jnp.einsum("sh,shp,sn->hpn", tail_weight, heads_in, write_vec, precision=PRECISE)
    return (cumulative, inner_out, fresh_state)


def finish_part(carry_state, cumulative, read_vec, inner_out, fresh_state):
    from_state = jnp.exp(cumulative)[:, :, None] * jnp.einsum(
        "tn,hpn->thp", read_vec, carry_state, precision=PRECISE
    )
    next_state = jnp.exp(cumulative[-1])[:, None, None] * carry_state + fresh_state
    return (next_state, inner_out + from_state)


def local_scan(heads_in, write_vec, read_vec, step_size, log_decay, carry_state):
    row_count = heads_in.shape[0]
    block_rows = min(row_count, SPAN)
    blocks = row_count // block_rows

    def block_step(running_state, block_item):
        heads_part, write_part, read_part, step_part, decay_part = block_item
        cumulative, inner_out, fresh_state = intra_part(
            heads_part, write_part, read_part, step_part, decay_part
        )
        return finish_part(running_state, cumulative, read_part, inner_out, fresh_state)

    final_state, mixed_out = lax.scan(
        block_step,
        carry_state,
        (
            heads_in.reshape(blocks, block_rows, H, P_SIZE),
            write_vec.reshape(blocks, block_rows, NS),
            read_vec.reshape(blocks, block_rows, NS),
            step_size.reshape(blocks, block_rows, H),
            log_decay.reshape(blocks, block_rows, H),
        ),
    )
    return (final_state, mixed_out.reshape(row_count, H, P_SIZE))


def ssm_slot(conv_slot, raw_slot, step_bias, decay_log, skip_gain, carry_state):
    row_count = conv_slot.shape[0]
    heads_in, write_vec, read_vec, step_size, log_decay = unpack_slot(
        conv_slot, raw_slot, step_bias, decay_log
    )
    next_state, mixed_out = local_scan(
        heads_in, write_vec, read_vec, step_size, log_decay, carry_state
    )
    return (next_state, (mixed_out + skip_gain[:, None] * heads_in).reshape(row_count, E))


def shards(
    block_in,
    lengths,
    norm_gain,
    in_weight,
    conv_weight,
    conv_bias,
    step_bias,
    decay_log,
    skip_gain,
    out_gain,
    out_weight,
    grad_out,
):
    slot_count, row_count, feature_count = block_in.shape
    gathered = (
        lax.all_gather(norm_gain, ("batch", "seq"), axis=0, tiled=True),
        lax.all_gather(in_weight, ("batch", "seq"), axis=0, tiled=True),
        lax.all_gather(conv_weight, ("batch", "seq"), axis=1, tiled=True),
        lax.all_gather(conv_bias, ("batch", "seq"), axis=0, tiled=True),
        lax.all_gather(out_gain, ("batch", "seq"), axis=0, tiled=True),
        lax.all_gather(out_weight, ("batch", "seq"), axis=0, tiled=True),
    )
    full_in = gathered[1]
    full_out = gathered[5]
    gain_in = gathered[0].astype(jnp.float32)
    conv_taps = gathered[2].astype(jnp.float32)
    conv_shift = gathered[3].astype(jnp.float32)
    gain_out = gathered[4].astype(jnp.float32)
    residual = block_in.astype(jnp.float32).reshape(slot_count * row_count, feature_count)
    local_lengths = lax.dynamic_slice_in_dim(
        lengths, lax.axis_index("batch") * slot_count, slot_count
    )
    positions = lax.axis_index("seq") * row_count + jnp.arange(row_count, dtype=jnp.int32)
    valid_mask = (
        (positions[None, :] < local_lengths[:, None])
        .astype(jnp.float32)
        .reshape(slot_count * row_count, 1)
    )
    normed = pre_norm(residual, gain_in).astype(jnp.bfloat16)
    projected = jnp.dot(normed, full_in, preferred_element_type=jnp.float32)
    gate_in = projected[:, :E]
    conv_in = projected[:, E : E + CH].reshape(slot_count, row_count, CH)
    step_raw = projected[:, E + CH :].reshape(slot_count, row_count, H)
    prev_rows = shifted(conv_in[:, row_count - (CONV - 1) :, :], "seq", 1)
    conv_out = conv_local(prev_rows, conv_in, conv_taps, conv_shift)

    def forward_slot(slot_item):
        conv_slot, raw_slot = slot_item
        heads_in, write_vec, read_vec, step_size, log_decay = unpack_slot(
            conv_slot, raw_slot, step_bias, decay_log
        )
        fresh_state, inner_out = local_scan(
            heads_in,
            write_vec,
            read_vec,
            step_size,
            log_decay,
            jnp.zeros((H, P_SIZE, NS), jnp.float32),
        )
        cumulative = jnp.cumsum(log_decay, axis=0)
        return (jnp.exp(cumulative[-1]), fresh_state, cumulative, inner_out)

    chain_decay, fresh_state, cumulative, inner_out = lax.map(forward_slot, (conv_out, step_raw))

    def forward_hop(hop_index, hop_carry):
        incoming, outgoing = hop_carry
        incoming = shifted(outgoing, "seq", 1)
        return (incoming, chain_decay[..., None, None] * incoming + fresh_state)

    state_in, _ = lax.fori_loop(
        0, lax.axis_size("seq") - 1, forward_hop, (jnp.zeros_like(fresh_state), fresh_state)
    )

    def finish_slot(slot_item):
        carry_state, cum_slot, conv_slot, inner_slot, fresh_slot = slot_item
        heads_in = conv_slot[:, :E].reshape(row_count, H, P_SIZE)
        _, mixed_out = finish_part(
            carry_state, cum_slot, conv_slot[:, E + NS :], inner_slot, fresh_slot
        )
        return (mixed_out + skip_gain[:, None] * heads_in).reshape(row_count, E)

    ssm_out = lax.map(
        finish_slot, (state_in, cumulative, conv_out, inner_out, fresh_state)
    ).reshape(slot_count * row_count, E)
    mixer_in = gate_norm(ssm_out, gate_in, gain_out).astype(jnp.bfloat16)
    mixer_out = jnp.dot(mixer_in, full_out, preferred_element_type=jnp.float32)
    block_value = valid_mask * (residual + mixer_out)
    block_out = block_value.astype(jnp.bfloat16).reshape(slot_count, row_count, feature_count)
    local_sums = jnp.stack(
        [
            jnp.sum(valid_mask * residual * residual),
            jnp.sum(valid_mask * mixer_out * mixer_out),
            jnp.sum(block_value * block_value),
        ]
    )
    regathered = (
        lax.all_gather(norm_gain, ("batch", "seq"), axis=0, tiled=True),
        lax.all_gather(in_weight, ("batch", "seq"), axis=0, tiled=True),
        lax.all_gather(conv_weight, ("batch", "seq"), axis=1, tiled=True),
        lax.all_gather(conv_bias, ("batch", "seq"), axis=0, tiled=True),
        lax.all_gather(out_gain, ("batch", "seq"), axis=0, tiled=True),
        lax.all_gather(out_weight, ("batch", "seq"), axis=0, tiled=True),
    )
    back_in = regathered[1]
    back_out = regathered[5]
    back_gain_in = regathered[0].astype(jnp.float32)
    back_taps = regathered[2].astype(jnp.float32)
    back_shift = regathered[3].astype(jnp.float32)
    back_gain_out = regathered[4].astype(jnp.float32)
    d_mix = valid_mask * grad_out.astype(jnp.float32).reshape(slot_count * row_count, feature_count)
    d_mix_low = d_mix.astype(jnp.bfloat16)
    grad_out_w = jnp.dot(mixer_in.T, d_mix_low, preferred_element_type=jnp.float32)
    d_mixer_in = jnp.dot(d_mix_low, back_out.T, preferred_element_type=jnp.float32)
    _, pull_gate = jax.vjp(gate_norm, ssm_out, gate_in, back_gain_out)
    d_ssm, d_gate_in, grad_gain_out = pull_gate(d_mixer_in)
    d_ssm_slots = d_ssm.reshape(slot_count, row_count, E)
    local_grad_state = jnp.einsum(
        "sth,sthp,stn->shpn",
        jnp.exp(cumulative),
        d_ssm_slots.reshape(slot_count, row_count, H, P_SIZE),
        conv_out[:, :, E + NS :],
        precision=PRECISE,
    )

    def backward_hop(hop_index, hop_carry):
        incoming, outgoing = hop_carry
        incoming = shifted(outgoing, "seq", -1)
        return (incoming, chain_decay[..., None, None] * incoming + local_grad_state)

    carried, _ = lax.fori_loop(
        0,
        lax.axis_size("seq") - 1,
        backward_hop,
        (jnp.zeros_like(local_grad_state), local_grad_state),
    )

    def backward_slot(slot_item):
        conv_slot, raw_slot, carry_state, carried_slot, d_slot = slot_item
        _, pull_ssm = jax.vjp(
            ssm_slot, conv_slot, raw_slot, step_bias, decay_log, skip_gain, carry_state
        )
        d_conv_slot, d_raw_slot, grad_bias, grad_log, grad_skip, _ = pull_ssm(
            (carried_slot, d_slot)
        )
        return (d_conv_slot, d_raw_slot, grad_bias, grad_log, grad_skip)

    d_conv_out, d_step_raw, bias_terms, log_terms, skip_terms = lax.map(
        backward_slot, (conv_out, step_raw, state_in, carried, d_ssm_slots)
    )
    _, pull_conv = jax.vjp(conv_local, prev_rows, conv_in, back_taps, back_shift)
    d_prev_rows, d_conv_in, grad_conv_w, grad_conv_b = pull_conv(d_conv_out)
    returned_rows = shifted(d_prev_rows.astype(jnp.bfloat16), "seq", -1).astype(d_prev_rows.dtype)
    d_conv_in = jnp.concatenate(
        [
            d_conv_in[:, : row_count - (CONV - 1)],
            d_conv_in[:, row_count - (CONV - 1) :] + returned_rows,
        ],
        axis=1,
    )
    d_projected = jnp.concatenate(
        [
            d_gate_in,
            d_conv_in.reshape(slot_count * row_count, CH),
            d_step_raw.reshape(slot_count * row_count, H),
        ],
        axis=1,
    ).astype(jnp.bfloat16)
    grad_in_w = jnp.dot(normed.T, d_projected, preferred_element_type=jnp.float32)
    d_normed = jnp.dot(d_projected, back_in.T, preferred_element_type=jnp.float32)
    _, pull_norm = jax.vjp(pre_norm, residual, back_gain_in)
    d_resid, grad_gain_in = pull_norm(d_normed)
    grad_in = (d_mix + d_resid).astype(jnp.bfloat16).reshape(slot_count, row_count, feature_count)
    shares = (
        lax.psum_scatter(grad_gain_in, ("batch", "seq"), scatter_dimension=0, tiled=True),
        lax.psum_scatter(grad_in_w, ("batch", "seq"), scatter_dimension=0, tiled=True),
        lax.psum_scatter(grad_conv_w, ("batch", "seq"), scatter_dimension=1, tiled=True),
        lax.psum_scatter(grad_conv_b, ("batch", "seq"), scatter_dimension=0, tiled=True),
        lax.psum_scatter(grad_gain_out, ("batch", "seq"), scatter_dimension=0, tiled=True),
        lax.psum_scatter(grad_out_w, ("batch", "seq"), scatter_dimension=0, tiled=True),
    )
    bias_local = jnp.sum(bias_terms, axis=0)
    log_local = jnp.sum(log_terms, axis=0)
    skip_local = jnp.sum(skip_terms, axis=0)
    grad_step, grad_decay, grad_skip, valid_sums = lax.psum(
        (bias_local, log_local, skip_local, local_sums), ("batch", "seq")
    )
    token_total = jnp.sum(lengths).astype(jnp.float32) * feature_count
    rms_stats = jnp.sqrt(valid_sums / token_total)
    return (
        block_out,
        grad_in,
        shares[0],
        shares[1],
        shares[2],
        shares[3],
        grad_step,
        grad_decay,
        grad_skip,
        shares[4],
        shares[5],
        rms_stats,
    )


def solution(mesh):
    return jax.shard_map(
        shards,
        mesh=mesh,
        in_specs=(
            P("batch", "seq", None),
            P(),
            P(("batch", "seq")),
            P(("batch", "seq"), None),
            P(None, ("batch", "seq")),
            P(("batch", "seq")),
            P(),
            P(),
            P(),
            P(("batch", "seq")),
            P(("batch", "seq"), None),
            P("batch", "seq", None),
        ),
        out_specs=(
            P("batch", "seq", None),
            P("batch", "seq", None),
            P(("batch", "seq")),
            P(("batch", "seq"), None),
            P(None, ("batch", "seq")),
            P(("batch", "seq")),
            P(),
            P(),
            P(),
            P(("batch", "seq")),
            P(("batch", "seq"), None),
            P(),
        ),
        check_vma=False,
    )
```

profile of v0, /device:TPU:0, one launch (start us, length us, event | category | flops | bytes accessed | tf_op | source)
XLA Modules:
  0.0 2647.6 jit_solution(17457075887192178467)
XLA Ops:
  12.2 43.2 %all-reduce.21 = (bf16[1536]{0:T(1024)(128)(2,1)S(1)}, bf16[3328]{0:T(1024)(128)(2,1)S(1)}, bf16[3072]{0:T(1024)(128)(2,1)S(1)}) all-reduce(bf16[1536]{0:T(1024)(128)(2,1)S(1)} %dynamic-update-slice, bf16[3328]{0:T(1024)(128)(2,1)S(1)} %dynamic-update-slice.1, ...), channel_id=1, replica_groups=mesh['batch'=4,'seq'=8] {'batch','seq'}, use_global_device_ids=true, to_apply=%add.13 | all-reduce | flops 7936 | bytes 31744
  59.7 66.9 %all-gather = bf16[32,104,4]{1,2,0:T(4,128)(2,1)S(1)} all-gather(bf16[1,104,4]{1,2,0:T(4,128)(2,1)} %bitcast.484), channel_id=1, replica_groups=mesh['batch'=4,'seq'=8] {'batch','seq'}, dimensions={0}, use_global_device_ids=true | all-gather | bytes 27456 | tf_op jit(solution)/shard_map/all_gather | solution.py:135
  129.6 16.0 all-gather.4.cloned.1.call-done
  145.7 17.6 fusion.139
  184.1 15.4 fusion.103
  202.2 80.2 %while.20 = (s32[]{:T(128)}, f32[2,48]{1,0:T(2,128)}, f32[2,48,64,128]{3,2,1,0:T(8,128)}, f32[2,256,48]{1,2,0:T(8,128)}, f32[2,256,48,64]{1,3,2,0:T(8,128)}, /*i...) while((s32[]{:T(128)}, f32[2,48]{1,0:T(2,128)}, ...), condition=%wide.region_4.5_spmd, body=%wide.region_1.4_spmd.sunk | while | flops 4949807104 | bytes 52293004 | solution.py:180
  226.7 15.6 bitcast_dynamic-update-slice_fusion.9
  266.7 15.6 bitcast_dynamic-update-slice_fusion.9
  288.4 522.7 %while.21 = (s32[]{:T(128)}, f32[2,48,64,128]{3,2,1,0:T(8,128)}, f32[2,48,64,128]{3,2,1,0:T(8,128)}, f32[2,48]{1,0:T(2,128)}, f32[2,48,64,128]{3,2,1,0:T(8,128)}, /*index=5*/s32[]{:T(128)}) while((s32[]{:T(128)}, f32[2,48,64,128]{3,2,1,0:T(8,128)}, f32[2,48,64,128]{3,2,1,0:T(8,128)}, f32[2,48]{1,0:T(2,128)}, f32[2,48,64,128]{3,2,1,0:T(8,128)}, ...), condition=%wide.region_6.7_spmd, body=%wide.region_5.6_spmd.sunk | while | flops 1572866 | bytes 34603528 | solution.py:187
  292.7 67.5 %collective-permute-done = f32[2,48,64,128]{3,2,1,0:T(8,128)S(1)} collective-permute-done((f32[2,48,64,128]{3,2,1,0:T(8,128)}, f32[2,48,64,128]{3,2,1,0:T(8,128)S(1)}, u32[]{:S(2)}, u32[]{:S(2)}) %collective-permute-start) | collective-permute-done | bytes 3145760 | tf_op jit(solution)/shard_map/while/body/eval_jaxpr/ppermute | solution.py:22
  370.1 66.2 %collective-permute-done = f32[2,48,64,128]{3,2,1,0:T(8,128)S(1)} collective-permute-done((f32[2,48,64,128]{3,2,1,0:T(8,128)}, f32[2,48,64,128]{3,2,1,0:T(8,128)S(1)}, u32[]{:S(2)}, u32[]{:S(2)}) %collective-permute-start) | collective-permute-done | bytes 3145760 | tf_op jit(solution)/shard_map/while/body/eval_jaxpr/ppermute | solution.py:22
  446.8 65.3 %collective-permute-done = f32[2,48,64,128]{3,2,1,0:T(8,128)S(1)} collective-permute-done((f32[2,48,64,128]{3,2,1,0:T(8,128)}, f32[2,48,64,128]{3,2,1,0:T(8,128)S(1)}, u32[]{:S(2)}, u32[]{:S(2)}) %collective-permute-start) | collective-permute-done | bytes 3145760 | tf_op jit(solution)/shard_map/while/body/eval_jaxpr/ppermute | solution.py:22
  522.6 64.4 %collective-permute-done = f32[2,48,64,128]{3,2,1,0:T(8,128)S(1)} collective-permute-done((f32[2,48,64,128]{3,2,1,0:T(8,128)}, f32[2,48,64,128]{3,2,1,0:T(8,128)S(1)}, u32[]{:S(2)}, u32[]{:S(2)}) %collective-permute-start) | collective-permute-done | bytes 3145760 | tf_op jit(solution)/shard_map/while/body/eval_jaxpr/ppermute | solution.py:22
  597.4 63.5 %collective-permute-done = f32[2,48,64,128]{3,2,1,0:T(8,128)S(1)} collective-permute-done((f32[2,48,64,128]{3,2,1,0:T(8,128)}, f32[2,48,64,128]{3,2,1,0:T(8,128)S(1)}, u32[]{:S(2)}, u32[]{:S(2)}) %collective-permute-start) | collective-permute-done | bytes 3145760 | tf_op jit(solution)/shard_map/while/body/eval_jaxpr/ppermute | solution.py:22
  671.4 62.5 %collective-permute-done = f32[2,48,64,128]{3,2,1,0:T(8,128)S(1)} collective-permute-done((f32[2,48,64,128]{3,2,1,0:T(8,128)}, f32[2,48,64,128]{3,2,1,0:T(8,128)S(1)}, u32[]{:S(2)}, u32[]{:S(2)}) %collective-permute-start) | collective-permute-done | bytes 3145760 | tf_op jit(solution)/shard_map/while/body/eval_jaxpr/ppermute | solution.py:22
  744.4 61.6 %collective-permute-done = f32[2,48,64,128]{3,2,1,0:T(8,128)S(1)} collective-permute-done((f32[2,48,64,128]{3,2,1,0:T(8,128)}, f32[2,48,64,128]{3,2,1,0:T(8,128)S(1)}, u32[]{:S(2)}, u32[]{:S(2)}) %collective-permute-start) | collective-permute-done | bytes 3145760 | tf_op jit(solution)/shard_map/while/body/eval_jaxpr/ppermute | solution.py:22
  811.1 180.4 %while.22 = (s32[]{:T(128)}, f32[2,256,3072]{1,0,2:T(2,128)}, f32[2,256,48,64]{1,3,2,0:T(8,128)}, f32[2,256,48]{1,2,0:T(8,128)S(1)}, f32[2,256,3328]{2,1,0:T(8,1...) while((s32[]{:T(128)}, f32[2,256,3072]{1,0,2:T(2,128)}, ...), condition=%wide.region_8.9_spmd, body=%wide.region_7.8_spmd.sunk | while | flops 1211105280 | bytes 69486248 | solution.py:199
  826.2 12.8 copy.376
  839.0 62.4 %dynamic_update_slice.131 = f32[2,256,3072]{1,0,2:T(2,128)} dynamic-update-slice(f32[2,256,3072]{1,0,2:T(2,128)} %get-tuple-element.1321, f32[1,256,3072]{1,0,2:T(1,128)S(1)} %copy.376, s32[]{:T(128)S(6)} %copy.435, s32[]{:T(128)} %constant.254.clone.1..sunk.1, s32[]{:T(128)} %constant.254.clone.1..sunk.1) | dynamic-update-slice | bytes 6291460 | tf_op jit(solution)/shard_map/while/body/jit(dynamic_update_index_in_dim)/dynamic_update_slice | solution.py:199
  916.3 12.8 copy.376
  929.1 62.4 %dynamic_update_slice.131 = f32[2,256,3072]{1,0,2:T(2,128)} dynamic-update-slice(f32[2,256,3072]{1,0,2:T(2,128)} %get-tuple-element.1321, f32[1,256,3072]{1,0,2:T(1,128)S(1)} %copy.376, s32[]{:T(128)S(6)} %copy.435, s32[]{:T(128)} %constant.254.clone.1..sunk.1, s32[]{:T(128)} %constant.254.clone.1..sunk.1) | dynamic-update-slice | bytes 6291460 | tf_op jit(solution)/shard_map/while/body/jit(dynamic_update_index_in_dim)/dynamic_update_slice | solution.py:199
  995.0 8.1 multiply_reduce_fusion.9
  1003.3 12.5 multiply_reduce_fusion.7
  1018.4 9.1 fusion.106
  1034.2 8.2 reshape_reshape.3
  1042.4 9.4 fusion.107
  1055.7 484.2 %while.23 = (s32[]{:T(128)}, f32[2,48,64,128]{3,2,1,0:T(8,128)}, f32[2,48,64,128]{3,2,1,0:T(8,128)}, f32[2,48]{1,0:T(2,128)}, f32[2,48,64,128]{3,2,1,0:T(8,128)}, /*index=5*/s32[]{:T(128)}) while((s32[]{:T(128)}, f32[2,48,64,128]{3,2,1,0:T(8,128)}, f32[2,48,64,128]{3,2,1,0:T(8,128)}, f32[2,48]{1,0:T(2,128)}, f32[2,48,64,128]{3,2,1,0:T(8,128)}, ...), condition=%wide.region_12.13_spmd, body=%wide.region_11.12_spmd.sunk | while | flops 1572866 | bytes 34603528 | solution.py:247
  1057.1 65.4 %collective-permute-done.1 = f32[2,48,64,128]{3,2,1,0:T(8,128)S(1)} collective-permute-done((f32[2,48,64,128]{3,2,1,0:T(8,128)}, f32[2,48,64,128]{3,2,1,0:T(8,128)S(1)}, u32[]{:S(2)}, u32[]{:S(2)}) %collective-permute-start.1) | collective-permute-done | bytes 3145760 | tf_op jit(solution)/shard_map/while/body/eval_jaxpr/ppermute | solution.py:22
  1129.0 64.8 %collective-permute-done.1 = f32[2,48,64,128]{3,2,1,0:T(8,128)S(1)} collective-permute-done((f32[2,48,64,128]{3,2,1,0:T(8,128)}, f32[2,48,64,128]{3,2,1,0:T(8,128)S(1)}, u32[]{:S(2)}, u32[]{:S(2)}) %collective-permute-start.1) | collective-permute-done | bytes 3145760 | tf_op jit(solution)/shard_map/while/body/eval_jaxpr/ppermute | solution.py:22
  1200.2 63.2 %collective-permute-done.1 = f32[2,48,64,128]{3,2,1,0:T(8,128)S(1)} collective-permute-done((f32[2,48,64,128]{3,2,1,0:T(8,128)}, f32[2,48,64,128]{3,2,1,0:T(8,128)S(1)}, u32[]{:S(2)}, u32[]{:S(2)}) %collective-permute-start.1) | collective-permute-done | bytes 3145760 | tf_op jit(solution)/shard_map/while/body/eval_jaxpr/ppermute | solution.py:22
  1269.8 62.3 %collective-permute-done.1 = f32[2,48,64,128]{3,2,1,0:T(8,128)S(1)} collective-permute-done((f32[2,48,64,128]{3,2,1,0:T(8,128)}, f32[2,48,64,128]{3,2,1,0:T(8,128)S(1)}, u32[]{:S(2)}, u32[]{:S(2)}) %collective-permute-start.1) | collective-permute-done | bytes 3145760 | tf_op jit(solution)/shard_map/while/body/eval_jaxpr/ppermute | solution.py:22
  1338.6 61.8 %collective-permute-done.1 = f32[2,48,64,128]{3,2,1,0:T(8,128)S(1)} collective-permute-done((f32[2,48,64,128]{3,2,1,0:T(8,128)}, f32[2,48,64,128]{3,2,1,0:T(8,128)S(1)}, u32[]{:S(2)}, u32[]{:S(2)}) %collective-permute-start.1) | collective-permute-done | bytes 3145760 | tf_op jit(solution)/shard_map/while/body/eval_jaxpr/ppermute | solution.py:22
  1406.8 61.8 %collective-permute-done.1 = f32[2,48,64,128]{3,2,1,0:T(8,128)S(1)} collective-permute-done((f32[2,48,64,128]{3,2,1,0:T(8,128)}, f32[2,48,64,128]{3,2,1,0:T(8,128)S(1)}, u32[]{:S(2)}, u32[]{:S(2)}) %collective-permute-start.1) | collective-permute-done | bytes 3145760 | tf_op jit(solution)/shard_map/while/body/eval_jaxpr/ppermute | solution.py:22
  1475.1 59.7 %collective-permute-done.1 = f32[2,48,64,128]{3,2,1,0:T(8,128)S(1)} collective-permute-done((f32[2,48,64,128]{3,2,1,0:T(8,128)}, f32[2,48,64,128]{3,2,1,0:T(8,128)S(1)}, u32[]{:S(2)}, u32[]{:S(2)}) %collective-permute-start.1) | collective-permute-done | bytes 3145760 | tf_op jit(solution)/shard_map/while/body/eval_jaxpr/ppermute | solution.py:22
  1541.6 301.2 %while.24 = (s32[]{:T(128)}, f32[2,256,3328]{2,1,0:T(8,128)}, bf16[2,256,48]{2,1,0:T(8,128)(2,1)}, f32[2,48]{1,0:T(2,128)}, f32[2,48]{1,0:T(2,128)}, /*index=5*/...) while((s32[]{:T(128)}, f32[2,256,3328]{2,1,0:T(8,128)}, ...), condition=%wide.region_29.30_spmd, body=%wide.region_13.29_spmd.sunk | while | flops 10035081216 | bytes 197000720 | solution.py:264
  1590.3 21.1 fusion.230
  1645.4 13.6 bitcast_add_fusion.7
  1727.6 21.1 fusion.230
  1782.7 13.6 bitcast_add_fusion.7
  1842.8 17.5 multiply_reduce_fusion.5
  1866.2 8.6 fusion.137
  1890.9 16.7 fusion.124
  1907.6 13.2 fusion.112
  1923.4 12.4 fusion.132
  1937.2 21.3 fusion.123
  1964.6 86.7 %all-reduce.24.cloned.1.call-done = (f32[1536]{0:T(1024)}, f32[4,3328]{1,0:T(4,128)}, f32[3328]{0:T(1024)}, f32[48]{0:T(128)}, f32[48]{0:T(128)}, /*index=5*/f32[48]{0:T(128)}, f32[3072]{0:T(1024)}, f32[3]{0:T(128)}) async-done(((f32[1536]{0:T(1024)}, f32[4,3328]{1,0:T(4,128)}, f32[3328]{0:T(1024)}, f32[48]{0:T(128)}, f32[48]{0:T(128)}, /*index=5*/f32[48]{0:T(128)}, f32[3072]{0:T(1024)}, f32[3]{0:T(128)}), ...) | async-done | bytes 85596
  2057.6 208.3 %reduce-scatter.6.cloned.1.call-done = f32[96,1536]{1,0:T(8,128)} async-done(((f32[3072,1536]{1,0:T(8,128)}), f32[96,1536]{1,0:T(8,128)}) %reduce-scatter.6.cloned.1.call-update) | async-done | bytes 589840 | tf_op jit(solution)/shard_map/reduce_scatter | solution.py:296
  2265.9 371.4 %reduce-scatter.4.cloned.1.call-done = f32[48,6448]{1,0:T(8,128)} async-done(((f32[1536,6448]{1,0:T(8,128)}), f32[48,6448]{1,0:T(8,128)}) %reduce-scatter.4.cloned.1.call-update) | async-done | bytes 1238032 | tf_op jit(solution)/shard_map/reduce_scatter | solution.py:292
  (539 shorter events, 500.7 us)
Async XLA Ops:
  7.2 120.2 %copy-start.13 = (bf16[2,256,1536]{2,1,0:T(8,128)(2,1)S(1)}, bf16[2,256,1536]{2,1,0:T(8,128)(2,1)}, u32[]{:S(2)}) copy-start(bf16[2,256,1536]{2,1,0:T(8,128)(2,1)} %param.22) | copy-start | bytes 4718596
  7.2 138.5 %all-gather.4.cloned.1.call-start = ((), (), s32[]{:S(2)}) async-start(), calls=%async_computation.2 | async-start | bytes 20680704 | tf_op jit(solution)/shard_map/all_gather | solution.py:134
  7.9 995.2 %all-gather.6.cloned.1.call-start = ((), (), s32[]{:S(2)}) async-start(), calls=%async_computation.3 | async-start | bytes 9732096 | tf_op jit(solution)/shard_map/all_gather | solution.py:138
  8.7 2042.6 %all-reduce.24.cloned.1.call-start = ((), (), s32[]{:S(2)}) async-start(), calls=%async_computation.6 | async-start | bytes 184320
  9.6 120.0 %copy-start.54 = (f32[1,2,2,128]{3,1,2,0:T(2,128)}, f32[1,2,2,128]{3,1,2,0:T(2,128)S(1)}, u32[]{:S(2)}) copy-start(f32[1,2,2,128]{3,1,2,0:T(2,128)S(1)} %copy.318) | copy-start | bytes 6148
  55.4 74.2 %copy-start.46 = (f32[1536]{0:T(1024)}, f32[1536]{0:T(1024)S(1)}, u32[]{:S(2)}) copy-start(f32[1536]{0:T(1024)S(1)} %convert_element_type.59) | copy-start | bytes 18436
  58.5 104.7 %copy-start.56 = (f32[512]{0:T(512)}, f32[512]{0:T(512)S(1)}, u32[]{:S(2)}) copy-start(f32[512]{0:T(512)S(1)} %rsqrt.22) | copy-start | bytes 6148
  127.8 35.5 %copy-start.17 = (bf16[512,1536]{1,0:T(8,128)(2,1)}, bf16[512,1536]{1,0:T(8,128)(2,1)S(1)}, u32[]{:S(2)}) copy-start(bf16[512,1536]{1,0:T(8,128)(2,1)S(1)} %fusion.116) | copy-start | bytes 4718596
  178.5 5.6 collective-permute-start.2
  181.7 17.8 copy-start.35
  181.7 17.8 copy-start.37
  181.7 17.8 copy-start.39
  181.8 17.8 copy-start.41
  184.1 18.1 copy-start.29
  222.8 19.5 copy-start.27
  262.8 19.5 copy-start.27
  288.4 522.7 %copy-start.28 = (f32[2,256,48]{1,2,0:T(8,128)S(1)}, f32[2,256,48]{1,2,0:T(8,128)}, u32[]{:S(2)}) copy-start(f32[2,256,48]{1,2,0:T(8,128)} %get-tuple-element.1454) | copy-start | bytes 294916
  288.4 71.8 %collective-permute-start = (f32[2,48,64,128]{3,2,1,0:T(8,128)}, f32[2,48,64,128]{3,2,1,0:T(8,128)S(1)}, u32[]{:S(2)}, u32[]{:S(2)}) collective-permute-start(f32[2,48,64,128]{3,2,1,0:T(8,128)} %get-tuple-element.1301), channel_id=1, source_target_pairs={{0,1},{1,2},{2,3},{3,4},{4,5},{5,6},{6,7},{8,9},{9,10},{10,11},{11... | collective-permute-start | bytes 9437192 | tf_op jit(solution)/shard_map/while/body/eval_jaxpr/ppermute | solution.py:22
  365.3 71.1 %collective-permute-start = (f32[2,48,64,128]{3,2,1,0:T(8,128)}, f32[2,48,64,128]{3,2,1,0:T(8,128)S(1)}, u32[]{:S(2)}, u32[]{:S(2)}) collective-permute-start(f32[2,48,64,128]{3,2,1,0:T(8,128)} %get-tuple-element.1301), channel_id=1, source_target_pairs={{0,1},{1,2},{2,3},{3,4},{4,5},{5,6},{6,7},{8,9},{9,10},{10,11},{11... | collective-permute-start | bytes 9437192 | tf_op jit(solution)/shard_map/while/body/eval_jaxpr/ppermute | solution.py:22
  441.4 70.7 %collective-permute-start = (f32[2,48,64,128]{3,2,1,0:T(8,128)}, f32[2,48,64,128]{3,2,1,0:T(8,128)S(1)}, u32[]{:S(2)}, u32[]{:S(2)}) collective-permute-start(f32[2,48,64,128]{3,2,1,0:T(8,128)} %get-tuple-element.1301), channel_id=1, source_target_pairs={{0,1},{1,2},{2,3},{3,4},{4,5},{5,6},{6,7},{8,9},{9,10},{10,11},{11... | collective-permute-start | bytes 9437192 | tf_op jit(solution)/shard_map/while/body/eval_jaxpr/ppermute | solution.py:22
  517.2 69.8 %collective-permute-start = (f32[2,48,64,128]{3,2,1,0:T(8,128)}, f32[2,48,64,128]{3,2,1,0:T(8,128)S(1)}, u32[]{:S(2)}, u32[]{:S(2)}) collective-permute-start(f32[2,48,64,128]{3,2,1,0:T(8,128)} %get-tuple-element.1301), channel_id=1, source_target_pairs={{0,1},{1,2},{2,3},{3,4},{4,5},{5,6},{6,7},{8,9},{9,10},{10,11},{11... | collective-permute-start | bytes 9437192 | tf_op jit(solution)/shard_map/while/body/eval_jaxpr/ppermute | solution.py:22
  592.1 68.8 %collective-permute-start = (f32[2,48,64,128]{3,2,1,0:T(8,128)}, f32[2,48,64,128]{3,2,1,0:T(8,128)S(1)}, u32[]{:S(2)}, u32[]{:S(2)}) collective-permute-start(f32[2,48,64,128]{3,2,1,0:T(8,128)} %get-tuple-element.1301), channel_id=1, source_target_pairs={{0,1},{1,2},{2,3},{3,4},{4,5},{5,6},{6,7},{8,9},{9,10},{10,11},{11... | collective-permute-start | bytes 9437192 | tf_op jit(solution)/shard_map/while/body/eval_jaxpr/ppermute | solution.py:22
  666.0 67.9 %collective-permute-start = (f32[2,48,64,128]{3,2,1,0:T(8,128)}, f32[2,48,64,128]{3,2,1,0:T(8,128)S(1)}, u32[]{:S(2)}, u32[]{:S(2)}) collective-permute-start(f32[2,48,64,128]{3,2,1,0:T(8,128)} %get-tuple-element.1301), channel_id=1, source_target_pairs={{0,1},{1,2},{2,3},{3,4},{4,5},{5,6},{6,7},{8,9},{9,10},{10,11},{11... | collective-permute-start | bytes 9437192 | tf_op jit(solution)/shard_map/while/body/eval_jaxpr/ppermute | solution.py:22
  739.0 67.0 %collective-permute-start = (f32[2,48,64,128]{3,2,1,0:T(8,128)}, f32[2,48,64,128]{3,2,1,0:T(8,128)S(1)}, u32[]{:S(2)}, u32[]{:S(2)}) collective-permute-start(f32[2,48,64,128]{3,2,1,0:T(8,128)} %get-tuple-element.1301), channel_id=1, source_target_pairs={{0,1},{1,2},{2,3},{3,4},{4,5},{5,6},{6,7},{8,9},{9,10},{10,11},{11... | collective-permute-start | bytes 9437192 | tf_op jit(solution)/shard_map/while/body/eval_jaxpr/ppermute | solution.py:22
  1055.7 485.9 %copy-start.31 = (f32[48]{0:T(128)S(1)}, f32[48]{0:T(128)}, u32[]{:S(2)}) copy-start(f32[48]{0:T(128)} %param.28) | copy-start | bytes 580
  1055.7 66.8 %collective-permute-start.1 = (f32[2,48,64,128]{3,2,1,0:T(8,128)}, f32[2,48,64,128]{3,2,1,0:T(8,128)S(1)}, u32[]{:S(2)}, u32[]{:S(2)}) collective-permute-start(f32[2,48,64,128]{3,2,1,0:T(8,128)} %get-tuple-element.1346), channel_id=1, source_target_pairs={{1,0},{2,1},{3,2},{4,3},{5,4},{6,5},{7,6},{9,8},{10,9},{11,10},{12... | collective-permute-start | bytes 9437192 | tf_op jit(solution)/shard_map/while/body/eval_jaxpr/ppermute | solution.py:22
  1127.7 66.1 %collective-permute-start.1 = (f32[2,48,64,128]{3,2,1,0:T(8,128)}, f32[2,48,64,128]{3,2,1,0:T(8,128)S(1)}, u32[]{:S(2)}, u32[]{:S(2)}) collective-permute-start(f32[2,48,64,128]{3,2,1,0:T(8,128)} %get-tuple-element.1346), channel_id=1, source_target_pairs={{1,0},{2,1},{3,2},{4,3},{5,4},{6,5},{7,6},{9,8},{10,9},{11,10},{12... | collective-permute-start | bytes 9437192 | tf_op jit(solution)/shard_map/while/body/eval_jaxpr/ppermute | solution.py:22
  1198.9 64.5 %collective-permute-start.1 = (f32[2,48,64,128]{3,2,1,0:T(8,128)}, f32[2,48,64,128]{3,2,1,0:T(8,128)S(1)}, u32[]{:S(2)}, u32[]{:S(2)}) collective-permute-start(f32[2,48,64,128]{3,2,1,0:T(8,128)} %get-tuple-element.1346), channel_id=1, source_target_pairs={{1,0},{2,1},{3,2},{4,3},{5,4},{6,5},{7,6},{9,8},{10,9},{11,10},{12... | collective-permute-start | bytes 9437192 | tf_op jit(solution)/shard_map/while/body/eval_jaxpr/ppermute | solution.py:22
  1268.5 63.6 %collective-permute-start.1 = (f32[2,48,64,128]{3,2,1,0:T(8,128)}, f32[2,48,64,128]{3,2,1,0:T(8,128)S(1)}, u32[]{:S(2)}, u32[]{:S(2)}) collective-permute-start(f32[2,48,64,128]{3,2,1,0:T(8,128)} %get-tuple-element.1346), channel_id=1, source_target_pairs={{1,0},{2,1},{3,2},{4,3},{5,4},{6,5},{7,6},{9,8},{10,9},{11,10},{12... | collective-permute-start | bytes 9437192 | tf_op jit(solution)/shard_map/while/body/eval_jaxpr/ppermute | solution.py:22
  1337.3 63.1 %collective-permute-start.1 = (f32[2,48,64,128]{3,2,1,0:T(8,128)}, f32[2,48,64,128]{3,2,1,0:T(8,128)S(1)}, u32[]{:S(2)}, u32[]{:S(2)}) collective-permute-start(f32[2,48,64,128]{3,2,1,0:T(8,128)} %get-tuple-element.1346), channel_id=1, source_target_pairs={{1,0},{2,1},{3,2},{4,3},{5,4},{6,5},{7,6},{9,8},{10,9},{11,10},{12... | collective-permute-start | bytes 9437192 | tf_op jit(solution)/shard_map/while/body/eval_jaxpr/ppermute | solution.py:22
  1405.5 63.1 %collective-permute-start.1 = (f32[2,48,64,128]{3,2,1,0:T(8,128)}, f32[2,48,64,128]{3,2,1,0:T(8,128)S(1)}, u32[]{:S(2)}, u32[]{:S(2)}) collective-permute-start(f32[2,48,64,128]{3,2,1,0:T(8,128)} %get-tuple-element.1346), channel_id=1, source_target_pairs={{1,0},{2,1},{3,2},{4,3},{5,4},{6,5},{7,6},{9,8},{10,9},{11,10},{12... | collective-permute-start | bytes 9437192 | tf_op jit(solution)/shard_map/while/body/eval_jaxpr/ppermute | solution.py:22
  1473.8 61.0 %collective-permute-start.1 = (f32[2,48,64,128]{3,2,1,0:T(8,128)}, f32[2,48,64,128]{3,2,1,0:T(8,128)S(1)}, u32[]{:S(2)}, u32[]{:S(2)}) collective-permute-start(f32[2,48,64,128]{3,2,1,0:T(8,128)} %get-tuple-element.1346), channel_id=1, source_target_pairs={{1,0},{2,1},{3,2},{4,3},{5,4},{6,5},{7,6},{9,8},{10,9},{11,10},{12... | collective-permute-start | bytes 9437192 | tf_op jit(solution)/shard_map/while/body/eval_jaxpr/ppermute | solution.py:22
  1588.3 23.1 copy-start.24
  1590.2 21.2 copy-start.25
  1590.3 21.2 copy-start.21
  1725.6 23.1 copy-start.24
  1727.6 21.2 copy-start.25
  1727.6 21.2 copy-start.21
  1842.7 17.6 copy-start.36
  1842.7 17.6 copy-start.38
  1842.7 17.6 copy-start.40
  1842.7 17.6 copy-start.42
  1876.3 11.3 collective-permute-start.3
  1888.8 18.7 slice-start.9
  1890.8 16.7 slice-start.10
  1890.8 16.7 copy-start.14
  1923.3 342.6 %reduce-scatter.6.cloned.1.call-start = ((), (), s32[]{:S(2)}) async-start(), calls=%async_computation.5 | async-start | bytes 19464192 | tf_op jit(solution)/shard_map/reduce_scatter | solution.py:296
  1935.8 701.5 %reduce-scatter.4.cloned.1.call-start = ((), (), s32[]{:S(2)}) async-start(), calls=%async_computation.4 | async-start | bytes 41361408 | tf_op jit(solution)/shard_map/reduce_scatter | solution.py:292
  (96 other events, 586.8 us)
Sparse Core Ops, SparseCore 0:
  10.9 134.7 all-gather.3
  148.6 80.8 all-gather.5
  1923.4 127.7 all-reduce.23
  2058.1 207.7 reduce-scatter.5
  2272.8 364.4 reduce-scatter.3
where the time goes:
time: 2670 us; the launch traced here: 2650 us
  waiting for transfers between devices  1580 us (59%)
  local copies, waits for them, and re-layouts  353 us (13%)
  matrix products  292 us (11%)
  other arithmetic  225 us (8%)
  blocking collectives  110 us (4%)
  starting transfers between devices  49.7 us (2%)
  loops' own time  27.5 us (1%)
    ppermute x16, waiting for transfers between devices, shifted(): return lax.ppermute(block, axis, route)  892 us
    reduce_scatter x1, waiting for transfers between devices, shards(): lax.psum_scatter(grad_in_w, ('batch', 'seq'), scatter_dimension=0, tiled=...  371 us
    reduce_scatter x1, waiting for transfers between devices, shards(): lax.psum_scatter(grad_out_w, ('batch', 'seq'), scatter_dimension=0, tiled...  208 us
    dynamic_update_slice x4, local copies, waits for them, and re-layouts, shards(): lax.map(finish_slot, (state_in, cumulative, conv_out, inner_out, fresh_st...  150 us
    dot_general x6, matrix products, intra_part(): inner_out = jnp.einsum('tsh,shp->thp', mixing, heads_in, precision=PRECISE)  101 us
    unnamed x6, waiting for transfers between devices  88.1 us
    all_gather x1, blocking collectives, shards(): lax.all_gather(conv_weight, ('batch', 'seq'), axis=1, tiled=True)  66.9 us
  transfers between devices with their start and end apart: 21, of which 19 were waited for; matrix products, arithmetic and copies ran while one was open for 16% of the time, Pallas kernels for 0%

commit v1 on v0

v1 whole, which is shorter than its diff:
```python
import functools

import jax
import jax.numpy as jnp
from jax import lax
from jax.experimental import pallas as pl
from jax.experimental.pallas import tpu as pltpu
from jax.sharding import Mesh
from jax.sharding import PartitionSpec as P

H = 48
P_SIZE = 64
NS = 128
CONV = 4
SPAN = 256
E = 3072
CH = 3328

HC = H // 2
EC = E // 2
HALO = 8
OWN = EC
STEP = EC + NS
OTHER = EC + 2 * NS
WIDE = EC + 3 * NS
BACK = EC + 2 * NS

EPSILON = 1e-05
BF16 = jnp.bfloat16
F32 = jnp.float32
VMEM_LIMIT = 56 * 1024 * 1024


def others(piece, axis):
    size = lax.axis_size(axis)
    here = lax.axis_index(axis)
    moved = []
    for step in range(1, size):
        route = [(i, (i + step) % size) for i in range(size)]
        moved.append((lax.rem(here - step + size, size), lax.ppermute(piece, axis, route)))
    return moved


def place(buffer, piece, index):
    return lax.dynamic_update_slice(buffer, piece, index)


def by_index(axis, mine, other):
    first = lax.axis_index(axis) == 0
    return jnp.where(first, jnp.stack([mine, other]), jnp.stack([other, mine]))


def swapped(piece, axis):
    return lax.ppermute(piece, axis, [(0, 1), (1, 0)])


def gather_chips(pieces, inner):
    _, rows, columns = pieces.shape
    nx, nz, ny = lax.axis_size("x"), lax.axis_size("z"), lax.axis_size("y")
    ix, iz, iy = lax.axis_index("x"), lax.axis_index("z"), lax.axis_index("y")
    line = jnp.zeros((2, nz, rows, columns), pieces.dtype)
    line = place(line, pieces[:, None], (0, iz, 0, 0))
    for index, moved in others(pieces, "z"):
        line = place(line, moved[:, None], (0, index, 0, 0))
    if inner:
        whole = jnp.zeros((nx, nz, ny, 2, rows, columns), pieces.dtype)
    else:
        whole = jnp.zeros((nx, 2, nz, ny, rows, columns), pieces.dtype)
    for half, (first, second) in enumerate((("y", "x"), ("x", "y"))):
        held = [((ix, iy), line[half])]
        for axis in (first, second):
            more = []
            for (at_x, at_y), piece in held:
                for index, moved in others(piece, axis):
                    more.append(((index, at_y) if axis == "x" else (at_x, index), moved))
            held = held + more
        for (at_x, at_y), piece in held:
            if inner:
                whole = place(whole, piece[None, :, None, None], (at_x, 0, at_y, half, 0, 0))
            else:
                whole = place(whole, piece[None, None, :, None], (at_x, half, 0, at_y, 0, 0))
    return whole


def take(value, index, axis):
    return lax.dynamic_index_in_dim(value, index, axis, keepdims=False)


def add_up(mine, moved):
    total = mine.astype(F32)
    for piece in moved:
        total = total + piece.astype(F32)
    return total


def sent_to(value, axis, dim):
    size = lax.axis_size(axis)
    here = lax.axis_index(axis)
    moved = []
    for step in range(1, size):
        route = [(i, (i + step) % size) for i in range(size)]
        moved.append(lax.ppermute(take(value, lax.rem(here + step, size), dim), axis, route))
    return take(value, here, dim), moved


def scatter_chips(whole, inner):
    shares = []
    for half, (first, second) in enumerate((("x", "y"), ("y", "x"))):
        part = whole[:, :, :, half] if inner else whole[:, half]
        for axis in (first, second):
            dim = 0 if axis == "x" else (2 if axis == first or first == "y" else 1)
            if axis == "y":
                dim = part.ndim - 3
            mine, moved = sent_to(part, axis, dim)
            part = add_up(mine, moved).astype(whole.dtype)
        mine, moved = sent_to(part, "z", 0)
        shares.append(add_up(mine, moved))
    return jnp.stack(shares)


def sum_everywhere(value):
    for axis in ("core", "x", "y", "z"):
        size = lax.axis_size(axis)
        step = 1
        while step < size:
            route = [(i, i ^ step) for i in range(size)]
            value = value + lax.ppermute(value, axis, route)
            step *= 2
    return value


def gather_small(piece):
    count = piece.shape[0]
    sizes = [lax.axis_size(a) for a in ("x", "core", "z", "y")]
    held = piece.reshape(1, 1, 1, 1, count)
    for dim, axis in ((2, "z"), (3, "y"), (0, "x"), (1, "core")):
        dims = list(held.shape)
        dims[dim] = lax.axis_size(axis)
        zero = (0,) * 5
        wide = jnp.zeros(dims, piece.dtype)
        at = list(zero)
        at[dim] = lax.axis_index(axis)
        wide = place(wide, held, at)
        for index, moved in others(held, axis):
            at = list(zero)
            at[dim] = index
            wide = place(wide, moved, at)
        held = wide
    return held.reshape(sizes[0] * sizes[1] * sizes[2] * sizes[3], count)


def nn(a, b):
    return lax.dot_general(a, b, (((1,), (0,)), ((), ())), preferred_element_type=F32)


def nt(a, b):
    return lax.dot_general(a, b, (((1,), (1,)), ((), ())), preferred_element_type=F32)


def tn(a, b):
    return lax.dot_general(a, b, (((0,), (0,)), ((), ())), preferred_element_type=F32)


def pieces_of(value, count):
    parts = []
    rest = value
    for index in range(count):
        part = rest.astype(BF16)
        parts.append(part)
        if index < count - 1:
            rest = rest - part.astype(F32)
    return parts


def head_map():
    row = lax.broadcasted_iota(jnp.int32, (NS, EC), 0)
    lane = lax.broadcasted_iota(jnp.int32, (NS, EC), 1)
    inside = (lane >= row * P_SIZE) & (lane < row * P_SIZE + P_SIZE)
    return jnp.where(inside, 1.0, 0.0).astype(BF16)


def spread(value, heads, count=2):
    return sum(nn(part, heads) for part in pieces_of(value, count))


def gathered_heads(value, heads, count=2):
    return sum(nt(part, heads) for part in pieces_of(value, count))


def triangle(kind):
    row = lax.broadcasted_iota(jnp.int32, (SPAN, SPAN), 0)
    col = lax.broadcasted_iota(jnp.int32, (SPAN, SPAN), 1)
    keep = {"ge": row >= col, "gt": row > col, "le": row <= col}[kind]
    return jnp.where(keep, 1.0, 0.0)


def exact_sum(matrix, value):
    low = matrix.astype(BF16)
    return sum(nn(low, part) for part in pieces_of(value, 3))


def sigmoid(v):
    return 1.0 / (1.0 + jnp.exp(-v))


def softplus(v):
    return jnp.maximum(v, 0.0) + jnp.log1p(jnp.exp(-jnp.abs(v)))


def call(kernel, grid, in_specs, out_specs, out_shape, scratch=(), flops=0, moved=0, **more):
    return pl.pallas_call(
        kernel,
        grid=grid,
        in_specs=in_specs,
        out_specs=out_specs,
        out_shape=out_shape,
        scratch_shapes=list(scratch),
        compiler_params=pltpu.CompilerParams(vmem_limit_bytes=VMEM_LIMIT),
        cost_estimate=pl.CostEstimate(flops=flops, bytes_accessed=moved, transcendentals=0),
        **more,
    )


def shape(*dims, dtype=F32):
    return jax.ShapeDtypeStruct(dims, dtype)


def fixed(*dims):
    return pl.BlockSpec(dims, lambda *_: (0,) * len(dims))


def conv_kernel(rows, nz, proj, taps, heads_par, x_out, bc_out, step_out, cum_out, state_out, local_out, total_out):
    heads = head_map()
    spans = rows // SPAN
    lower = triangle("ge")
    state = jnp.zeros((NS, EC), F32)
    total = jnp.zeros((1, NS), F32)
    core_one = heads_par[3:4, :] > 0.5
    for span in range(spans):
        start = HALO + span * SPAN

        def activated(first, width):
            running = taps[4:5, first : first + width]
            for k in range(CONV):
                at = start - (CONV - 1) + k
                running = running + taps[k : k + 1, first : first + width] * proj[0, at : at + SPAN, first : first + width]
            return running * sigmoid(running)

        own = activated(OWN, NS)
        other = activated(OTHER, NS)
        write = jnp.where(core_one, other, own).astype(BF16)
        read = jnp.where(core_one, own, other).astype(BF16)
        here = slice(span * SPAN, span * SPAN + SPAN)
        bc_out[0, here, :NS] = write
        bc_out[0, here, NS:] = read
        raw = proj[0, start : start + SPAN, STEP : STEP + NS] + heads_par[0:1, :]
        step = softplus(raw)
        cum = exact_sum(lower, -step * heads_par[1:2, :])
        step_out[0, here] = step
        cum_out[0, here] = cum
        last = cum[SPAN - 1 : SPAN]
        tail = jnp.exp(last - cum) * step
        local_out[0, span] = state.astype(BF16)
        decay = spread(jnp.broadcast_to(jnp.exp(last), (8, NS)), heads)[0:1]
        wide = EC // 2
        fresh = []
        for half in range(2):
            cols = slice(half * wide, half * wide + wide)
            x = activated(half * wide, wide)
            x_out[0, here, cols] = x.astype(BF16)
            tail_wide = sum(nn(part, heads[:, cols]) for part in pieces_of(tail, 2))
            fresh.append(tn(write, (x * tail_wide).astype(BF16)))
        state = state * decay + jnp.concatenate(fresh, axis=1)
        total = total + last
    depth = NS // nz
    for group in range(nz):
        state_out[group, 0] = state[group * depth : (group + 1) * depth].astype(BF16)
    total_out[0] = jnp.broadcast_to(total, (8, NS))


def intra_kernel(x_ref, bc_ref, step_ref, cum_ref, heads_par, out_ref, xs_ref, cross_ref, cumt_ref):
    heads = head_map()
    step_wide = spread(step_ref[0], heads)
    xs_ref[...] = (x_ref[0].astype(F32) * step_wide).astype(BF16)
    cum = cum_ref[0]
    cumt_ref[...] = cum.T
    cross_ref[...] = nt(bc_ref[0, :, NS:], bc_ref[0, :, :NS]) * triangle("ge")
    skip = spread(jnp.broadcast_to(heads_par[2:3, :], (8, NS)), heads, 3)[0:1]
    out_ref[0] = x_ref[0].astype(F32) * skip
    low = lax.broadcasted_iota(jnp.int32, (SPAN, NS), 1) < P_SIZE

    def pair(p, carry):
        lanes = pl.ds(pl.multiple_of(p * NS, NS), NS)
        xs = xs_ref[:, lanes]
        made = []
        for j in range(2):
            h = 2 * p + j
            col = pltpu.roll(cum, lax.rem(NS - h, NS), 1)[:, 0:1]
            row = cumt_ref[pl.ds(h, 1), :]
            mix = jnp.exp(jnp.minimum(col - row, 0.0)) * cross_ref[...]
            made.append(nn(mix.astype(BF16), xs))
        out_ref[0, :, lanes] += jnp.where(low, made[0], made[1])
        return carry

    lax.fori_loop(0, HC // 2, pair, 0)


def span_state(state_ref, local_ref, before, heads):
    whole = jnp.concatenate([state_ref[g, 0] for g in range(state_ref.shape[0])], axis=0)
    decay = spread(jnp.broadcast_to(jnp.exp(before), (8, NS)), heads)[0:1]
    return whole.astype(F32) * decay + local_ref[0, 0].astype(F32)


def finish_kernel(part_ref, bc_ref, cum_ref, before_ref, state_ref, local_ref, gate_ref, dmix_ref, gain_ref, out_ref, sums_ref):
    heads = head_map()
    state = span_state(state_ref, local_ref, before_ref[0, 0, 0:1], heads).astype(BF16)
    grown = spread(jnp.exp(cum_ref[0]), heads)
    y = part_ref[0] + grown * nn(bc_ref[0, :, NS:], state)
    out_ref[0] = y
    gate = gate_ref[0]
    gated = y * gate * sigmoid(gate)
    squares = jnp.sum(gated * gated, axis=1, keepdims=True)
    slopes = jnp.sum(gated * gain_ref[0:1, :] * dmix_ref[0], axis=1, keepdims=True)
    lane = lax.broadcasted_iota(jnp.int32, (SPAN, NS), 1)
    sums_ref[0] = jnp.where(lane == 0, squares, jnp.where(lane == 1, slopes, 0.0))


def gate_kernel(
    spans, nz, y_ref, gate_ref, dmix_ref, sums_ref, gain_ref, bc_ref, cum_ref,
    mix_out, dy_out, dgate_out, ggain_out, state_out, local_out, run_ref,
):
    step = pl.program_id(1)
    heads = head_map()
    squares = sums_ref[0, :, 0:1]
    slopes = sums_ref[0, :, 1:2]
    scale = lax.rsqrt(squares / E + EPSILON)
    y = y_ref[0]
    gate = gate_ref[0]
    soft = sigmoid(gate)
    silu = gate * soft
    gated = y * silu
    gain = gain_ref[0:1, :]
    dmix = dmix_ref[0]
    mix_out[0] = (gated * scale * gain).astype(BF16)
    dgated = scale * (gain * dmix - gated * (scale * scale * slopes / E))
    dy = dgated * silu
    dy_out[0] = dy.astype(BF16)
    dgate_out[0] = (dgated * y * (soft * (1.0 + gate * (1.0 - soft)))).astype(BF16)

    @pl.when((step == 0) & (pl.program_id(0) == 0))
    def _():
        ggain_out[...] = jnp.zeros_like(ggain_out)

    ggain_out[...] += jnp.broadcast_to(jnp.sum(gated * scale * dmix, axis=0, keepdims=True), (8, EC))

    @pl.when(step == 0)
    def _():
        run_ref[...] = jnp.zeros_like(run_ref)

    cum = cum_ref[0]
    grown = spread(jnp.exp(cum), heads)
    fresh = tn(bc_ref[0, :, NS:], (dy * grown).astype(BF16))
    local_out[0, 0] = run_ref[...].astype(BF16)
    run_ref[...] = fresh + run_ref[...] * grown[SPAN - 1 : SPAN]

    @pl.when(step == spans - 1)
    def _():
        depth = NS // nz
        for group in range(nz):
            state_out[group, 0] = run_ref[group * depth : (group + 1) * depth].astype(BF16)


def back_kernel(
    x_ref, bc_ref, step_ref, cum_ref, before_ref, dy_ref, state_ref, local_ref,
    dxs_out, dbc_out, dcum_out, xs_ref, cross_ref, dcross_ref, cumt_ref, rows_ref,
):
    heads = head_map()
    cum = cum_ref[0]
    xs_ref[...] = (x_ref[0].astype(F32) * spread(step_ref[0], heads)).astype(BF16)
    cumt_ref[...] = cum.T
    write = bc_ref[0, :, :NS]
    read = bc_ref[0, :, NS:]
    mask = triangle("le")
    cross_ref[...] = nt(write, read) * mask
    dcross_ref[...] = jnp.zeros_like(dcross_ref)
    rows_ref[...] = jnp.zeros_like(rows_ref)
    lane = lax.broadcasted_iota(jnp.int32, (SPAN, NS), 1)
    low = lane < P_SIZE

    def pair(p, cols):
        lanes = pl.ds(pl.multiple_of(p * NS, NS), NS)
        xs = xs_ref[:, lanes]
        dy = dy_ref[0, :, lanes]
        made = []
        for j in range(2):
            h = 2 * p + j
            col = pltpu.roll(cum, lax.rem(NS - h, NS), 1)[:, 0:1]
            row = cumt_ref[pl.ds(h, 1), :]
            decay = jnp.exp(jnp.minimum(row - col, 0.0))
            xs_one = jnp.where(low if j == 0 else ~low, xs, jnp.zeros_like(xs))
            slope = nt(xs_one, dy) * decay
            dcross_ref[...] += slope
            cross = cross_ref[...]
            weight = slope * cross
            rows_ref[pl.ds(h, 1), :] = jnp.sum(weight, axis=0, keepdims=True)
            cols = jnp.where(lane == h, jnp.sum(weight, axis=1, keepdims=True), cols)
            made.append(nn((decay * cross).astype(BF16), dy))
        dxs_out[0, :, lanes] = jnp.where(low, made[0], made[1])
        return cols

    cols = lax.fori_loop(0, HC // 2, pair, jnp.zeros((SPAN, NS), F32))
    dcross = (dcross_ref[...] * mask).astype(BF16)
    state = span_state(state_ref, local_ref, before_ref[0, 0, 0:1], heads).astype(BF16)
    grown = spread(jnp.exp(cum), heads)
    dye = dy_ref[0].astype(F32) * grown
    inter = gathered_heads(dye * nn(read, state), heads)
    dbc_out[0, :, :NS] = nn(dcross, read)
    dbc_out[0, :, NS:] = tn(dcross, write) + nt(dye.astype(BF16), state)
    dcum_out[0] = rows_ref[...].T - cols + inter


def close_kernel(
    rows, nz, x_ref, bc_ref, step_ref, cum_ref, dy_ref, proj_ref, taps, heads_par, dxs_ref, dbc_ref, dcum_ref,
    state_ref, local_ref, back_ref, blocal_ref, dproj_out, dbc_out, gtaps_out, ghead_out, dpre_ref,
):
    heads = head_map()
    spans = rows // SPAN
    upper = triangle("le")
    below = triangle("gt")
    whole_in = jnp.concatenate([state_ref[g, 0] for g in range(nz)], axis=0).astype(F32)
    whole_back = jnp.concatenate([back_ref[g, 0] for g in range(nz)], axis=0).astype(F32)
    lasts = [cum_ref[0, (c + 1) * SPAN - 1 : (c + 1) * SPAN] for c in range(spans)]
    skip = spread(jnp.broadcast_to(heads_par[2:3, :], (8, NS)), heads, 3)[0:1]
    real = lax.broadcasted_iota(jnp.int32, (SPAN, NS), 1) < HC
    dpre_ref[:HALO] = jnp.zeros((HALO, EC), F32)
    dpre_ref[HALO + rows :] = jnp.zeros((HALO, EC), F32)
    zero_row = jnp.zeros((1, NS), F32)
    gbias, gdecay, gskip = zero_row, zero_row, zero_row
    for span in range(spans):
        here = slice(span * SPAN, span * SPAN + SPAN)
        before = sum(lasts[:span], zero_row)
        after = sum(lasts[span + 1 :], zero_row)
        both = spread(jnp.exp(jnp.concatenate([before, after, lasts[span], jnp.zeros((5, NS), F32)], axis=0)), heads)
        state = whole_in * both[0:1] + local_ref[0, span].astype(F32)
        back = whole_back * both[1:2] + blocal_ref[0, span].astype(F32)
        back_low = back.astype(BF16)
        at_last = gathered_heads(
            jnp.broadcast_to(jnp.sum(state * back, axis=0, keepdims=True) * both[2:3], (8, EC)), heads
        )[0:1]
        write = bc_ref[0, here, :NS]
        cum = cum_ref[0, here]
        step = step_ref[0, here]
        x = x_ref[0, here].astype(F32)
        dy = dy_ref[0, here].astype(F32)
        tail = spread(jnp.exp(lasts[span] - cum), heads)
        step_wide = spread(step, heads)
        from_back = tail * nn(write, back_low)
        dxs = dxs_ref[0, here] + from_back
        dstep = gathered_heads(x * dxs, heads)
        moved = step * gathered_heads(x * from_back, heads)
        dbc_out[0, here, :NS] = dbc_ref[0, here, :NS] + nt((x * tail * step_wide).astype(BF16), back_low)
        dbc_out[0, here, NS:] = dbc_ref[0, here, NS:]
        dlog = exact_sum(upper, dcum_ref[0, here]) + exact_sum(below, moved) + at_last
        raw = proj_ref[0, HALO + span * SPAN : HALO + span * SPAN + SPAN, STEP : STEP + NS] + heads_par[0:1, :]
        draw = jnp.where(real, (dstep - heads_par[1:2, :] * dlog) * sigmoid(raw), 0.0)
        dproj_out[0, HALO + span * SPAN : HALO + span * SPAN + SPAN, STEP : STEP + NS] = draw.astype(BF16)
        gbias = gbias + jnp.sum(draw, axis=0, keepdims=True)
        gdecay = gdecay + jnp.sum(jnp.where(real, dlog * (-step * heads_par[1:2, :]), 0.0), axis=0, keepdims=True)
        gskip = gskip + gathered_heads(jnp.broadcast_to(jnp.sum(dy * x, axis=0, keepdims=True), (8, EC)), heads, 3)[0:1]
        dx = dxs * step_wide + skip * dy
        start = HALO + span * SPAN
        pre = taps[4:5, :EC]
        for k in range(CONV):
            at = start - (CONV - 1) + k
            pre = pre + taps[k : k + 1, :EC] * proj_ref[0, at : at + SPAN, :EC]
        soft = sigmoid(pre)
        dpre_ref[start : start + SPAN] = dx * (soft * (1.0 + pre * (1.0 - soft)))
    conv_back(rows, dpre_ref, proj_ref, taps, 0, EC, dproj_out, 0, gtaps_out)
    dproj_out[0, :HALO, STEP : STEP + NS] = jnp.zeros((HALO, NS), BF16)
    ghead_out[0] = jnp.concatenate([gbias, gdecay, gskip, jnp.zeros((5, NS), F32)], axis=0)


def conv_back(rows, dpre_ref, proj_ref, taps, first, width, dproj_out, out_first, gtaps_out):
    sums = [jnp.zeros((1, width), F32)] * (CONV + 1)
    blocks = [(0, HALO)] + [(HALO + s * SPAN, SPAN) for s in range(rows // SPAN)]
    for start, count in blocks:
        running = jnp.zeros((count, width), F32)
        for k in range(CONV):
            at = start + (CONV - 1) - k
            running = running + taps[k : k + 1, first : first + width] * dpre_ref[at : at + count]
        dproj_out[0, start : start + count, out_first : out_first + width] = running.astype(BF16)
        if count == SPAN:
            dpre = dpre_ref[start : start + count]
            for k in range(CONV):
                at = start - (CONV - 1) + k
                sums[k] = sums[k] + jnp.sum(dpre * proj_ref[0, at : at + count, first : first + width], axis=0, keepdims=True)
            sums[CONV] = sums[CONV] + jnp.sum(dpre, axis=0, keepdims=True)
    gtaps_out[0, :, :width] = jnp.concatenate(sums + [jnp.zeros((3, width), F32)], axis=0)


def own_kernel(rows, dproj_in, mine_ref, came_ref, proj_ref, taps, dproj_out, gtaps_out, dpre_ref):
    dpre_ref[:HALO] = jnp.zeros((HALO, NS), F32)
    dpre_ref[HALO + rows :] = jnp.zeros((HALO, NS), F32)
    for span in range(rows // SPAN):
        start = HALO + span * SPAN
        pre = taps[4:5, :]
        for k in range(CONV):
            at = start - (CONV - 1) + k
            pre = pre + taps[k : k + 1, :] * proj_ref[0, at : at + SPAN]
        soft = sigmoid(pre)
        here = slice(span * SPAN, span * SPAN + SPAN)
        dconv = mine_ref[0, here] + came_ref[0, here]
        dpre_ref[start : start + SPAN] = dconv * (soft * (1.0 + pre * (1.0 - soft)))
    conv_back(rows, dpre_ref, proj_ref, taps, 0, NS, dproj_out, 0, gtaps_out)


def dot(a, b):
    return jnp.dot(a, b, preferred_element_type=F32)


def shards(
    block_in,
    lengths,
    norm_gain,
    in_weight,
    conv_weight,
    conv_bias,
    step_bias,
    decay_log,
    skip_gain,
    out_gain,
    out_weight,
    grad_out,
):
    slot_count, row_count, features = block_in.shape
    nx, nz, ny = lax.axis_size("x"), lax.axis_size("z"), lax.axis_size("y")
    ix, iz, iy = lax.axis_index("x"), lax.axis_index("z"), lax.axis_index("y")
    core = lax.axis_index("core")
    rows = ny * row_count
    spans = rows // SPAN
    deep = in_weight.shape[0]
    thin = out_weight.shape[0]

    def half_of(value, width, which):
        parts = value.reshape(value.shape[:-1] + (nx, 2, width // (2 * nx)))
        chosen = take(parts, which, value.ndim)
        return chosen.reshape(value.shape[:-1] + (width // 2,))

    def rows_of(block):
        send = take(block, 1 - iy, 0)
        keep = take(block, iy, 0)
        mine = by_index("y", keep, swapped(send, "y")).reshape(rows, features)
        return mine, by_index("core", mine, swapped(mine, "core"))

    own_in, all_in = rows_of(block_in)
    before_rows = lax.ppermute(all_in[:, rows - HALO :], "z", [(i, i + 1) for i in range(nz - 1)])
    own_grad, all_grad = rows_of(grad_out)

    def in_part(which):
        heads_in = half_of(in_weight[:, E : 2 * E], E, which)
        write = in_weight[:, 2 * E : 2 * E + NS]
        read = in_weight[:, 2 * E + NS : E + CH]
        first = which == 0
        steps = jnp.pad(half_of(in_weight[:, E + CH :], H, which), ((0, 0), (0, NS - HC)))
        scan_part = jnp.concatenate(
            [heads_in, jnp.where(first, write, read), steps, jnp.where(first, read, write)], axis=1
        )
        return scan_part, half_of(in_weight[:, :E], E, which)

    my_scan, my_gate = in_part(core)
    its_scan, its_gate = in_part(1 - core)
    scan_pieces = by_index("core", my_scan, swapped(its_scan, "core"))
    gate_pieces = by_index("core", my_gate, swapped(its_gate, "core"))
    small = jnp.concatenate([norm_gain, conv_weight.reshape(-1), conv_bias, out_gain])
    small_count = small.shape[0]
    small = gather_small(jnp.pad(small, (0, -small_count % 1024)))
    scan_weight = gather_chips(scan_pieces, False).reshape(features, WIDE)
    gate_weight = gather_chips(gate_pieces, False).reshape(features, EC)
    back_weight = gather_chips(out_weight.reshape(2, thin // 2, features), True).reshape(EC, features)

    chan = CH // (2 * nx * nz * ny)
    gain_in = small[:, :deep].reshape(1, features).astype(F32)
    taps_all = small[:, deep : deep + CONV * chan].reshape(-1, CONV, chan).transpose(1, 0, 2).reshape(CONV, CH)
    at = deep + CONV * chan
    bias_all = small[:, at : at + chan].reshape(1, CH)
    gain_out_all = small[:, at + chan : at + chan + thin].reshape(E)
    taps_all = jnp.concatenate([taps_all, bias_all, jnp.zeros((3, CH), BF16)], axis=0).astype(F32)
    own_taps = jnp.where(core == 0, taps_all[:, E : E + NS], taps_all[:, E + NS :])
    other_taps = jnp.where(core == 0, taps_all[:, E + NS :], taps_all[:, E : E + NS])
    taps = jnp.concatenate(
        [half_of(taps_all[:, :E], E, core), own_taps, jnp.zeros((8, NS), F32), other_taps], axis=1
    )
    gain_out = jnp.broadcast_to(half_of(gain_out_all, E, core).astype(F32), (8, EC))

    def head_row(value):
        return jnp.pad(half_of(value, H, core), (0, NS - HC))

    heads_par = jnp.stack(
        [
            head_row(step_bias),
            head_row(jnp.exp(decay_log)),
            head_row(skip_gain),
            jnp.full((NS,), core, F32),
        ]
        + [jnp.zeros((NS,), F32)] * 4
    )

    positions = iz * rows + jnp.arange(rows, dtype=jnp.int32)
    slot_lengths = jnp.stack(
        [take(lengths, (ix * 2 + s) * slot_count + iy, 0) for s in range(2)]
    )
    all_valid = positions[None, :] < slot_lengths[:, None]
    own_valid = (positions < take(slot_lengths, core, 0)).astype(F32)[:, None]

    def scaled(value):
        wide = value.astype(F32)
        return wide * lax.rsqrt(jnp.mean(wide * wide, axis=-1, keepdims=True) + EPSILON)

    joined = jnp.concatenate([before_rows, all_in], axis=1)
    normed = (scaled(joined) * gain_in).astype(BF16)
    tall = HALO + rows
    proj = dot(normed.reshape(2 * tall, features), scan_weight).reshape(2, tall, WIDE)
    d_mix = jnp.where(all_valid[:, :, None], all_grad, jnp.zeros_like(all_grad))

    whole_row = lambda *dims: pl.BlockSpec((1,) + dims, lambda s: (s,) + (0,) * len(dims))
    x, bc, step, cum, state_part, local, total = call(
        functools.partial(conv_kernel, rows, nz),
        (2,),
        [whole_row(tall, WIDE), fixed(8, WIDE), fixed(8, NS)],
        [
            whole_row(rows, EC), whole_row(rows, 2 * NS), whole_row(rows, NS), whole_row(rows, NS),
            pl.BlockSpec((nz, 1, NS // nz, EC), lambda s: (0, s, 0, 0)), whole_row(spans, NS, EC), whole_row(8, NS),
        ],
        [
            shape(2, rows, EC, dtype=BF16), shape(2, rows, 2 * NS, dtype=BF16), shape(2, rows, NS), shape(2, rows, NS),
            shape(nz, 2, NS // nz, EC, dtype=BF16), shape(2, spans, NS, EC, dtype=BF16), shape(2, 8, NS),
        ],
        flops=2 * 2 * rows * EC * NS * 3,
        moved=2 * (tall * WIDE * 4 + rows * EC * 2),
    )(proj, taps, heads_par)

    totals = jnp.zeros((nz, 2, NS), F32)
    totals = place(totals, total[None, :, 0], (iz, 0, 0))
    for index, moved in others(total, "z"):
        totals = place(totals, moved[None, :, 0], (index, 0, 0))
    decays = jnp.exp(totals)[:, :, :HC]
    decays = jnp.broadcast_to(decays[..., None], decays.shape + (P_SIZE,)).reshape(nz, 2, 1, EC)

    def exchange(value):
        return lax.all_to_all(value, "z", 0, 0, tiled=True)

    ends = exchange(state_part).astype(F32)
    running = jnp.zeros_like(ends[0])
    starts = []
    for k in range(nz):
        starts.append(running.astype(BF16))
        running = running * decays[k] + ends[k]
    state_in = exchange(jnp.stack(starts))

    in_span = lambda *dims: pl.BlockSpec((1, SPAN) + dims, lambda s, c: (s, c) + (0,) * len(dims))
    local_span = pl.BlockSpec((1, 1, NS, EC), lambda s, c: (s, c, 0, 0))
    state_spec = pl.BlockSpec((nz, 1, NS // nz, EC), lambda s, c: (0, s, 0, 0))
    before_spec = pl.BlockSpec((1, 1, 8, NS), lambda s, c: (s, c, 0, 0))
    part = call(
        intra_kernel,
        (2, spans),
        [in_span(EC), in_span(2 * NS), in_span(NS), in_span(NS), fixed(8, NS)],
        in_span(EC),
        shape(2, rows, EC),
        [
            pltpu.VMEM((SPAN, EC), BF16), pltpu.VMEM((SPAN, SPAN), F32), pltpu.VMEM((NS, SPAN), F32),
        ],
        flops=2 * rows * SPAN * EC * 2 * 6,
        moved=2 * rows * EC * 6,
    )(x, bc, step, cum, heads_par)

    gate = dot(normed[:, HALO:].reshape(2 * rows, features), gate_weight).reshape(2, rows, EC)
    d_mixer_in = lax.dot_general(
        d_mix.reshape(2 * rows, features), back_weight, (((1,), (1,)), ((), ())), preferred_element_type=F32
    ).reshape(2, rows, EC)
    span_ends = cum.reshape(2, spans, SPAN, NS)[:, :, SPAN - 1]
    before = jnp.cumsum(span_ends, axis=1) - span_ends
    before = jnp.broadcast_to(before[:, :, None], (2, spans, 8, NS))
    ssm_out, sums = call(
        finish_kernel,
        (2, spans),
        [
            in_span(EC), in_span(2 * NS), in_span(NS), before_spec, state_spec, local_span, in_span(EC), in_span(EC),
            fixed(8, EC),
        ],
        [in_span(EC), in_span(NS)],
        [shape(2, rows, EC), shape(2, rows, NS)],
        flops=2 * 2 * rows * EC * NS * 3,
        moved=2 * rows * EC * 16,
    )(part, bc, cum, before, state_in, local, gate, d_mixer_in, gain_out)
    sums = sums + swapped(sums, "core")

    rev = lambda *dims: pl.BlockSpec((1, SPAN) + dims, lambda s, c: (s, spans - 1 - c) + (0,) * len(dims))
    rev_local = pl.BlockSpec((1, 1, NS, EC), lambda s, c: (s, spans - 1 - c, 0, 0))
    mixer_in, d_ssm, d_gate, g_gain_out, back_part, back_local = call(
        functools.partial(gate_kernel, spans, nz),
        (2, spans),
        [rev(EC), rev(EC), rev(EC), rev(NS), fixed(8, EC), rev(2 * NS), rev(NS)],
        [rev(EC), rev(EC), rev(EC), fixed(8, EC), state_spec, rev_local],
        [
            shape(2, rows, EC, dtype=BF16), shape(2, rows, EC, dtype=BF16), shape(2, rows, EC, dtype=BF16), shape(8, EC),
            shape(nz, 2, NS // nz, EC, dtype=BF16), shape(2, spans, NS, EC, dtype=BF16),
        ],
        [pltpu.VMEM((NS, EC), F32)],
        flops=2 * 2 * rows * EC * NS * 3,
        moved=2 * rows * EC * 18,
    )(ssm_out, gate, d_mixer_in, sums, gain_out, bc, cum)

    tails = exchange(back_part).astype(F32)
    running = jnp.zeros_like(tails[0])
    backs = [None] * nz
    for k in reversed(range(nz)):
        backs[k] = running.astype(BF16)
        running = running * decays[k] + tails[k]
    back_in = exchange(jnp.stack(backs))

    flat_mix = mixer_in.reshape(2 * rows, EC)
    flat_dmix = d_mix.reshape(2 * rows, features)
    g_out = lax.dot_general(flat_mix, flat_dmix, (((0,), (0,)), ((), ())), preferred_element_type=BF16)
    g_out = scatter_chips(g_out.reshape(nx, nz, ny, 2, thin // 2, features), True).reshape(thin, features)
    flat_normed = normed.reshape(2 * tall, features)
    g_gate = lax.dot_general(
        normed[:, HALO:].reshape(2 * rows, features), d_gate.reshape(2 * rows, EC), (((0,), (0,)), ((), ())),
        preferred_element_type=BF16,
    )
    g_gate = scatter_chips(g_gate.reshape(nx, 2, nz, ny, deep, EC), False)

    mixer_part = dot(flat_mix, back_weight).reshape(2, rows, features)
    mixer_out = take(mixer_part, core, 0) + swapped(take(mixer_part, 1 - core, 0), "core")
    residual = own_in.astype(F32)
    block_value = own_valid * (residual + mixer_out)
    local_sums = jnp.stack(
        [
            jnp.sum(own_valid * residual * residual),
            jnp.sum(own_valid * mixer_out * mixer_out),
            jnp.sum(block_value * block_value),
        ]
    )

    def slots_of(value):
        parts = value.reshape(ny, row_count, features)
        return by_index("y", take(parts, iy, 0), swapped(take(parts, 1 - iy, 0), "y"))

    block_out = slots_of(block_value.astype(BF16))

    dxs, d_bc, d_cum = call(
        back_kernel,
        (2, spans),
        [in_span(EC), in_span(2 * NS), in_span(NS), in_span(NS), before_spec, in_span(EC), state_spec, local_span],
        [in_span(EC), in_span(2 * NS), in_span(NS)],
        [shape(2, rows, EC), shape(2, rows, 2 * NS), shape(2, rows, NS)],
        [
            pltpu.VMEM((SPAN, EC), BF16), pltpu.VMEM((SPAN, SPAN), F32), pltpu.VMEM((SPAN, SPAN), F32),
            pltpu.VMEM((NS, SPAN), F32), pltpu.VMEM((NS, SPAN), F32),
        ],
        flops=2 * rows * SPAN * EC * 2 * 16,
        moved=2 * rows * EC * 10,
    )(x, bc, step, cum, before, d_ssm, state_in, local)

    slot_state = pl.BlockSpec((nz, 1, NS // nz, EC), lambda s: (0, s, 0, 0))
    d_proj, d_bc, g_taps, g_heads = call(
        functools.partial(close_kernel, rows, nz),
        (2,),
        [
            whole_row(rows, EC), whole_row(rows, 2 * NS), whole_row(rows, NS), whole_row(rows, NS), whole_row(rows, EC),
            whole_row(tall, WIDE), fixed(8, WIDE), fixed(8, NS), whole_row(rows, EC), whole_row(rows, 2 * NS),
            whole_row(rows, NS), slot_state, whole_row(spans, NS, EC), slot_state, whole_row(spans, NS, EC),
        ],
        [whole_row(tall, BACK), whole_row(rows, 2 * NS), whole_row(8, EC), whole_row(8, NS)],
        [shape(2, tall, BACK, dtype=BF16), shape(2, rows, 2 * NS), shape(2, 8, EC), shape(2, 8, NS)],
        [pltpu.VMEM((HALO + rows + HALO, EC), F32)],
        flops=2 * 2 * rows * EC * NS * 8,
        moved=2 * rows * EC * 16,
    )(x, bc, step, cum, d_ssm, proj, taps, heads_par, dxs, d_bc, d_cum, state_in, local, back_in, back_local)

    bc_parts = d_bc.reshape(2, rows, 2, NS)
    mine = jnp.where(core == 0, d_bc[:, :, :NS], d_bc[:, :, NS:])
    theirs = jnp.where(core == 0, d_bc[:, :, NS:], d_bc[:, :, :NS])
    column = pl.BlockSpec((1, tall, NS), lambda s: (s, 0, OWN // NS))
    d_proj, g_own = call(
        functools.partial(own_kernel, rows),
        (2,),
        [pl.BlockSpec(memory_space=pl.ANY), whole_row(rows, NS), whole_row(rows, NS), column, fixed(8, NS)],
        [column, whole_row(8, NS)],
        [shape(2, tall, BACK, dtype=BF16), shape(2, 8, NS)],
        [pltpu.VMEM((HALO + rows + HALO, NS), F32)],
        input_output_aliases={0: 0},
    )(d_proj, mine, swapped(theirs, "core"), proj, own_taps)

    flat_dproj = d_proj.reshape(2 * tall, BACK)
    g_scan = lax.dot_general(flat_normed, flat_dproj, (((0,), (0,)), ((), ())), preferred_element_type=BF16)
    g_scan = scatter_chips(g_scan.reshape(nx, 2, nz, ny, deep, BACK), False)

    d_normed = lax.dot_general(
        flat_dproj, scan_weight[:, :BACK], (((1,), (1,)), ((), ())), preferred_element_type=F32
    ).reshape(2, tall, features)
    d_normed_gate = lax.dot_general(
        d_gate.reshape(2 * rows, EC), gate_weight, (((1,), (1,)), ((), ())), preferred_element_type=F32
    ).reshape(2, rows, features)
    d_normed = jnp.concatenate([d_normed[:, :HALO], d_normed[:, HALO:] + d_normed_gate], axis=1)
    d_own = take(d_normed, core, 0) + swapped(take(d_normed, 1 - core, 0), "core")
    returned = lax.ppermute(d_own[:HALO], "z", [(i + 1, i) for i in range(nz - 1)])
    d_own = jnp.concatenate([d_own[HALO:tall - HALO], d_own[tall - HALO :] + returned], axis=0)

    _, pull_norm = jax.vjp(lambda value, gain: scaled(value) * gain, residual, gain_in)
    d_resid, g_gain_in = pull_norm(d_own)
    grad_in = slots_of((own_valid * own_grad.astype(F32) + d_resid).astype(BF16))

    def spread_half(value, width):
        parts = value.reshape(value.shape[:-1] + (nx, 1, width // (2 * nx)))
        zero = jnp.zeros_like(parts)
        first = core == 0
        both = jnp.concatenate([jnp.where(first, parts, zero), jnp.where(first, zero, parts)], axis=-2)
        return both.reshape(value.shape[:-1] + (width,))

    taps_sum = jnp.sum(g_taps, axis=0)
    own_sum = jnp.sum(g_own, axis=0)
    nothing = jnp.zeros_like(own_sum)
    taps_sum = jnp.concatenate(
        [
            spread_half(taps_sum, E),
            jnp.where(core == 0, own_sum, nothing),
            jnp.where(core == 0, nothing, own_sum),
        ],
        axis=1,
    )
    head_sum = spread_half(jnp.sum(g_heads, axis=0)[:3, :HC], H)
    packed = jnp.concatenate(
        [
            taps_sum[: CONV + 1].reshape(-1),
            spread_half(g_gain_out[0], E),
            g_gain_in.reshape(-1),
            head_sum.reshape(-1),
            local_sums,
        ]
    )
    count = packed.shape[0]
    packed = sum_everywhere(jnp.pad(packed, (0, -count % 1024)).reshape(-1, NS)).reshape(-1)
    place_at = [0]
    for size in ((CONV + 1) * CH, E, features, 3 * H, 3):
        place_at.append(place_at[-1] + size)
    device = ((ix * 2 + core) * nz + iz) * ny + iy
    taps_total = packed[: place_at[1]].reshape(CONV + 1, CH)
    taps_mine = lax.dynamic_slice_in_dim(taps_total, device * chan, chan, 1)
    gain_out_mine = lax.dynamic_slice_in_dim(packed[place_at[1] : place_at[2]], device * thin, thin)
    gain_in_mine = lax.dynamic_slice_in_dim(packed[place_at[2] : place_at[3]], device * deep, deep)
    head_total = packed[place_at[3] : place_at[4]].reshape(3, H)
    valid_sums = packed[place_at[4] : place_at[5]]

    def row_share(value):
        return take(value, core, 0), swapped(take(value, 1 - core, 0), "core")

    scan_mine, scan_came = row_share(g_scan)
    gate_mine, gate_came = row_share(g_gate)

    def both_halves(mine_part, came_part):
        pair = by_index("core", mine_part, came_part)
        width = mine_part.shape[-1]
        return pair.reshape(2, deep, nx, width // nx).transpose(1, 2, 0, 3).reshape(deep, 2 * width)

    own_pair = by_index("core", scan_mine[:, OWN:STEP], scan_came[:, OWN:STEP])
    g_in_weight = jnp.concatenate(
        [
            both_halves(gate_mine, gate_came),
            both_halves(scan_mine[:, :EC], scan_came[:, :EC]),
            own_pair[0],
            own_pair[1],
            both_halves(scan_mine[:, STEP : STEP + HC], scan_came[:, STEP : STEP + HC]),
        ],
        axis=1,
    )
    token_total = jnp.sum(lengths).astype(F32) * features
    rms_stats = jnp.sqrt(valid_sums / token_total)
    return (
        block_out,
        grad_in,
        gain_in_mine,
        g_in_weight,
        taps_mine[:CONV],
        taps_mine[CONV],
        head_total[0],
        head_total[1],
        head_total[2],
        gain_out_mine,
        g_out,
        rms_stats,
    )


def solution(mesh):
    nb, ns = mesh.shape["batch"], mesh.shape["seq"]
    fine = Mesh(mesh.devices.reshape(nb // 2, 2, ns // 2, 2), ("x", "core", "z", "y"))
    batch, seq = ("x", "core"), ("z", "y")
    every = batch + seq
    act = P(batch, seq, None)
    return jax.shard_map(
        shards,
        mesh=fine,
        in_specs=(
            act, P(), P(every), P(every, None), P(None, every), P(every), P(), P(), P(), P(every), P(every, None), act,
        ),
        out_specs=(
            act, act, P(every), P(every, None), P(None, every), P(every), P(), P(), P(), P(every), P(every, None), P(),
        ),
        check_vma=False,
    )
```

time: 2670 us -> 836 us (0.31)
  waiting for transfers between devices: 1580 us -> 275 us
  local copies, waits for them, and re-layouts: 353 us -> 102 us
  matrix products: 292 us -> 71.3 us
  Pallas kernels: 0 us -> 148 us
  other arithmetic: 225 us -> 80.6 us
  blocking collectives: 110 us -> 0 us
  starting transfers between devices: 49.7 us -> 146 us
  loops' own time: 27.5 us -> 0 us
    ppermute x16 -> x87, waiting for transfers between devices: 892 us -> 271 us  [the longest x36 172 us: others(): lax.ppermute(piece, axis, route)]
    reduce_scatter x2 -> x0, waiting for transfers between devices: 580 us -> none  [the longest x1 371 us: shards(): lax.psum_scatter(grad_in_w, ('batch', 'seq'), scatter_dimension=0, tiled=...]
    dot_general x35 -> x9, matrix products: 292 us -> 71.3 us  [the longest x3 27 us: dot(): return jnp.dot(a, b, preferred_element_type=F32)]
    pallas_call x0 -> x7, Pallas kernels: none -> 148 us  [the longest x1 38.7 us: shards(): call(back_kernel, (2, spans), [in_span(EC), in_span(2 * NS), in_span(NS),...]
    dynamic_update_slice x16 -> x47, local copies, waits for them, and re-layouts: 153 us -> 7.14 us  [place(): return lax.dynamic_update_slice(buffer, piece, index)]
    unnamed x6 -> x0, waiting for transfers between devices: 88.1 us -> none
    ppermute x16 -> x87, starting transfers between devices: 49.5 us -> 127 us  [the longest x30 59.4 us: sent_to(): lax.ppermute(take(value, lax.rem(here + step, size), dim), axis, route)]
    all_gather x1 -> x0, blocking collectives: 66.9 us -> none  [shards(): lax.all_gather(conv_weight, ('batch', 'seq'), axis=1, tiled=True)]
  transfers between devices with their start and end apart: 21 -> 91, of which waited for: 19 -> 41; matrix products, arithmetic and copies ran while one was open for 16% -> 24% of each run, Pallas kernels for 0% -> 12%
where the time goes in v1:
time: 836 us; the launch traced here: 827 us
  waiting for transfers between devices  275 us (33%)
  Pallas kernels  148 us (18%)
  starting transfers between devices  146 us (17%)
  local copies, waits for them, and re-layouts  102 us (12%)
  other arithmetic  80.6 us (10%)
  matrix products  71.3 us (9%)
    ppermute x36, waiting for transfers between devices, others(): lax.ppermute(piece, axis, route)  172 us
    ppermute x30, waiting for transfers between devices, sent_to(): lax.ppermute(take(value, lax.rem(here + step, size), dim), axis, route)  67.7 us
    ppermute x30, starting transfers between devices, sent_to(): lax.ppermute(take(value, lax.rem(here + step, size), dim), axis, route)  59.4 us
    ppermute x36, starting transfers between devices, others(): lax.ppermute(piece, axis, route)  51 us
    pallas_call x1, Pallas kernels, shards(): call(back_kernel, (2, spans), [in_span(EC), in_span(2 * NS), in_span(NS),...  38.7 us
    pallas_call x1, Pallas kernels, shards(): call(functools.partial(close_kernel, rows, nz), (2,), [whole_row(rows, EC...  36 us
    dot_general x3, matrix products, dot(): return jnp.dot(a, b, preferred_element_type=F32)  27 us
    pallas_call x1, Pallas kernels, shards(): call(intra_kernel, (2, spans), [in_span(EC), in_span(2 * NS), in_span(NS)...  25.5 us
  transfers between devices with their start and end apart: 91, of which 41 were waited for; matrix products, arithmetic and copies ran while one was open for 24% of the time, Pallas kernels for 12%

profile of v1, /device:TPU:0, one launch (start us, length us, event | category | flops | bytes accessed | tf_op | source)
XLA Modules:
  0.0 826.8 jit_solution(7229899125143199711)
XLA Ops:
  86.6 5.9 collective-permute-done.23
  93.8 10.5 %collective-permute-done.24 = bf16[2,48,1536]{2,1,0:T(8,128)(2,1)S(1)} collective-permute-done((bf16[2,48,1536]{2,1,0:T(8,128)(2,1)S(1)}, bf16[2,48,1536]{2,1,0:T(8,128)(2,1)S(1)}, u32[]{:S(2)}, u32[]{:S(2)}) %collective-permute-start.24) | collective-permute-done | bytes 294944 | tf_op jit(solution)/shard_map/ppermute | solution.py:40
  104.3 4.2 collective-permute-start.10
  114.6 6.4 collective-permute-done.10
  121.5 14.0 %collective-permute-done.11 = bf16[2,48,1920]{2,1,0:T(8,128)(2,1)S(1)} collective-permute-done((bf16[2,48,1920]{2,1,0:T(8,128)(2,1)S(1)}, bf16[2,48,1920]{2,1,0:T(8,128)(2,1)S(1)}, u32[]{:S(2)}, u32[]{:S(2)}) %collective-permute-start.11) | collective-permute-done | bytes 368672 | tf_op jit(solution)/shard_map/ppermute | solution.py:40
  145.4 6.3 collective-permute-done.38
  153.2 12.4 %collective-permute-done.26 = bf16[4,48,1536]{2,1,0:T(8,128)(2,1)S(1)} collective-permute-done((bf16[4,48,1536]{2,1,0:T(8,128)(2,1)S(1)}, bf16[4,48,1536]{2,1,0:T(8,128)(2,1)S(1)}, u32[]{:S(2)}, u32[]{:S(2)}) %collective-permute-start.26) | collective-permute-done | bytes 589856 | tf_op jit(solution)/shard_map/ppermute | solution.py:40
  166.2 10.7 %collective-permute-done.27 = bf16[4,48,1536]{2,1,0:T(8,128)(2,1)S(1)} collective-permute-done((bf16[4,48,1536]{2,1,0:T(8,128)(2,1)S(1)}, bf16[4,48,1536]{2,1,0:T(8,128)(2,1)S(1)}, u32[]{:S(2)}, u32[]{:S(2)}) %collective-permute-start.27) | collective-permute-done | bytes 589856 | tf_op jit(solution)/shard_map/ppermute | solution.py:40
  184.1 21.3 %collective-permute-done.14 = bf16[4,48,1920]{2,1,0:T(8,128)(2,1)S(1)} collective-permute-done((bf16[4,48,1920]{2,1,0:T(8,128)(2,1)S(1)}, bf16[4,48,1920]{2,1,0:T(8,128)(2,1)S(1)}, u32[]{:S(2)}, u32[]{:S(2)}) %collective-permute-start.14) | collective-permute-done | bytes 737312 | tf_op jit(solution)/shard_map/ppermute | solution.py:40
  206.0 11.0 %collective-permute-done.39 = bf16[4,48,1536]{2,1,0:T(8,128)(2,1)S(1)} collective-permute-done((bf16[4,48,1536]{2,1,0:T(8,128)(2,1)S(1)}, bf16[4,48,1536]{2,1,0:T(8,128)(2,1)S(1)}, u32[]{:S(2)}, u32[]{:S(2)}) %collective-permute-start.39) | collective-permute-done | bytes 589856 | tf_op jit(solution)/shard_map/ppermute | solution.py:40
  218.6 12.7 %collective-permute-done.28 = bf16[4,48,1536]{2,1,0:T(8,128)(2,1)S(1)} collective-permute-done((bf16[4,48,1536]{2,1,0:T(8,128)(2,1)S(1)}, bf16[4,48,1536]{2,1,0:T(8,128)(2,1)S(1)}, u32[]{:S(2)}, u32[]{:S(2)}) %collective-permute-start.28) | collective-permute-done | bytes 589856 | tf_op jit(solution)/shard_map/ppermute | solution.py:40
  235.3 26.9 %collective-permute-done.42 = bf16[4,48,1536]{2,1,0:T(8,128)(2,1)S(1)} collective-permute-done((bf16[4,48,1536]{2,1,0:T(8,128)(2,1)S(1)}, bf16[4,48,1536]{2,1,0:T(8,128)(2,1)S(1)}, u32[]{:S(2)}, u32[]{:S(2)}) %collective-permute-start.42) | collective-permute-done | bytes 589856 | tf_op jit(solution)/shard_map/ppermute | solution.py:40
  263.6 12.2 %collective-permute-done.31 = bf16[4,48,1536]{2,1,0:T(8,128)(2,1)S(1)} collective-permute-done((bf16[4,48,1536]{2,1,0:T(8,128)(2,1)S(1)}, bf16[4,48,1536]{2,1,0:T(8,128)(2,1)S(1)}, u32[]{:S(2)}, u32[]{:S(2)}) %collective-permute-start.31) | collective-permute-done | bytes 589856 | tf_op jit(solution)/shard_map/ppermute | solution.py:40
  277.9 12.3 %collective-permute-done.18 = bf16[4,48,1920]{2,1,0:T(8,128)(2,1)S(1)} collective-permute-done((bf16[4,48,1920]{2,1,0:T(8,128)(2,1)S(1)}, bf16[4,48,1920]{2,1,0:T(8,128)(2,1)S(1)}, u32[]{:S(2)}, u32[]{:S(2)}) %collective-permute-start.18) | collective-permute-done | bytes 737312 | tf_op jit(solution)/shard_map/ppermute | solution.py:40
  295.8 7.0 fusion.105.dmix_ref
  306.1 8.9 %fusion.104.proj.proj_ref = f32[2,520,1920]{2,1,0:T(8,128)} fusion(bf16[2,520,1536]{2,1,0:T(8,128)(2,1)S(1)} %multiply_convert_fusion, bf16[1536,1920,1]{1,0,2:T(8,128)(2,1)S(1)} %bitcast.457), kind=kOutput, calls=%fused_computation.344 | convolution fusion | flops 6134169600 | bytes 17080320 | tf_op jit(solution)/shard_map/dot_general | solution.py:518
  315.0 15.8 %shard_map.211 = (bf16[2,512,1536]{2,1,0:T(8,128)(2,1)}, bf16[2,512,256]{2,1,0:T(8,128)(2,1)}, f32[2,512,128]{2,1,0:T(8,128)}, f32[2,512,128]{2,1,0:T(8,128)}, b...) custom-call(f32[2,520,1920]{2,1,0:T(8,128)} %fusion.104.proj.proj_ref, ...), custom_call_target="tpu_custom_call" | custom-call | flops 1207959552 | bytes 11132928 | tf_op jit(solution)/shard_map/pallas_call | solution.py:626
  330.9 5.2 all-to-all-start
  344.9 25.5 %shard_map.212.part_ref = f32[2,512,1536]{2,1,0:T(8,128)} custom-call(bf16[2,512,1536]{2,1,0:T(8,128)(2,1)} %get-tuple-element.36.x_ref, bf16[2,512,256]{2,1,0:T(8,128)(2,1)} %get-tuple-element.37.bc_ref, f32[2,512,128]{2,1,0:T(8,128)} %get-tuple-element.38.step_ref, f32[2,512,128]{2,1,0:T(8,128)} %get-tuple-element.39.cum_ref, f32[8,128]{1,0:T(8,128)} %stack.255.heads_par), custom_call_target="tpu_custom_call" | custom-call | flops 4831838208 | bytes 9437184 | tf_op jit(solution)/shard_map/pallas_call | solution.py:664
  374.9 4.4 all-to-all-start.1
  379.3 9.2 %fusion.96.gate_ref = f32[2,512,1536]{2,1,0:T(8,128)} fusion(bf16[1536,1536,1]{1,0,2:T(8,128)(2,1)} %bitcast.466, bf16[2,520,1536]{2,1,0:T(8,128)(2,1)S(1)} %copy-done.4), kind=kOutput, calls=%fused_computation.336 | convolution fusion | flops 4831838208 | bytes 14155776 | tf_op jit(solution)/shard_map/dot_general | solution.py:518
  388.5 4.3 all-to-all-done.1.state_ref
  394.0 12.9 %shard_map.213 = (f32[2,512,1536]{2,1,0:T(8,128)}, f32[2,512,128]{2,1,0:T(8,128)}) custom-call(f32[2,512,1536]{2,1,0:T(8,128)} %shard_map.212.part_ref, bf16[2,512,256]{2,1,0:T(8,128)(2,1)} %get-tuple-element.37.bc_ref, f32[2,512,128]{2,1,0:T(8,128)} %get-tuple-element.39.cum_ref, f32[2,2,8,128]{3,2,1,0:T(8,128)} %broadcast_in_dim.187.before_ref, ...), custom_call_target="tpu_custom_call" | custom-call | flops 1207959552 | bytes 25165824 | tf_op jit(solution)/shard_map/pallas_call | solution.py:684
  416.3 4.7 copy.98
  423.7 16.5 %shard_map.214 = (bf16[2,512,1536]{2,1,0:T(8,128)(2,1)}, bf16[2,512,1536]{2,1,0:T(8,128)(2,1)}, bf16[2,512,1536]{2,1,0:T(8,128)(2,1)}, f32[8,1536]{1,0:T(8,128)}...) custom-call(f32[2,512,1536]{2,1,0:T(8,128)} %get-tuple-element.43.y_ref, ...), custom_call_target="tpu_custom_call" | custom-call | flops 1207959552 | bytes 28311552 | tf_op jit(solution)/shard_map/pallas_call | solution.py:700
  440.2 8.8 %fusion.106 = f32[2,512,1536]{2,1,0:T(8,128)} fusion(bf16[2,512,1536]{2,1,0:T(8,128)(2,1)} %get-tuple-element.45, bf16[1536,1536,1]{1,0,2:T(8,128)(2,1)S(1)} %bitcast.465), kind=kOutput, calls=%fused_computation.346 | convolution fusion | flops 4831838208 | bytes 14155776 | tf_op jit(solution)/shard_map/dot_general | solution.py:518
  449.0 4.8 copy.108
  453.9 7.6 fusion.109
  470.8 7.1 fusion.107
  490.5 38.7 %shard_map.215 = (f32[2,512,1536]{2,1,0:T(8,128)}, f32[2,512,256]{2,1,0:T(8,128)}, f32[2,512,128]{2,1,0:T(8,128)}) custom-call(bf16[2,512,1536]{2,1,0:T(8,128)(2,1)} %get-tuple-element.36.x_ref, bf16[2,512,256]{2,1,0:T(8,128)(2,1)} %get-tuple-element.37.bc_ref, f32[2,512,128]{2,1,0:T(8,128)} %get-tuple-element.38.step_ref, ...), custom_call_target="tpu_custom_call" | custom-call | flops 12884901888 | bytes 15728640 | tf_op jit(solution)/shard_map/pallas_call | solution.py:751
  539.0 5.0 all-to-all-start.3
  553.7 9.8 %collective-permute-done.61 = bf16[4,48,1536]{2,1,0:T(8,128)(2,1)S(1)} collective-permute-done((bf16[4,48,1536]{2,1,0:T(8,128)(2,1)S(1)}, bf16[4,48,1536]{2,1,0:T(8,128)(2,1)S(1)}, u32[]{:S(2)}, u32[]{:S(2)}) %collective-permute-start.61) | collective-permute-done | bytes 589856 | tf_op jit(solution)/shard_map/ppermute | solution.py:102
  572.5 5.4 collective-permute-start.57
  584.4 9.6 %collective-permute-start.80 = (bf16[48,1536]{1,0:T(8,128)(2,1)S(1)}, bf16[48,1536]{1,0:T(8,128)(2,1)S(1)}, u32[]{:S(2)}, u32[]{:S(2)}) collective-permute-start(bf16[48,1536]{1,0:T(8,128)(2,1)S(1)} %get-tuple-element.123), channel_id=1, source_target_pairs={{0,4},{2,6},{4,0},{6,2},{1,5},{3,7},{5,1},{7,3},{8,12},{10,14},{12... | collective-permute-start | bytes 442376 | tf_op jit(solution)/shard_map/ppermute | solution.py:102
  598.9 4.7 collective-permute-done.80
  606.6 6.4 collective-permute-done.85
  616.4 36.0 %shard_map.216 = (bf16[2,520,1792]{2,1,0:T(8,128)(2,1)}, f32[2,512,256]{2,1,0:T(8,128)}, f32[2,8,1536]{2,1,0:T(8,128)}, f32[2,8,128]{2,1,0:T(8,128)}) custom-call(bf16[2,512,1536]{2,1,0:T(8,128)(2,1)} %get-tuple-element.36.x_ref, bf16[2,512,256]{2,1,0:T(8,128)(2,1)} %get-tuple-element.37.bc_ref, f32[2,512,128]{2,1,0:T(8,128)} %get-tuple-element.38.step_ref, ...), custom_call_target="tpu_custom_call" | custom-call | flops 3221225472 | bytes 25165824 | tf_op jit(solution)/shard_map/pallas_call | solution.py:766
  660.2 9.5 %fusion.108 = bf16[2,2,4,2,48,1792]{5,4,3,2,1,0:T(8,128)(2,1)S(1)} fusion(bf16[2,2,4,2,48,1040]{5,4,3,2,1,0:T(8,128)(2,1)S(1)} %bitcast.471, bf16[1040,1792,1,1,1,1]{1,0,5,4,3,2:T(8,128)(2,1)} %bitcast.470), kind=kOutput, calls=%fused_computation.348 | convolution fusion | flops 5725224960 | bytes 12427264 | tf_op jit(solution)/shard_map/dot_general | solution.py:796
  676.1 6.1 fusion.2
  682.2 7.1 slice_add_fusion
  693.3 11.0 %collective-permute-done.71 = bf16[2,4,48,1792]{3,2,1,0:T(8,128)(2,1)} collective-permute-done((bf16[2,4,48,1792]{3,2,1,0:T(8,128)(2,1)}, bf16[2,4,48,1792]{3,2,1,0:T(8,128)(2,1)}, u32[]{:S(2)}, u32[]{:S(2)}) %collective-permute-start.71) | collective-permute-done | bytes 1376288 | tf_op jit(solution)/shard_map/ppermute | solution.py:102
  710.3 12.8 %collective-permute-done.72 = bf16[4,48,1792]{2,1,0:T(8,128)(2,1)S(1)} collective-permute-done((bf16[4,48,1792]{2,1,0:T(8,128)(2,1)S(1)}, bf16[4,48,1792]{2,1,0:T(8,128)(2,1)S(1)}, u32[]{:S(2)}, u32[]{:S(2)}) %collective-permute-start.72) | collective-permute-done | bytes 688160 | tf_op jit(solution)/shard_map/ppermute | solution.py:102
  736.9 6.8 collective-permute-done.74
  743.7 5.3 collective-permute-start.70
  749.1 4.4 collective-permute-done.69
  766.0 4.3 collective-permute-done.48
  770.3 7.1 multiply_reduce_fusion.1
  810.6 13.0 %collective-permute-done.45 = bf16[256,1536]{1,0:T(8,128)(2,1)} collective-permute-done((bf16[256,1536]{1,0:T(8,128)(2,1)S(1)}, bf16[256,1536]{1,0:T(8,128)(2,1)}, u32[]{:S(2)}, u32[]{:S(2)}) %collective-permute-start.45) | collective-permute-done | bytes 786464 | tf_op jit(solution)/shard_map/ppermute | solution.py:54
  (583 shorter events, 310.7 us)
Async XLA Ops:
  0.7 80.1 %collective-permute-start.34 = (bf16[2,48,1536]{2,1,0:T(8,128)(2,1)}, bf16[2,48,1536]{2,1,0:T(8,128)(2,1)}, u32[]{:S(2)}, u32[]{:S(2)}) collective-permute-start(bf16[2,48,1536]{2,1,0:T(8,128)(2,1)} %bitcast.491), channel_id=1, source_target_pairs={{0,2},{2,4},{4,6},{6,0},{1,3},{3,5},{5,7},{7,1},{8,10},{10,12},{12... | collective-permute-start | bytes 884744 | tf_op jit(solution)/shard_map/ppermute | solution.py:40
  3.7 80.0 %collective-permute-start.35 = (bf16[2,48,1536]{2,1,0:T(8,128)(2,1)}, bf16[2,48,1536]{2,1,0:T(8,128)(2,1)}, u32[]{:S(2)}, u32[]{:S(2)}) collective-permute-start(bf16[2,48,1536]{2,1,0:T(8,128)(2,1)} %bitcast.492), channel_id=1, source_target_pairs={{0,4},{2,6},{4,0},{6,2},{1,5},{3,7},{5,1},{7,3},{8,12},{10,14},{12... | collective-permute-start | bytes 884744 | tf_op jit(solution)/shard_map/ppermute | solution.py:40
  6.3 102.2 %collective-permute-start.36 = (bf16[2,48,1536]{2,1,0:T(8,128)(2,1)}, bf16[2,48,1536]{2,1,0:T(8,128)(2,1)}, u32[]{:S(2)}, u32[]{:S(2)}) collective-permute-start(bf16[2,48,1536]{2,1,0:T(8,128)(2,1)} %bitcast.493), channel_id=1, source_target_pairs={{0,6},{2,0},{4,2},{6,4},{1,7},{3,1},{5,3},{7,5},{8,14},{10,8},{12,... | collective-permute-start | bytes 884744 | tf_op jit(solution)/shard_map/ppermute | solution.py:40
  9.2 26.1 %collective-permute-start.3 = (bf16[1,1,1,1,1024]{4,3,2,1,0:T(2,128)(2,1)S(1)}, bf16[1,1,1,1,1024]{4,3,2,1,0:T(2,128)(2,1)S(1)}, u32[]{:S(2)}, u32[]{:S(2)}) collective-permute-start(bf16[1,1,1,1,1024]{4,3,2,1,0:T(2,128)(2,1)S(1)} %reshape.857), channel_id=1, source_target_pairs={{0,2},{2,4},{4,6},{6,0},{1,3},{3,5},{5,7},{7,1},{8,10},{10,12},{12... | collective-permute-start | bytes 6152 | tf_op jit(solution)/shard_map/ppermute | solution.py:40
  9.9 28.2 %collective-permute-start.4 = (bf16[1,1,1,1,1024]{4,3,2,1,0:T(2,128)(2,1)S(1)}, bf16[1,1,1,1,1024]{4,3,2,1,0:T(2,128)(2,1)S(1)}, u32[]{:S(2)}, u32[]{:S(2)}) collective-permute-start(bf16[1,1,1,1,1024]{4,3,2,1,0:T(2,128)(2,1)S(1)} %reshape.857), channel_id=1, source_target_pairs={{0,4},{2,6},{4,0},{6,2},{1,5},{3,7},{5,1},{7,3},{8,12},{10,14},{12... | collective-permute-start | bytes 6152 | tf_op jit(solution)/shard_map/ppermute | solution.py:40
  38.2 36.9 %collective-permute-start.22 = (bf16[48,1536]{1,0:T(8,128)(2,1)}, bf16[48,1536]{1,0:T(8,128)(2,1)}, u32[]{:S(2)}, u32[]{:S(2)}) collective-permute-start(bf16[48,1536]{1,0:T(8,128)(2,1)} %bitcast.257), channel_id=1, source_target_pairs={{0,8},{8,0},{1,9},{9,1},{2,10},{10,2},{3,11},{11,3},{4,12},{12,4},... | collective-permute-start | bytes 442376 | tf_op jit(solution)/shard_map/ppermute | solution.py:54
  52.8 85.6 %collective-permute-start.32 = (bf16[256,1536]{1,0:T(8,128)(2,1)}, bf16[256,1536]{1,0:T(8,128)(2,1)S(1)}, u32[]{:S(2)}, u32[]{:S(2)}) collective-permute-start(bf16[256,1536]{1,0:T(8,128)(2,1)} %get-tuple-element.96), channel_id=1, source_target_pairs={{0,1},{1,0},{2,3},{3,2},{4,5},{5,4},{6,7},{7,6},{8,9},{9,8},{10,11... | collective-permute-start | bytes 2359304 | tf_op jit(solution)/shard_map/ppermute | solution.py:54
  77.8 61.4 %collective-permute-start = (bf16[256,1536]{1,0:T(8,128)(2,1)}, bf16[256,1536]{1,0:T(8,128)(2,1)S(1)}, u32[]{:S(2)}, u32[]{:S(2)}) collective-permute-start(bf16[256,1536]{1,0:T(8,128)(2,1)} %get-tuple-element.97), channel_id=1, source_target_pairs={{0,1},{1,0},{2,3},{3,2},{4,5},{5,4},{6,7},{7,6},{8,9},{9,8},{10,11... | collective-permute-start | bytes 2359304 | tf_op jit(solution)/shard_map/ppermute | solution.py:54
  83.8 20.5 %collective-permute-start.24 = (bf16[2,48,1536]{2,1,0:T(8,128)(2,1)S(1)}, bf16[2,48,1536]{2,1,0:T(8,128)(2,1)S(1)}, u32[]{:S(2)}, u32[]{:S(2)}) collective-permute-start(bf16[2,48,1536]{2,1,0:T(8,128)(2,1)S(1)} %maximum_select_fusion.11), channel_id=1, source_target_pairs={{0,4},{2,6},{4,0},{6,2},{1,5},{3,7},{5,1},{7,3},{8,12},{10,14},{12... | collective-permute-start | bytes 884744 | tf_op jit(solution)/shard_map/ppermute | solution.py:40
  92.5 19.5 %collective-permute-start.25 = (bf16[2,48,1536]{2,1,0:T(8,128)(2,1)S(1)}, bf16[2,48,1536]{2,1,0:T(8,128)(2,1)S(1)}, u32[]{:S(2)}, u32[]{:S(2)}) collective-permute-start(bf16[2,48,1536]{2,1,0:T(8,128)(2,1)S(1)} %maximum_select_fusion.11), channel_id=1, source_target_pairs={{0,6},{2,0},{4,2},{6,4},{1,7},{3,1},{5,3},{7,5},{8,14},{10,8},{12,... | collective-permute-start | bytes 884744 | tf_op jit(solution)/shard_map/ppermute | solution.py:40
  108.5 26.9 %collective-permute-start.11 = (bf16[2,48,1920]{2,1,0:T(8,128)(2,1)S(1)}, bf16[2,48,1920]{2,1,0:T(8,128)(2,1)S(1)}, u32[]{:S(2)}, u32[]{:S(2)}) collective-permute-start(bf16[2,48,1920]{2,1,0:T(8,128)(2,1)S(1)} %maximum_select_fusion.9), channel_id=1, source_target_pairs={{0,4},{2,6},{4,0},{6,2},{1,5},{3,7},{5,1},{7,3},{8,12},{10,14},{12... | collective-permute-start | bytes 1105928 | tf_op jit(solution)/shard_map/ppermute | solution.py:40
  112.0 25.0 %collective-permute-start.12 = (bf16[2,48,1920]{2,1,0:T(8,128)(2,1)S(1)}, bf16[2,48,1920]{2,1,0:T(8,128)(2,1)S(1)}, u32[]{:S(2)}, u32[]{:S(2)}) collective-permute-start(bf16[2,48,1920]{2,1,0:T(8,128)(2,1)S(1)} %maximum_select_fusion.9), channel_id=1, source_target_pairs={{0,6},{2,0},{4,2},{6,4},{1,7},{3,1},{5,3},{7,5},{8,14},{10,8},{12,... | collective-permute-start | bytes 1105928 | tf_op jit(solution)/shard_map/ppermute | solution.py:40
  121.0 22.9 %collective-permute-start.37 = (bf16[4,48,1536]{2,1,0:T(8,128)(2,1)S(1)}, bf16[4,48,1536]{2,1,0:T(8,128)(2,1)S(1)}, u32[]{:S(2)}, u32[]{:S(2)}) collective-permute-start(bf16[4,48,1536]{2,1,0:T(8,128)(2,1)S(1)} %get-tuple-element.102), channel_id=1, source_target_pairs={{0,1},{1,0},{2,3},{3,2},{4,5},{5,4},{6,7},{7,6},{8,9},{9,8},{10,11... | collective-permute-start | bytes 1769480 | tf_op jit(solution)/shard_map/ppermute | solution.py:40
  137.0 95.9 %collective-permute-start.40 = (bf16[4,48,1536]{2,1,0:T(8,128)(2,1)S(1)}, bf16[4,48,1536]{2,1,0:T(8,128)(2,1)S(1)}, u32[]{:S(2)}, u32[]{:S(2)}) collective-permute-start(bf16[4,48,1536]{2,1,0:T(8,128)(2,1)S(1)} %get-tuple-element.101), channel_id=1, source_target_pairs={{0,16},{16,0},{1,17},{17,1},{2,18},{18,2},{3,19},{19,3},{4,20},{20... | collective-permute-start | bytes 1769480 | tf_op jit(solution)/shard_map/ppermute | solution.py:40
  138.4 95.2 %collective-permute-start.41 = (bf16[4,48,1536]{2,1,0:T(8,128)(2,1)S(1)}, bf16[4,48,1536]{2,1,0:T(8,128)(2,1)S(1)}, u32[]{:S(2)}, u32[]{:S(2)}) collective-permute-start(bf16[4,48,1536]{2,1,0:T(8,128)(2,1)S(1)} %get-tuple-element.101), channel_id=1, source_target_pairs={{0,1},{1,0},{2,3},{3,2},{4,5},{5,4},{6,7},{7,6},{8,9},{9,8},{10,11... | collective-permute-start | bytes 1769480 | tf_op jit(solution)/shard_map/ppermute | solution.py:40
  139.2 26.5 %collective-permute-start.26 = (bf16[4,48,1536]{2,1,0:T(8,128)(2,1)S(1)}, bf16[4,48,1536]{2,1,0:T(8,128)(2,1)S(1)}, u32[]{:S(2)}, u32[]{:S(2)}) collective-permute-start(bf16[4,48,1536]{2,1,0:T(8,128)(2,1)S(1)} %get-tuple-element.104), channel_id=1, source_target_pairs={{0,1},{1,0},{2,3},{3,2},{4,5},{5,4},{6,7},{7,6},{8,9},{9,8},{10,11... | collective-permute-start | bytes 1769480 | tf_op jit(solution)/shard_map/ppermute | solution.py:40
  143.9 33.1 %collective-permute-start.27 = (bf16[4,48,1536]{2,1,0:T(8,128)(2,1)S(1)}, bf16[4,48,1536]{2,1,0:T(8,128)(2,1)S(1)}, u32[]{:S(2)}, u32[]{:S(2)}) collective-permute-start(bf16[4,48,1536]{2,1,0:T(8,128)(2,1)S(1)} %get-tuple-element.104), channel_id=1, source_target_pairs={{0,16},{16,0},{1,17},{17,1},{2,18},{18,2},{3,19},{19,3},{4,20},{20... | collective-permute-start | bytes 1769480 | tf_op jit(solution)/shard_map/ppermute | solution.py:40
  151.7 83.5 %collective-permute-start.29 = (bf16[4,48,1536]{2,1,0:T(8,128)(2,1)S(1)}, bf16[4,48,1536]{2,1,0:T(8,128)(2,1)S(1)}, u32[]{:S(2)}, u32[]{:S(2)}) collective-permute-start(bf16[4,48,1536]{2,1,0:T(8,128)(2,1)S(1)} %get-tuple-element.103), channel_id=1, source_target_pairs={{0,16},{16,0},{1,17},{17,1},{2,18},{18,2},{3,19},{19,3},{4,20},{20... | collective-permute-start | bytes 1769480 | tf_op jit(solution)/shard_map/ppermute | solution.py:40
  177.0 28.4 %collective-permute-start.14 = (bf16[4,48,1920]{2,1,0:T(8,128)(2,1)S(1)}, bf16[4,48,1920]{2,1,0:T(8,128)(2,1)S(1)}, u32[]{:S(2)}, u32[]{:S(2)}) collective-permute-start(bf16[4,48,1920]{2,1,0:T(8,128)(2,1)S(1)} %get-tuple-element.100), channel_id=1, source_target_pairs={{0,16},{16,0},{1,17},{17,1},{2,18},{18,2},{3,19},{19,3},{4,20},{20... | collective-permute-start | bytes 2211848 | tf_op jit(solution)/shard_map/ppermute | solution.py:40
  182.5 34.5 %collective-permute-start.39 = (bf16[4,48,1536]{2,1,0:T(8,128)(2,1)S(1)}, bf16[4,48,1536]{2,1,0:T(8,128)(2,1)S(1)}, u32[]{:S(2)}, u32[]{:S(2)}) collective-permute-start(bf16[4,48,1536]{2,1,0:T(8,128)(2,1)S(1)} %collective-permute-done.37), channel_id=1, source_target_pairs={{0,16},{16,0},{1,17},{17,1},{2,18},{18,2},{3,19},{19,3},{4,20},{20... | collective-permute-start | bytes 1769480 | tf_op jit(solution)/shard_map/ppermute | solution.py:40
  205.4 57.4 %collective-permute-start.30 = (bf16[4,48,1536]{2,1,0:T(8,128)(2,1)S(1)}, bf16[4,48,1536]{2,1,0:T(8,128)(2,1)S(1)}, u32[]{:S(2)}, u32[]{:S(2)}) collective-permute-start(bf16[4,48,1536]{2,1,0:T(8,128)(2,1)S(1)} %get-tuple-element.103), channel_id=1, source_target_pairs={{0,1},{1,0},{2,3},{3,2},{4,5},{5,4},{6,7},{7,6},{8,9},{9,8},{10,11... | collective-permute-start | bytes 1769480 | tf_op jit(solution)/shard_map/ppermute | solution.py:40
  231.3 32.2 %collective-permute-start.16 = (bf16[4,48,1920]{2,1,0:T(8,128)(2,1)S(1)}, bf16[4,48,1920]{2,1,0:T(8,128)(2,1)S(1)}, u32[]{:S(2)}, u32[]{:S(2)}) collective-permute-start(bf16[4,48,1920]{2,1,0:T(8,128)(2,1)S(1)} %get-tuple-element.99), channel_id=1, source_target_pairs={{0,16},{16,0},{1,17},{17,1},{2,18},{18,2},{3,19},{19,3},{4,20},{20... | collective-permute-start | bytes 2211848 | tf_op jit(solution)/shard_map/ppermute | solution.py:40
  232.9 44.9 %collective-permute-start.17 = (bf16[4,48,1920]{2,1,0:T(8,128)(2,1)S(1)}, bf16[4,48,1920]{2,1,0:T(8,128)(2,1)S(1)}, u32[]{:S(2)}, u32[]{:S(2)}) collective-permute-start(bf16[4,48,1920]{2,1,0:T(8,128)(2,1)S(1)} %get-tuple-element.99), channel_id=1, source_target_pairs={{0,1},{1,0},{2,3},{3,2},{4,5},{5,4},{6,7},{7,6},{8,9},{9,8},{10,11... | collective-permute-start | bytes 2211848 | tf_op jit(solution)/shard_map/ppermute | solution.py:40
  233.5 28.7 %collective-permute-start.42 = (bf16[4,48,1536]{2,1,0:T(8,128)(2,1)S(1)}, bf16[4,48,1536]{2,1,0:T(8,128)(2,1)S(1)}, u32[]{:S(2)}, u32[]{:S(2)}) collective-permute-start(bf16[4,48,1536]{2,1,0:T(8,128)(2,1)S(1)} %collective-permute-done.40), channel_id=1, source_target_pairs={{0,1},{1,0},{2,3},{3,2},{4,5},{5,4},{6,7},{7,6},{8,9},{9,8},{10,11... | collective-permute-start | bytes 1769480 | tf_op jit(solution)/shard_map/ppermute | solution.py:40
  235.2 59.9 %collective-permute-start.33 = (bf16[512,1536]{1,0:T(8,128)(2,1)S(1)}, bf16[512,1536]{1,0:T(8,128)(2,1)S(1)}, u32[]{:S(2)}, u32[]{:S(2)}) collective-permute-start(bf16[512,1536]{1,0:T(8,128)(2,1)S(1)} %bitcast.455), channel_id=1, source_target_pairs={{0,8},{8,0},{1,9},{9,1},{2,10},{10,2},{3,11},{11,3},{4,12},{12,4},... | collective-permute-start | bytes 4718600 | tf_op jit(solution)/shard_map/ppermute | solution.py:54
  263.5 26.9 %collective-permute-start.1 = (bf16[512,1536]{1,0:T(8,128)(2,1)S(1)}, bf16[512,1536]{1,0:T(8,128)(2,1)S(1)}, u32[]{:S(2)}, u32[]{:S(2)}) collective-permute-start(bf16[512,1536]{1,0:T(8,128)(2,1)S(1)} %bitcast.447), channel_id=1, source_target_pairs={{0,8},{8,0},{1,9},{9,1},{2,10},{10,2},{3,11},{11,3},{4,12},{12,4},... | collective-permute-start | bytes 4718600 | tf_op jit(solution)/shard_map/ppermute | solution.py:54
  330.8 40.3 %collective-permute-start.19 = (f32[2,8,128]{2,1,0:T(8,128)}, f32[2,8,128]{2,1,0:T(8,128)S(1)}, u32[]{:S(2)}, u32[]{:S(2)}) collective-permute-start(f32[2,8,128]{2,1,0:T(8,128)} %get-tuple-element.40), channel_id=1, source_target_pairs={{0,2},{2,4},{4,6},{6,0},{1,3},{3,5},{5,7},{7,1},{8,10},{10,12},{12... | collective-permute-start | bytes 24584 | tf_op jit(solution)/shard_map/ppermute | solution.py:40
  330.9 40.9 %all-to-all-start = ((bf16[4,2,32,1536]{3,2,1,0:T(8,128)(2,1)}), bf16[4,2,32,1536]{3,2,1,0:T(8,128)(2,1)}, u32[]{:S(2)}, u32[]{:S(2)}) async-start(bf16[4,2,32,1536]{3,2,1,0:T(8,128)(2,1)} %get-tuple-element.41), calls=%async_computation | async-start | bytes 1572864 | tf_op jit(solution)/shard_map/all_to_all | solution.py:650
  339.6 31.6 %collective-permute-start.20 = (f32[2,8,128]{2,1,0:T(8,128)S(1)}, f32[2,8,128]{2,1,0:T(8,128)S(1)}, u32[]{:S(2)}, u32[]{:S(2)}) collective-permute-start(f32[2,8,128]{2,1,0:T(8,128)S(1)} %copy-done.48), channel_id=1, source_target_pairs={{0,4},{2,6},{4,0},{6,2},{1,5},{3,7},{5,1},{7,3},{8,12},{10,14},{12... | collective-permute-start | bytes 24584 | tf_op jit(solution)/shard_map/ppermute | solution.py:40
  342.5 28.6 %collective-permute-start.21 = (f32[2,8,128]{2,1,0:T(8,128)S(1)}, f32[2,8,128]{2,1,0:T(8,128)S(1)}, u32[]{:S(2)}, u32[]{:S(2)}) collective-permute-start(f32[2,8,128]{2,1,0:T(8,128)S(1)} %copy-done.48), channel_id=1, source_target_pairs={{0,6},{2,0},{4,2},{6,4},{1,7},{3,1},{5,3},{7,5},{8,14},{10,8},{12,... | collective-permute-start | bytes 24584 | tf_op jit(solution)/shard_map/ppermute | solution.py:40
  464.4 64.8 %collective-permute-start.77 = (bf16[4,2,48,1536]{3,2,0,1:T(8,128)(2,1)}, bf16[4,2,48,1536]{3,2,0,1:T(8,128)(2,1)}, u32[]{:S(2)}, u32[]{:S(2)}) collective-permute-start(bf16[4,2,48,1536]{3,2,0,1:T(8,128)(2,1)} %bitcast.444), channel_id=1, source_target_pairs={{0,16},{16,0},{1,17},{17,1},{2,18},{18,2},{3,19},{19,3},{4,20},{20... | collective-permute-start | bytes 3538952 | tf_op jit(solution)/shard_map/ppermute | solution.py:102
  466.1 66.3 %collective-permute-start.82 = (bf16[2,4,48,1536]{3,2,1,0:T(8,128)(2,1)}, bf16[2,4,48,1536]{3,2,1,0:T(8,128)(2,1)}, u32[]{:S(2)}, u32[]{:S(2)}) collective-permute-start(bf16[2,4,48,1536]{3,2,1,0:T(8,128)(2,1)} %dynamic-slice_bitcast_fusion.2), channel_id=1, source_target_pairs={{0,1},{1,0},{2,3},{3,2},{4,5},{5,4},{6,7},{7,6},{8,9},{9,8},{10,11... | collective-permute-start | bytes 3538952 | tf_op jit(solution)/shard_map/ppermute | solution.py:102
  466.6 69.2 %all-to-all-start.2 = ((bf16[4,2,32,1536]{3,2,1,0:T(8,128)(2,1)}), bf16[4,2,32,1536]{3,2,1,0:T(8,128)(2,1)}, u32[]{:S(2)}, u32[]{:S(2)}) async-start(bf16[4,2,32,1536]{3,2,1,0:T(8,128)(2,1)} %get-tuple-element.50), calls=%async_computation.2 | async-start | bytes 1572864 | tf_op jit(solution)/shard_map/all_to_all | solution.py:650
  479.6 64.4 %collective-permute-start.60 = (bf16[2,4,48,1536]{3,2,1,0:T(8,128)(2,1)}, bf16[2,4,48,1536]{3,2,1,0:T(8,128)(2,1)}, u32[]{:S(2)}, u32[]{:S(2)}) collective-permute-start(bf16[2,4,48,1536]{3,2,1,0:T(8,128)(2,1)} %dynamic-slice_bitcast_fusion.3), channel_id=1, source_target_pairs={{0,1},{1,0},{2,3},{3,2},{4,5},{5,4},{6,7},{7,6},{8,9},{9,8},{10,11... | collective-permute-start | bytes 3538952 | tf_op jit(solution)/shard_map/ppermute | solution.py:102
  482.4 64.8 %collective-permute-start.55 = (bf16[4,2,48,1536]{3,2,0,1:T(8,128)(2,1)}, bf16[4,2,48,1536]{3,2,0,1:T(8,128)(2,1)}, u32[]{:S(2)}, u32[]{:S(2)}) collective-permute-start(bf16[4,2,48,1536]{3,2,0,1:T(8,128)(2,1)} %bitcast.445), channel_id=1, source_target_pairs={{0,16},{16,0},{1,17},{17,1},{2,18},{18,2},{3,19},{19,3},{4,20},{20... | collective-permute-start | bytes 3538952 | tf_op jit(solution)/shard_map/ppermute | solution.py:102
  490.5 279.8 %collective-permute-start.44 = (f32[512,1536]{1,0:T(8,128)}, f32[512,1536]{1,0:T(8,128)}, u32[]{:S(2)}, u32[]{:S(2)}) collective-permute-start(f32[512,1536]{1,0:T(8,128)} %dynamic-slice_bitcast_fusion), channel_id=1, source_target_pairs={{0,8},{8,0},{1,9},{9,1},{2,10},{10,2},{3,11},{11,3},{4,12},{12,4},... | collective-permute-start | bytes 9437192 | tf_op jit(solution)/shard_map/ppermute | solution.py:54
  531.9 18.5 %collective-permute-start.78 = (bf16[4,48,1536]{2,1,0:T(8,128)(2,1)}, bf16[4,48,1536]{2,1,0:T(8,128)(2,1)}, u32[]{:S(2)}, u32[]{:S(2)}) collective-permute-start(bf16[4,48,1536]{2,1,0:T(8,128)(2,1)} %dynamic-slice_bitcast_fusion.11), channel_id=1, source_target_pairs={{0,1},{1,0},{2,3},{3,2},{4,5},{5,4},{6,7},{7,6},{8,9},{9,8},{10,11... | collective-permute-start | bytes 1769480 | tf_op jit(solution)/shard_map/ppermute | solution.py:102
  535.2 30.5 %collective-permute-start.83 = (bf16[4,48,1536]{2,1,0:T(8,128)(2,1)}, bf16[4,48,1536]{2,1,0:T(8,128)(2,1)}, u32[]{:S(2)}, u32[]{:S(2)}) collective-permute-start(bf16[4,48,1536]{2,1,0:T(8,128)(2,1)} %dynamic-slice_bitcast_fusion.10), channel_id=1, source_target_pairs={{0,16},{16,0},{1,17},{17,1},{2,18},{18,2},{3,19},{19,3},{4,20},{20... | collective-permute-start | bytes 1769480 | tf_op jit(solution)/shard_map/ppermute | solution.py:102
  539.0 77.4 %all-to-all-start.3 = ((bf16[4,2,32,1536]{3,2,1,0:T(8,128)(2,1)}), bf16[4,2,32,1536]{3,2,1,0:T(8,128)(2,1)}, u32[]{:S(2)}, u32[]{:S(2)}) async-start(bf16[4,2,32,1536]{3,2,1,0:T(8,128)(2,1)} %pad_maximum_fusion.2), calls=%async_computation.3 | async-start | bytes 1572864 | tf_op jit(solution)/shard_map/all_to_all | solution.py:650
  548.8 20.6 %collective-permute-start.56 = (bf16[4,48,1536]{2,1,0:T(8,128)(2,1)S(1)}, bf16[4,48,1536]{2,1,0:T(8,128)(2,1)S(1)}, u32[]{:S(2)}, u32[]{:S(2)}) collective-permute-start(bf16[4,48,1536]{2,1,0:T(8,128)(2,1)S(1)} %dynamic-slice_bitcast_fusion.13), channel_id=1, source_target_pairs={{0,1},{1,0},{2,3},{3,2},{4,5},{5,4},{6,7},{7,6},{8,9},{9,8},{10,11... | collective-permute-start | bytes 1769480 | tf_op jit(solution)/shard_map/ppermute | solution.py:102
  551.7 46.6 %collective-permute-start.79 = (bf16[48,1536]{1,0:T(8,128)(2,1)S(1)}, bf16[48,1536]{1,0:T(8,128)(2,1)S(1)}, u32[]{:S(2)}, u32[]{:S(2)}) collective-permute-start(bf16[48,1536]{1,0:T(8,128)(2,1)S(1)} %get-tuple-element.121), channel_id=1, source_target_pairs={{0,2},{2,4},{4,6},{6,0},{1,3},{3,5},{5,7},{7,1},{8,10},{10,12},{12... | collective-permute-start | bytes 442376 | tf_op jit(solution)/shard_map/ppermute | solution.py:102
  584.4 19.2 %collective-permute-start.80 = (bf16[48,1536]{1,0:T(8,128)(2,1)S(1)}, bf16[48,1536]{1,0:T(8,128)(2,1)S(1)}, u32[]{:S(2)}, u32[]{:S(2)}) collective-permute-start(bf16[48,1536]{1,0:T(8,128)(2,1)S(1)} %get-tuple-element.123), channel_id=1, source_target_pairs={{0,4},{2,6},{4,0},{6,2},{1,5},{3,7},{5,1},{7,3},{8,12},{10,14},{12... | collective-permute-start | bytes 442376 | tf_op jit(solution)/shard_map/ppermute | solution.py:102
  671.3 32.9 %collective-permute-start.71 = (bf16[2,4,48,1792]{3,2,1,0:T(8,128)(2,1)}, bf16[2,4,48,1792]{3,2,1,0:T(8,128)(2,1)}, u32[]{:S(2)}, u32[]{:S(2)}) collective-permute-start(bf16[2,4,48,1792]{3,2,1,0:T(8,128)(2,1)} %dynamic-slice_bitcast_fusion.1), channel_id=1, source_target_pairs={{0,1},{1,0},{2,3},{3,2},{4,5},{5,4},{6,7},{7,6},{8,9},{9,8},{10,11... | collective-permute-start | bytes 4128776 | tf_op jit(solution)/shard_map/ppermute | solution.py:102
  675.3 32.6 %collective-permute-start.66 = (bf16[4,2,48,1792]{3,2,0,1:T(8,128)(2,1)}, bf16[4,2,48,1792]{3,2,0,1:T(8,128)(2,1)}, u32[]{:S(2)}, u32[]{:S(2)}) collective-permute-start(bf16[4,2,48,1792]{3,2,0,1:T(8,128)(2,1)} %bitcast.443), channel_id=1, source_target_pairs={{0,16},{16,0},{1,17},{17,1},{2,18},{18,2},{3,19},{19,3},{4,20},{20... | collective-permute-start | bytes 4128776 | tf_op jit(solution)/shard_map/ppermute | solution.py:102
  693.1 67.2 %collective-permute-start.47 = (f32[520,1536]{1,0:T(8,128)}, f32[520,1536]{1,0:T(8,128)}, u32[]{:S(2)}, u32[]{:S(2)}) collective-permute-start(f32[520,1536]{1,0:T(8,128)} %fusion.4), channel_id=1, source_target_pairs={{0,8},{8,0},{1,9},{9,1},{2,10},{10,2},{3,11},{11,3},{4,12},{12,4},... | collective-permute-start | bytes 9584648 | tf_op jit(solution)/shard_map/ppermute | solution.py:54
  709.7 18.2 %collective-permute-start.67 = (bf16[4,48,1792]{2,1,0:T(8,128)(2,1)S(1)}, bf16[4,48,1792]{2,1,0:T(8,128)(2,1)S(1)}, u32[]{:S(2)}, u32[]{:S(2)}) collective-permute-start(bf16[4,48,1792]{2,1,0:T(8,128)(2,1)S(1)} %dynamic-slice_bitcast_fusion.9), channel_id=1, source_target_pairs={{0,1},{1,0},{2,3},{3,2},{4,5},{5,4},{6,7},{7,6},{8,9},{9,8},{10,11... | collective-permute-start | bytes 2064392 | tf_op jit(solution)/shard_map/ppermute | solution.py:102
  787.2 20.7 %collective-permute-start.49 = (bf16[256,1536]{1,0:T(8,128)(2,1)S(1)}, bf16[256,1536]{1,0:T(8,128)(2,1)}, u32[]{:S(2)}, u32[]{:S(2)}) collective-permute-start(bf16[256,1536]{1,0:T(8,128)(2,1)S(1)} %get-tuple-element.92), channel_id=1, source_target_pairs={{0,1},{1,0},{2,3},{3,2},{4,5},{5,4},{6,7},{7,6},{8,9},{9,8},{10,11... | collective-permute-start | bytes 2359304 | tf_op jit(solution)/shard_map/ppermute | solution.py:54
  797.0 26.6 %collective-permute-start.45 = (bf16[256,1536]{1,0:T(8,128)(2,1)S(1)}, bf16[256,1536]{1,0:T(8,128)(2,1)}, u32[]{:S(2)}, u32[]{:S(2)}) collective-permute-start(bf16[256,1536]{1,0:T(8,128)(2,1)S(1)} %get-tuple-element.94), channel_id=1, source_target_pairs={{0,1},{1,0},{2,3},{3,2},{4,5},{5,4},{6,7},{7,6},{8,9},{9,8},{10,11... | collective-permute-start | bytes 2359304 | tf_op jit(solution)/shard_map/ppermute | solution.py:54
  (103 other events, 1282.0 us)

commit v2 on v1

v2 whole, which is shorter than its diff:
```python
import functools
import types

import jax
import jax.numpy as jnp
from jax import lax
from jax.experimental import pallas as pl
from jax.experimental.pallas import tpu as pltpu
from jax.sharding import Mesh
from jax.sharding import PartitionSpec as P

H = 48
P_SIZE = 64
NS = 128
CONV = 4
SPAN = 256
E = 3072
CH = 3328

HC = H // 2
EC = E // 2
HALO = 16
OWN = EC
STEP = EC + NS
OTHER = EC + 2 * NS
WIDE = EC + 3 * NS
BACK = EC + 2 * NS

EPSILON = 1e-05
BF16 = jnp.bfloat16
VM = 60
F32 = jnp.float32


def settle(live):
    live.__dict__.update(lax.optimization_barrier(dict(live.__dict__)))


def others(piece, axis):
    size = lax.axis_size(axis)
    here = lax.axis_index(axis)
    moved = []
    for step in range(1, size):
        route = [(i, (i + step) % size) for i in range(size)]
        moved.append((lax.rem(here - step + size, size), lax.ppermute(piece, axis, route)))
    return moved


def everyone(piece, axis):
    return [(lax.axis_index(axis), piece)] + others(piece, axis)


def shared(value, axes):
    count = 1
    for axis in axes:
        count *= lax.axis_size(axis)
    return lax.all_to_all(jnp.broadcast_to(value, (count,) + value.shape), axes, 0, 0, tiled=True)


def by_index(axis, mine, other):
    first = lax.axis_index(axis) == 0
    return jnp.where(first, jnp.stack([mine, other]), jnp.stack([other, mine]))


def swapped(piece, axis):
    return lax.ppermute(piece, axis, [(0, 1), (1, 0)])


def take(value, index, axis):
    return lax.dynamic_index_in_dim(value, index, axis, keepdims=False)


def copy_plan(items):
    values, scalars, plan = [], [], []
    for piece, source, out, target in items:
        known = [i for i, v in enumerate(values) if v is piece]
        if not known:
            values.append(piece)
            known = [len(values) - 1]
        at = []
        for index in target:
            if index is None or isinstance(index, int):
                at.append(index)
            else:
                scalars.append(index)
                at.append((len(scalars) - 1,))
        plan.append((known[0], source, out, at))
    return values, jnp.stack(scalars).astype(jnp.int32), plan


def copy_all(plan, table, inputs, results, sems):
    copies = []
    for number, (known, source, out, at) in enumerate(plan):
        here = tuple(slice(None) if i is None else i for i in source)
        there = tuple(slice(None) if i is None else (table[i[0]] if isinstance(i, tuple) else i) for i in at)
        origin = inputs[known].at[here] if here else inputs[known]
        copies.append(pltpu.make_async_copy(origin, results[out].at[there], sems.at[number]))
    for copy in copies:
        copy.start()
    for copy in copies:
        copy.wait()


ANYWHERE = pl.BlockSpec(memory_space=pltpu.HBM)
NO_COST = pl.CostEstimate(flops=0, bytes_accessed=1024, transcendentals=0)


def assemble(outs, items, dtype):
    values, table, plan = copy_plan(items)
    count = len(values)

    def kernel(table_ref, *refs):
        copy_all(plan, table_ref, refs[:count], refs[count:-1], refs[-1])

    return pl.pallas_call(
        kernel,
        in_specs=[pl.BlockSpec(memory_space=pltpu.SMEM)] + [ANYWHERE] * count,
        out_specs=[pl.BlockSpec(memory_space=pltpu.VMEM)] * len(outs),
        out_shape=[jax.ShapeDtypeStruct(dims, dtype) for dims in outs],
        scratch_shapes=[pltpu.SemaphoreType.DMA((len(plan),))],
        compiler_params=pltpu.CompilerParams(vmem_limit_bytes=16 * 1024 * 1024),
        cost_estimate=NO_COST,
    )(table, *values)


ORDERS = (("y", "x"), ("x", "y"))


def join_line(everybody):
    _, rows, columns = everybody[0][1].shape
    items = [(piece, (half,), half, (index,)) for index, piece in everybody for half in range(2)]
    return assemble([(len(everybody), rows, columns)] * 2, items, everybody[0][1].dtype)


def plane_first(line):
    return [everyone(line[half], ORDERS[half][0]) for half in range(2)]


def plane_stack(held):
    items, outs = [], []
    for half, pieces in enumerate(held):
        outs.append((len(pieces),) + pieces[0][1].shape)
        items += [(piece, (), half, (index,)) for index, piece in pieces]
    return assemble(outs, items, held[0][0][1].dtype)


def plane_second(both):
    return [everyone(both[half], ORDERS[half][1]) for half in range(2)]


def plane_items(held, inner):
    nx, ny = lax.axis_size("x"), lax.axis_size("y")
    _, nz, rows, columns = held[0][0][1].shape
    dims = (nx, nz, ny, 2, rows, columns) if inner else (nx, 2, nz, ny, rows, columns)
    items = []
    for half, pieces in enumerate(held):
        for index, piece in pieces:
            for k in range(piece.shape[0]):
                at_x, at_y = (index, k) if half == 0 else (k, index)
                items.append((piece, (k,), 0, (at_x, None, at_y, half) if inner else (at_x, half, None, at_y)))
    return dims, items


def cut(value, axis, dim):
    size = lax.axis_size(axis)
    here = lax.axis_index(axis)
    return take(value, here, dim), [take(value, lax.rem(here + step, size), dim) for step in range(1, size)]


def move(held, axis):
    mine, going = held
    size = lax.axis_size(axis)
    came = []
    for step, piece in enumerate(going, 1):
        came.append(lax.ppermute(piece, axis, [(i, (i + step) % size) for i in range(size)]))
    return mine, came


def add_up(held):
    mine, came = held
    total = mine.astype(F32)
    for piece in came:
        total = total + piece.astype(F32)
    return total


def cut_first(whole, inner):
    return [
        cut(whole[:, :, :, half] if inner else whole[:, half], axis, 0 if axis == "x" else 2)
        for half, (_, axis) in enumerate(ORDERS)
    ]


def move_first(held):
    return [move(one, axis) for one, (_, axis) in zip(held, ORDERS)]


def cut_second(held):
    return [cut(add_up(one).astype(BF16), axis, 0 if axis == "x" else 1) for one, (axis, _) in zip(held, ORDERS)]


def move_second(held):
    return [move(one, axis) for one, (axis, _) in zip(held, ORDERS)]


def cut_line(held):
    return cut(jnp.stack([add_up(one).astype(BF16) for one in held]), "z", 1)


def sum_everywhere(value):
    for axis in ("core", "x", "z", "y"):
        size = lax.axis_size(axis)
        step = 1
        while step < size:
            route = [(i, i ^ step) for i in range(size)]
            value = value + lax.ppermute(value, axis, route)
            step *= 2
    return value


def nn(a, b):
    return lax.dot_general(a, b, (((1,), (0,)), ((), ())), preferred_element_type=F32)


def nt(a, b):
    return lax.dot_general(a, b, (((1,), (1,)), ((), ())), preferred_element_type=F32)


def tn(a, b):
    return lax.dot_general(a, b, (((0,), (0,)), ((), ())), preferred_element_type=F32)


def pieces_of(value, count):
    parts = []
    rest = value
    for index in range(count):
        part = rest.astype(BF16)
        parts.append(part)
        if index < count - 1:
            rest = rest - part.astype(F32)
    return parts


PIECE = 32


def nt_fine(a, b):
    a_high, a_low = pieces_of(a, 2)
    b_high, b_low = pieces_of(b, 2)
    return nt(jnp.concatenate([a_high, a_low, a_high], axis=1), jnp.concatenate([b_high, b_high, b_low], axis=1))


def head_map():
    row = lax.rem(lax.broadcasted_iota(jnp.int32, (NS, EC), 0), PIECE)
    lane = lax.broadcasted_iota(jnp.int32, (NS, EC), 1)
    inside = (lane >= row * P_SIZE) & (lane < row * P_SIZE + P_SIZE)
    return jnp.where(inside, 1.0, 0.0).astype(BF16)


def head_sums():
    row = lax.broadcasted_iota(jnp.int32, (EC, NS), 0)
    lane = lax.broadcasted_iota(jnp.int32, (EC, NS), 1)
    inside = (row >= lane * P_SIZE) & (row < lane * P_SIZE + P_SIZE)
    return jnp.where(inside, 1.0, 0.0).astype(BF16)


def packed(value):
    lane = lax.broadcasted_iota(jnp.int32, value.shape, 1)
    high, mid, low = (p.astype(F32) for p in pieces_of(jnp.where(lane < HC, value, 0.0), 3))
    return (high + pltpu.roll(mid, PIECE, 1) + pltpu.roll(low, 2 * PIECE, 1)).astype(BF16)


def spread(value, heads):
    return nn(packed(value), heads)


def gathered_heads(value, sums, count=1):
    return sum(nn(part, sums) for part in pieces_of(value, count))


def triangle(kind):
    row = lax.broadcasted_iota(jnp.int32, (SPAN, SPAN), 0)
    col = lax.broadcasted_iota(jnp.int32, (SPAN, SPAN), 1)
    keep = {"ge": row >= col, "gt": row > col, "le": row <= col}[kind]
    return jnp.where(keep, 1.0, 0.0)


def exact_sum(matrix, value):
    low = matrix.astype(BF16)
    return sum(nn(low, part) for part in pieces_of(value, 3))


def sigmoid(v):
    return 0.5 * jnp.tanh(0.5 * v) + 0.5


def softplus(v):
    return jnp.maximum(v, 0.0) + jnp.log1p(jnp.exp(-jnp.abs(v)))


def call(kernel, grid, in_specs, out_specs, out_shape, scratch=(), vmem=VM, **more):
    return pl.pallas_call(
        kernel,
        grid=grid,
        in_specs=in_specs,
        out_specs=out_specs,
        out_shape=out_shape,
        scratch_shapes=list(scratch),
        compiler_params=pltpu.CompilerParams(vmem_limit_bytes=vmem * 1024 * 1024),
        cost_estimate=NO_COST,
        **more,
    )


def shape(*dims, dtype=F32):
    return jax.ShapeDtypeStruct(dims, dtype)


def fixed(*dims):
    return pl.BlockSpec(dims, lambda *_: (0,) * len(dims))


def conv_kernel(rows, nz, proj, taps, heads_par, x_out, bc_out, step_out, cum_out, state_out, local_out):
    heads = head_map()
    spans = rows // SPAN
    lower = triangle("ge")
    state = jnp.zeros((NS, EC), F32)
    total = jnp.zeros((1, NS), F32)
    core_one = heads_par[3:4, :] > 0.5
    for span in range(spans):
        start = HALO + span * SPAN

        def activated(first, width):
            running = taps[4:5, first : first + width]
            for k in range(CONV):
                at = start - (CONV - 1) + k
                running = running + taps[k : k + 1, first : first + width] * proj[0, at : at + SPAN, first : first + width]
            return running * sigmoid(running)

        own = activated(OWN, NS)
        other = activated(OTHER, NS)
        write_full = jnp.where(core_one, other, own)
        write = write_full.astype(BF16)
        here = slice(span * SPAN, span * SPAN + SPAN)
        bc_out[0, here, :NS] = write_full
        bc_out[0, here, NS:] = jnp.where(core_one, own, other)
        raw = proj[0, start : start + SPAN, STEP : STEP + NS] + heads_par[0:1, :]
        step = softplus(raw)
        cum = exact_sum(lower, -step * heads_par[1:2, :])
        step_out[0, here] = step
        cum_out[0, here] = cum
        last = cum[SPAN - 1 : SPAN]
        tail_low = packed(jnp.exp(last - cum) * step)
        local_out[0, span] = state.astype(BF16)
        decay = spread(jnp.broadcast_to(jnp.exp(last), (8, NS)), heads)[0:1]
        wide = EC // 2
        fresh = []
        for half in range(2):
            cols = slice(half * wide, half * wide + wide)
            x = activated(half * wide, wide)
            x_out[0, here, cols] = x
            fresh.append(tn(write, (x * nn(tail_low, heads[:, cols])).astype(BF16)))
        state = state * decay + jnp.concatenate(fresh, axis=1)
        total = total + last
    depth = NS // nz
    for group in range(nz):
        state_out[group, 0, :, :EC] = state[group * depth : (group + 1) * depth].astype(BF16)
    row = lax.broadcasted_iota(jnp.int32, (depth, NS), 0)
    high, mid, low = (part.astype(F32) for part in pieces_of(total, 3))
    total_rows = jnp.where(row == 0, high, jnp.where(row == 1, mid, jnp.where(row == 2, low, 0.0))).astype(BF16)
    for group in range(nz):
        state_out[group, 0, :, EC:] = total_rows


def intra_kernel(x_ref, bc_ref, step_ref, cum_ref, heads_par, out_ref, xs_ref, cross_ref, cumt_ref):
    heads = head_map()
    step_wide = spread(step_ref[0], heads)
    xs_ref[...] = (x_ref[0] * step_wide).astype(BF16)
    cum = cum_ref[0]
    cumt_ref[...] = cum.T
    cross_ref[...] = nt_fine(bc_ref[0, :, NS:], bc_ref[0, :, :NS]) * triangle("ge")
    skip = spread(jnp.broadcast_to(heads_par[2:3, :], (8, NS)), heads)[0:1]
    out_ref[0] = x_ref[0] * skip
    low = lax.broadcasted_iota(jnp.int32, (SPAN, NS), 1) < P_SIZE

    def pair(p, carry):
        lanes = pl.ds(pl.multiple_of(p * NS, NS), NS)
        xs = xs_ref[:, lanes]
        made = []
        for j in range(2):
            h = 2 * p + j
            col = pltpu.roll(cum, lax.rem(NS - h, NS), 1)[:, 0:1]
            row = cumt_ref[pl.ds(h, 1), :]
            mix = jnp.exp(jnp.minimum(col - row, 0.0)) * cross_ref[...]
            made.append(nn(mix.astype(BF16), xs))
        out_ref[0, :, lanes] += jnp.where(low, made[0], made[1])
        return carry

    lax.fori_loop(0, HC // 2, pair, 0)


def span_state(state_ref, local_ref, before, heads):
    whole = jnp.concatenate([state_ref[g, 0] for g in range(state_ref.shape[0])], axis=0)
    decay = spread(jnp.broadcast_to(jnp.exp(before), (8, NS)), heads)[0:1]
    return whole.astype(F32) * decay + local_ref[0, 0].astype(F32)


def finish_kernel(part_ref, bc_ref, cum_ref, before_ref, state_ref, local_ref, gate_ref, dmix_ref, gain_ref, out_ref, sums_ref):
    heads = head_map()
    state = span_state(state_ref, local_ref, before_ref[0, 0, 0:1], heads).astype(BF16)
    grown = spread(jnp.exp(cum_ref[0]), heads)
    y = part_ref[0] + grown * nn(bc_ref[0, :, NS:].astype(BF16), state)
    out_ref[0] = y
    gate = gate_ref[0]
    gated = y * gate * sigmoid(gate)
    squares = jnp.sum(gated * gated, axis=1, keepdims=True)
    slopes = jnp.sum(gated * gain_ref[0:1, :] * dmix_ref[0], axis=1, keepdims=True)
    lane = lax.broadcasted_iota(jnp.int32, (SPAN, NS), 1)
    sums_ref[0] = jnp.where(lane == 0, squares, jnp.where(lane == 1, slopes, 0.0))


def gate_kernel(
    spans, nz, y_ref, gate_ref, dmix_ref, sums_ref, gain_ref, bc_ref, cum_ref,
    mix_out, dy_out, dgate_out, ggain_out, state_out, local_out, run_ref,
):
    step = pl.program_id(1)
    heads = head_map()
    squares = sums_ref[0, :, 0:1]
    slopes = sums_ref[0, :, 1:2]
    scale = lax.rsqrt(squares / E + EPSILON)
    y = y_ref[0]
    gate = gate_ref[0]
    soft = sigmoid(gate)
    silu = gate * soft
    gated = y * silu
    gain = gain_ref[0:1, :]
    dmix = dmix_ref[0]
    mix_out[0] = (gated * scale * gain).astype(BF16)
    dgated = scale * (gain * dmix - gated * (scale * scale * slopes / E))
    dy = dgated * silu
    dy_out[0] = dy
    dgate_out[0] = (dgated * y * (soft * (1.0 + gate * (1.0 - soft)))).astype(BF16)

    @pl.when((step == 0) & (pl.program_id(0) == 0))
    def _():
        ggain_out[...] = jnp.zeros_like(ggain_out)

    ggain_out[...] += jnp.broadcast_to(jnp.sum(gated * scale * dmix, axis=0, keepdims=True), (8, EC))

    @pl.when(step == 0)
    def _():
        run_ref[...] = jnp.zeros_like(run_ref)

    cum = cum_ref[0]
    grown = spread(jnp.exp(cum), heads)
    fresh = tn(bc_ref[0, :, NS:].astype(BF16), (dy * grown).astype(BF16))
    local_out[0, 0] = run_ref[...].astype(BF16)
    run_ref[...] = fresh + run_ref[...] * grown[SPAN - 1 : SPAN]

    @pl.when(step == spans - 1)
    def _():
        depth = NS // nz
        for group in range(nz):
            state_out[group, 0] = run_ref[group * depth : (group + 1) * depth].astype(BF16)


def back_kernel(kept, x_ref, bc_ref, step_ref, cum_ref, before_ref, dy_ref, state_ref, local_ref, *refs):
    dxs_out, dbc_out, dcum_out, dstep_out, cross_ref, dcross_ref, cumt_ref, rows_ref = refs[kept:]
    heads = head_map()
    sums = head_sums()
    cum = cum_ref[0]
    step = step_ref[0]
    cumt_ref[...] = cum.T
    write = bc_ref[0, :, :NS].astype(BF16)
    read = bc_ref[0, :, NS:].astype(BF16)
    mask = triangle("le")
    cross_ref[...] = nt_fine(bc_ref[0, :, :NS], bc_ref[0, :, NS:]) * mask
    dcross_ref[...] = jnp.zeros_like(dcross_ref)
    rows_ref[...] = jnp.zeros_like(rows_ref)
    lane = lax.broadcasted_iota(jnp.int32, (SPAN, NS), 1)
    low = lane < P_SIZE

    def pair(p, cols):
        lanes = pl.ds(pl.multiple_of(p * NS, NS), NS)
        x_high, x_low = (part.astype(F32) for part in pieces_of(x_ref[0, :, lanes], 2))
        dy, dy_low = pieces_of(dy_ref[0, :, lanes], 2)
        right = jnp.concatenate([dy, dy, dy_low], axis=1)
        made = []
        for j in range(2):
            h = 2 * p + j
            col = pltpu.roll(cum, lax.rem(NS - h, NS), 1)[:, 0:1]
            step_col = pltpu.roll(step, lax.rem(NS - h, NS), 1)[:, 0:1]
            row = cumt_ref[pl.ds(h, 1), :]
            decay = jnp.exp(jnp.minimum(row - col, 0.0))
            mine = low if j == 0 else ~low
            high = jnp.where(mine, x_high, 0.0).astype(BF16)
            rest = jnp.where(mine, x_low, 0.0).astype(BF16)
            slope = nt(jnp.concatenate([high, rest, high], axis=1), right) * decay
            cross = cross_ref[...]
            cols = jnp.where(lane == h, jnp.sum(slope * cross, axis=1, keepdims=True), cols)
            slope = slope * step_col
            dcross_ref[...] += slope
            rows_ref[pl.ds(h, 1), :] = jnp.sum(slope * cross, axis=0, keepdims=True)
            made.append(nn((decay * cross).astype(BF16), dy))
        dxs_out[0, :, lanes] = jnp.where(low, made[0], made[1])
        return cols

    cols = lax.fori_loop(0, HC // 2, pair, jnp.zeros((SPAN, NS), F32))
    dcross = (dcross_ref[...] * mask).astype(BF16)
    state = span_state(state_ref, local_ref, before_ref[0, 0, 0:1], heads).astype(BF16)
    grown = spread(jnp.exp(cum), heads)
    dye = dy_ref[0] * grown
    inter = gathered_heads(dye * nn(read, state), sums)
    dstep_out[0] = cols
    dbc_out[0, :, :NS] = nn(dcross, read)
    dbc_out[0, :, NS:] = tn(dcross, write) + nt(dye.astype(BF16), state)
    dcum_out[0] = rows_ref[...].T - step * cols + inter


def close_kernel(
    rows, nz, x_ref, bc_ref, step_ref, cum_ref, dy_ref, proj_ref, taps, heads_par, dxs_ref, dbc_ref, dcum_ref, dstep_ref,
    state_ref, local_ref, back_ref, blocal_ref, dproj_out, mine_out, theirs_out, gtaps_out, ghead_out, dpre_ref,
):
    core_one = heads_par[3:4, :] > 0.5
    heads = head_map()
    sums = head_sums()
    spans = rows // SPAN
    upper = triangle("le")
    below = triangle("gt")
    whole_in = jnp.concatenate([state_ref[g, 0] for g in range(nz)], axis=0).astype(F32)
    whole_back = jnp.concatenate([back_ref[g, 0] for g in range(nz)], axis=0).astype(F32)
    lasts = [cum_ref[0, (c + 1) * SPAN - 1 : (c + 1) * SPAN] for c in range(spans)]
    skip = spread(jnp.broadcast_to(heads_par[2:3, :], (8, NS)), heads)[0:1]
    real = lax.broadcasted_iota(jnp.int32, (SPAN, NS), 1) < HC
    dpre_ref[:HALO] = jnp.zeros((HALO, EC), F32)
    dpre_ref[HALO + rows :] = jnp.zeros((HALO, EC), F32)
    zero_row = jnp.zeros((1, NS), F32)
    gbias, gdecay, gskip = zero_row, zero_row, zero_row
    for span in range(spans):
        here = slice(span * SPAN, span * SPAN + SPAN)
        before = sum(lasts[:span], zero_row)
        after = sum(lasts[span + 1 :], zero_row)
        both = spread(jnp.exp(jnp.concatenate([before, after, lasts[span], jnp.zeros((5, NS), F32)], axis=0)), heads)
        state = whole_in * both[0:1] + local_ref[0, span].astype(F32)
        back = whole_back * both[1:2] + blocal_ref[0, span].astype(F32)
        back_low = back.astype(BF16)
        at_last = gathered_heads(
            jnp.broadcast_to(jnp.sum(state * back, axis=0, keepdims=True) * both[2:3], (8, EC)), sums, 2
        )[0:1]
        write = bc_ref[0, here, :NS].astype(BF16)
        cum = cum_ref[0, here]
        step = step_ref[0, here]
        x = x_ref[0, here]
        dy = dy_ref[0, here]
        tail = spread(jnp.exp(lasts[span] - cum), heads)
        step_wide = spread(step, heads)
        from_back = tail * nn(write, back_low)
        dxs = dxs_ref[0, here] + from_back
        later = gathered_heads(x * from_back, sums)
        dstep = dstep_ref[0, here] + later
        moved = step * later
        dwrite = dbc_ref[0, here, :NS] + nt((x * tail * step_wide).astype(BF16), back_low)
        dread = dbc_ref[0, here, NS:]
        mine_out[0, here] = jnp.where(core_one, dread, dwrite)
        theirs_out[0, here] = jnp.where(core_one, dwrite, dread)
        dlog = exact_sum(upper, dcum_ref[0, here]) + exact_sum(below, moved) + at_last
        raw = proj_ref[0, HALO + span * SPAN : HALO + span * SPAN + SPAN, STEP : STEP + NS] + heads_par[0:1, :]
        draw = jnp.where(real, (dstep - heads_par[1:2, :] * dlog) * sigmoid(raw), 0.0)
        dproj_out[0, HALO + span * SPAN : HALO + span * SPAN + SPAN, STEP : STEP + NS] = draw.astype(BF16)
        gbias = gbias + jnp.sum(draw, axis=0, keepdims=True)
        gdecay = gdecay + jnp.sum(jnp.where(real, dlog * (-step * heads_par[1:2, :]), 0.0), axis=0, keepdims=True)
        gskip = gskip + gathered_heads(jnp.broadcast_to(jnp.sum(dy * x, axis=0, keepdims=True), (8, EC)), sums, 3)[0:1]
        dx = dxs * step_wide + skip * dy
        start = HALO + span * SPAN
        pre = taps[4:5, :EC]
        for k in range(CONV):
            at = start - (CONV - 1) + k
            pre = pre + taps[k : k + 1, :EC] * proj_ref[0, at : at + SPAN, :EC]
        soft = sigmoid(pre)
        dpre_ref[start : start + SPAN] = dx * (soft * (1.0 + pre * (1.0 - soft)))
    conv_back(rows, dpre_ref, proj_ref, taps, 0, EC, dproj_out, 0, gtaps_out)
    dproj_out[0, :HALO, STEP : STEP + NS] = jnp.zeros((HALO, NS), BF16)
    ghead_out[0] = jnp.concatenate([gbias, gdecay, gskip, jnp.zeros((5, NS), F32)], axis=0)


def conv_back(rows, dpre_ref, proj_ref, taps, first, width, dproj_out, out_first, gtaps_out):
    sums = [jnp.zeros((1, width), F32)] * (CONV + 1)
    blocks = [(0, HALO)] + [(HALO + s * SPAN, SPAN) for s in range(rows // SPAN)]
    for start, count in blocks:
        running = jnp.zeros((count, width), F32)
        for k in range(CONV):
            at = start + (CONV - 1) - k
            running = running + taps[k : k + 1, first : first + width] * dpre_ref[at : at + count]
        dproj_out[0, start : start + count, out_first : out_first + width] = running.astype(BF16)
        if count == SPAN:
            dpre = dpre_ref[start : start + count]
            for k in range(CONV):
                at = start - (CONV - 1) + k
                sums[k] = sums[k] + jnp.sum(dpre * proj_ref[0, at : at + count, first : first + width], axis=0, keepdims=True)
            sums[CONV] = sums[CONV] + jnp.sum(dpre, axis=0, keepdims=True)
    gtaps_out[0, :, :width] = jnp.concatenate(sums + [jnp.zeros((3, width), F32)], axis=0)


def own_kernel(rows, dproj_in, mine_ref, came_ref, proj_ref, taps, dproj_out, gtaps_out, dpre_ref):
    dpre_ref[:HALO] = jnp.zeros((HALO, NS), F32)
    dpre_ref[HALO + rows :] = jnp.zeros((HALO, NS), F32)
    for span in range(rows // SPAN):
        start = HALO + span * SPAN
        pre = taps[4:5, :]
        for k in range(CONV):
            at = start - (CONV - 1) + k
            pre = pre + taps[k : k + 1, :] * proj_ref[0, at : at + SPAN]
        soft = sigmoid(pre)
        here = slice(span * SPAN, span * SPAN + SPAN)
        dconv = mine_ref[0, here] + came_ref[0, here]
        dpre_ref[start : start + SPAN] = dconv * (soft * (1.0 + pre * (1.0 - soft)))
    conv_back(rows, dpre_ref, proj_ref, taps, 0, NS, dproj_out, 0, gtaps_out)


def outer_kernel(halo, a_ref, b_ref, out_ref):
    slots, _, width = a_ref.shape
    left = a_ref[...][:, halo:].reshape(-1, width)
    right = b_ref[...].reshape(left.shape[0], -1)
    out_ref[...] = tn(left, right).astype(BF16)


def outer(a, b, halo=0):
    slots, tall, left = a.shape
    rows, right = b.shape[1:]
    tile = 256
    return call(
        functools.partial(outer_kernel, halo),
        (left // tile,),
        [pl.BlockSpec((slots, tall, tile), lambda i: (0, 0, i)), fixed(slots, rows, right)],
        pl.BlockSpec((tile, right), lambda i: (i, 0)),
        shape(left, right, dtype=BF16),
    )(a, b)


def rows_kernel(turned, halo, a_ref, b_ref, out_ref):
    value = a_ref[0, halo:]
    out_ref[0] = (nt if turned else nn)(value, b_ref[...])


def by_rows(a, b, turned=False, halo=0):
    slots, tall, depth = a.shape
    right = b.shape[0 if turned else 1]
    return call(
        functools.partial(rows_kernel, turned, halo),
        (slots,),
        [pl.BlockSpec((1, tall, depth), lambda s: (s, 0, 0)), fixed(*b.shape)],
        pl.BlockSpec((1, tall - halo, right), lambda s: (s, 0, 0)),
        shape(slots, tall - halo, right),
    )(a, b)


def by_rows_of(a, held, inner, turned=False, halo=0):
    dims, items = plane_items(held, inner)
    wide = dims[-1]
    deep = EC if inner else dims[0] * dims[1] * dims[2] * dims[3] * dims[4]
    if dims[4] % 16:
        whole = assemble([dims], items, BF16)[0].reshape(deep, wide)
        return by_rows(a, whole, turned, halo), whole
    values, table, plan = copy_plan(items)
    count = len(values)
    slots, tall, depth = a.shape
    right = deep if turned else wide

    def kernel(table_ref, a_ref, *refs):
        pieces, out_ref, whole_ref, held_ref, sems, whole_sem = refs[:count], *refs[count:]
        store = pltpu.make_async_copy(held_ref, whole_ref, whole_sem)

        @pl.when(pl.program_id(0) == 0)
        def _():
            copy_all(plan, table_ref, pieces, [held_ref], sems)
            store.start()

        matrix = held_ref[...].reshape(deep, wide)
        out_ref[0] = (nt if turned else nn)(a_ref[0, halo:], matrix)

        @pl.when(pl.program_id(0) == slots - 1)
        def _():
            store.wait()

    out, whole = call(
        kernel,
        (slots,),
        [pl.BlockSpec(memory_space=pltpu.SMEM), pl.BlockSpec((1, tall, depth), lambda s: (s, 0, 0))]
        + [ANYWHERE] * count,
        [pl.BlockSpec((1, tall - halo, right), lambda s: (s, 0, 0)), ANYWHERE],
        [shape(slots, tall - halo, right), shape(*dims, dtype=BF16)],
        [pltpu.VMEM(dims, BF16), pltpu.SemaphoreType.DMA((len(plan),)), pltpu.SemaphoreType.DMA],
    )(table, a, *values)
    return out, whole.reshape(deep, wide)


def normed_kernel(core_ref, dproj_ref, dgate_ref, scan_ref, gate_ref, own_ref, other_ref):
    scan, gate = scan_ref[...], gate_ref[...]
    core = core_ref[0]
    for slot, out_ref in ((core, own_ref), (1 - core, other_ref)):
        out_ref[:HALO] = nt(dproj_ref[slot, :HALO], scan)
        out_ref[HALO:] = nt(dproj_ref[slot, HALO:], scan) + nt(dgate_ref[slot], gate)


SMALL = pl.BlockSpec(memory_space=pltpu.SMEM)


def to_normed(core, d_proj, d_gate, scan_weight, gate_weight):
    slots, tall, _ = d_proj.shape
    features = gate_weight.shape[0]
    tile = 256
    return call(
        normed_kernel,
        (features // tile,),
        [
            SMALL, fixed(slots, tall, BACK), fixed(slots, tall - HALO, EC),
            pl.BlockSpec((tile, BACK), lambda i: (i, 0)), pl.BlockSpec((tile, EC), lambda i: (i, 0)),
        ],
        [pl.BlockSpec((tall, tile), lambda i: (0, i))] * 2,
        [shape(tall, features)] * 2,
    )(core.reshape(1), d_proj, d_gate, scan_weight, gate_weight)


def two_kernel(core_ref, a_ref, b_ref, own_ref, other_ref):
    core = core_ref[0]
    own_ref[...] = nn(a_ref[core], b_ref[...])
    other_ref[...] = nn(a_ref[1 - core], b_ref[...])


def two_slots(core, a, b):
    slots, rows, depth = a.shape
    right = b.shape[1]
    tile = 256
    return call(
        two_kernel,
        (right // tile,),
        [SMALL, fixed(slots, rows, depth), pl.BlockSpec((depth, tile), lambda i: (0, i))],
        [pl.BlockSpec((rows, tile), lambda i: (0, i))] * 2,
        [shape(rows, right)] * 2,
    )(core.reshape(1), a, b)


def valid_rows(bounds_ref, count):
    row = lax.broadcasted_iota(jnp.int32, (count, 1), 0) + pl.program_id(0) * count + bounds_ref[0]
    return jnp.where(row < bounds_ref[1], 1.0, 0.0)


def block_kernel(bounds_ref, in_ref, own_ref, came_ref, out_ref, sums_ref):
    valid = valid_rows(bounds_ref, SPAN)
    residual = in_ref[...].astype(F32)
    mixed = own_ref[...] + came_ref[...]
    value = valid * (residual + mixed)
    out_ref[...] = value.astype(BF16)
    lane = lax.broadcasted_iota(jnp.int32, (8, NS), 1)
    total = jnp.zeros((8, NS), F32)
    for number, part in enumerate((valid * residual * residual, valid * mixed * mixed, value * value)):
        part = jnp.sum(jnp.sum(part, axis=1, keepdims=True), axis=0, keepdims=True)
        total = jnp.where(lane == number, part, total)

    @pl.when(pl.program_id(0) == 0)
    def _():
        sums_ref[...] = jnp.zeros_like(sums_ref)

    sums_ref[...] += total


def block_rows(bounds, own_in, mixer_own, mixer_came):
    rows, features = own_in.shape
    tile = pl.BlockSpec((SPAN, features), lambda i: (i, 0))
    return call(
        block_kernel,
        (rows // SPAN,),
        [SMALL, tile, tile, tile],
        [tile, fixed(8, NS)],
        [shape(rows, features, dtype=BF16), shape(8, NS)],
    )(bounds, own_in, mixer_own, mixer_came)


def input_kernel(bounds_ref, in_ref, grad_ref, own_ref, came_ref, later_ref, across_ref, gain_ref, out_ref, gain_out):
    valid = valid_rows(bounds_ref, SPAN)
    at = pl.program_id(0)
    start = pl.multiple_of(HALO + at * SPAN, HALO)
    slope = own_ref[pl.ds(start, SPAN)] + came_ref[pl.ds(start, SPAN)]
    tail = jnp.where(at == pl.num_programs(0) - 1, later_ref[...] + across_ref[...], 0.0)
    slope = jnp.concatenate([slope[: SPAN - HALO], slope[SPAN - HALO :] + tail], axis=0)
    residual = in_ref[...].astype(F32)
    features = residual.shape[1]
    scale = lax.rsqrt(jnp.sum(residual * residual, axis=1, keepdims=True) / features + EPSILON)
    unit = residual * scale
    along = slope * gain_ref[...]
    mean = jnp.sum(along * unit, axis=1, keepdims=True) / features
    out_ref[...] = (valid * grad_ref[...].astype(F32) + scale * (along - unit * mean)).astype(BF16)

    @pl.when(at == 0)
    def _():
        gain_out[...] = jnp.zeros_like(gain_out)

    gain_out[...] += jnp.broadcast_to(jnp.sum(slope * unit, axis=0, keepdims=True), gain_out.shape)


def input_rows(bounds, own_in, own_grad, d_own, d_came, back_own, back_came, gain):
    rows, features = own_in.shape
    tile = pl.BlockSpec((SPAN, features), lambda i: (i, 0))
    return call(
        input_kernel,
        (rows // SPAN,),
        [
            SMALL, tile, tile, fixed(*d_own.shape), fixed(*d_came.shape), fixed(HALO, features), fixed(HALO, features),
            fixed(1, features),
        ],
        [tile, fixed(8, features)],
        [shape(rows, features, dtype=BF16), shape(8, features)],
    )(bounds, own_in, own_grad, d_own, d_came, back_own, back_came, gain)


def shards(
    block_in,
    lengths,
    norm_gain,
    in_weight,
    conv_weight,
    conv_bias,
    step_bias,
    decay_log,
    skip_gain,
    out_gain,
    out_weight,
    grad_out,
):
    slot_count, row_count, features = block_in.shape
    nx, nz, ny = lax.axis_size("x"), lax.axis_size("z"), lax.axis_size("y")
    ix, iz, iy = lax.axis_index("x"), lax.axis_index("z"), lax.axis_index("y")
    core = lax.axis_index("core")
    rows = ny * row_count
    spans = rows // SPAN
    deep = in_weight.shape[0]
    thin = out_weight.shape[0]

    def half_of(value, width, which):
        parts = value.reshape(value.shape[:-1] + (nx, 2, width // (2 * nx)))
        chosen = take(parts, which, value.ndim)
        return chosen.reshape(value.shape[:-1] + (width // 2,))

    def one_slot(block):
        return by_index("y", take(block, iy, 0), swapped(take(block, 1 - iy, 0), "y")).reshape(rows, features)

    def by_slots(value):
        parts = value.reshape(ny, row_count, features)
        return take(parts, iy, 0), take(parts, 1 - iy, 0)

    def exchange(value):
        return lax.all_to_all(value, "z", 0, 0, tiled=True)

    def scaled(value):
        wide = value.astype(F32)
        return wide * lax.rsqrt(jnp.mean(wide * wide, axis=-1, keepdims=True) + EPSILON)

    tall = HALO + rows
    own_length = take(lengths, (ix * 2 + core) * slot_count + iy, 0)
    bounds = jnp.stack([iz * rows, own_length]).astype(jnp.int32)
    live = types.SimpleNamespace()

    def columns_of(which):
        heads_in = half_of(in_weight[:, E : 2 * E], E, which)
        write = in_weight[:, 2 * E : 2 * E + NS]
        read = in_weight[:, 2 * E + NS : E + CH]
        first = which == 0
        steps = jnp.pad(half_of(in_weight[:, E + CH :], H, which), ((0, 0), (0, NS - HC)))
        gate = half_of(in_weight[:, :E], E, which)
        return jnp.concatenate(
            [heads_in, jnp.where(first, write, read), steps, jnp.where(first, read, write), gate], axis=1
        )

    live.mine = columns_of(core)
    live.came = swapped(columns_of(1 - core), "core")
    live.block_in, live.grad_out = block_in, grad_out
    live.small = jnp.concatenate([norm_gain, conv_weight.reshape(-1), conv_bias, out_gain])
    settle(live)

    pieces = by_index("core", live.mine, live.came)
    live.scan = everyone(pieces[:, :, :WIDE], "z")
    live.gate = pieces[:, :, WIDE:]
    live.own_in = one_slot(live.block_in)
    live.own_grad = one_slot(live.grad_out)
    live.small = shared(jnp.pad(live.small, (0, -live.small.shape[0] % 1024)).reshape(-1, NS), ("x", "core", "z", "y"))
    del live.mine, live.came, live.block_in, live.grad_out
    settle(live)

    live.scan = join_line(live.scan)
    settle(live)
    live.scan = plane_first(live.scan)
    last_rows = live.own_in[rows - HALO :]
    live.other_in = swapped(live.own_in, "core")
    live.before_own = lax.ppermute(last_rows, "z", [(i, i + 1) for i in range(nz - 1)])
    across = [(c * nz + i, (1 - c) * nz + i + 1) for c in range(2) for i in range(nz - 1)]
    live.before_other = lax.ppermute(last_rows, ("core", "z"), across)
    small = live.small.reshape(2 * nx * nz * ny, -1)
    chan = CH // (2 * nx * nz * ny)
    gain_in = small[:, :deep].reshape(1, features).astype(F32)
    taps_all = small[:, deep : deep + CONV * chan].reshape(-1, CONV, chan).transpose(1, 0, 2).reshape(CONV, CH)
    at = deep + CONV * chan
    bias_all = small[:, at : at + chan].reshape(1, CH)
    gain_out_all = small[:, at + chan : at + chan + thin].reshape(E)
    taps_all = jnp.concatenate([taps_all, bias_all, jnp.zeros((3, CH), BF16)], axis=0).astype(F32)
    own_taps = jnp.where(core == 0, taps_all[:, E : E + NS], taps_all[:, E + NS :])
    other_taps = jnp.where(core == 0, taps_all[:, E + NS :], taps_all[:, E : E + NS])
    taps = jnp.concatenate(
        [half_of(taps_all[:, :E], E, core), own_taps, jnp.zeros((8, NS), F32), other_taps], axis=1
    )
    gain_out = jnp.broadcast_to(half_of(gain_out_all, E, core).astype(F32), (8, EC))

    def head_row(value):
        return jnp.pad(half_of(value, H, core), (0, NS - HC))

    heads_par = jnp.stack(
        [
            head_row(step_bias),
            head_row(jnp.exp(decay_log)),
            head_row(skip_gain),
            jnp.full((NS,), core, F32),
        ]
        + [jnp.zeros((NS,), F32)] * 4
    )

    live.gain_in, live.taps, live.own_taps, live.gain_out, live.heads_par = gain_in, taps, own_taps, gain_out, heads_par
    del live.small
    settle(live)

    live.scan = plane_stack(live.scan)
    settle(live)
    live.scan = plane_second(live.scan)
    live.gate = everyone(live.gate, "z")
    joined = jnp.concatenate(
        [by_index("core", live.before_own, live.before_other), by_index("core", live.own_in, live.other_in)], axis=1
    )
    live.normed = (scaled(joined) * live.gain_in).astype(BF16)
    del live.before_own, live.before_other, live.other_in
    settle(live)

    live.gate = join_line(live.gate)
    settle(live)
    live.gate = plane_first(live.gate)
    live.other_grad = swapped(live.own_grad, "core")
    live.proj, live.scan_weight = by_rows_of(live.normed, live.scan, False)
    del live.scan
    settle(live)

    live.gate = plane_stack(live.gate)
    live.out_rows = out_weight.reshape(2, thin // 2, features)
    settle(live)
    live.gate = plane_second(live.gate)
    live.out_rows = everyone(live.out_rows, "z")
    proj, taps, heads_par = live.proj, live.taps, live.heads_par
    whole_row = lambda *dims: pl.BlockSpec((1,) + dims, lambda s: (s,) + (0,) * len(dims))
    x, bc, step, cum, state_part, local = call(
        functools.partial(conv_kernel, rows, nz),
        (2,),
        [whole_row(tall, WIDE), fixed(8, WIDE), fixed(8, NS)],
        [
            whole_row(rows, EC), whole_row(rows, 2 * NS), whole_row(rows, NS), whole_row(rows, NS),
            pl.BlockSpec((nz, 1, NS // nz, EC + NS), lambda s: (0, s, 0, 0)), whole_row(spans, NS, EC),
        ],
        [
            shape(2, rows, EC), shape(2, rows, 2 * NS), shape(2, rows, NS), shape(2, rows, NS),
            shape(nz, 2, NS // nz, EC + NS, dtype=BF16), shape(2, spans, NS, EC, dtype=BF16),
        ],
    )(proj, taps, heads_par)

    live.state_part, live.x, live.bc, live.step, live.cum, live.local = state_part, x, bc, step, cum, local
    settle(live)

    live.out_rows = join_line(live.out_rows)
    settle(live)
    live.ends = exchange(live.state_part)
    live.out_rows = plane_first(live.out_rows)
    x, bc, step, cum, heads_par = live.x, live.bc, live.step, live.cum, live.heads_par
    in_span = lambda *dims: pl.BlockSpec((1, SPAN) + dims, lambda s, c: (s, c) + (0,) * len(dims))
    local_span = pl.BlockSpec((1, 1, NS, EC), lambda s, c: (s, c, 0, 0))
    state_spec = pl.BlockSpec((nz, 1, NS // nz, EC), lambda s, c: (0, s, 0, 0))
    before_spec = pl.BlockSpec((1, 1, 8, NS), lambda s, c: (s, c, 0, 0))
    part = call(
        intra_kernel,
        (2, spans),
        [in_span(EC), in_span(2 * NS), in_span(NS), in_span(NS), fixed(8, NS)],
        in_span(EC),
        shape(2, rows, EC),
        [
            pltpu.VMEM((SPAN, EC), BF16), pltpu.VMEM((SPAN, SPAN), F32), pltpu.VMEM((NS, SPAN), F32),
        ],
    )(x, bc, step, cum, heads_par)

    live.part = part
    del live.state_part
    settle(live)

    decays = jnp.exp(jnp.sum(live.ends[:, :, :3, EC : EC + HC].astype(F32), axis=2))
    live.decays = jnp.broadcast_to(decays[..., None], decays.shape + (P_SIZE,)).reshape(nz, 2, 1, EC)
    ends = live.ends[..., :EC].astype(F32)
    running = jnp.zeros_like(ends[0])
    starts = []
    for k in range(nz):
        starts.append(running.astype(BF16))
        running = running * live.decays[k] + ends[k]
    live.starts = jnp.stack(starts)
    live.out_rows = plane_stack(live.out_rows)
    del live.ends
    settle(live)
    live.state_in = exchange(live.starts)
    live.out_rows = plane_second(live.out_rows)
    live.gate, live.gate_weight = by_rows_of(live.normed, live.gate, False, halo=HALO)

    positions = iz * rows + jnp.arange(rows, dtype=jnp.int32)
    slot_lengths = jnp.stack(
        [take(lengths, (ix * 2 + s) * slot_count + iy, 0) for s in range(2)]
    )
    all_valid = positions[None, :] < slot_lengths[:, None]

    all_grad = by_index("core", live.own_grad, live.other_grad)
    live.d_mix = jnp.where(all_valid[:, :, None], all_grad, jnp.zeros_like(all_grad))
    del live.starts, live.other_grad
    settle(live)

    d_mixer_in, live.back_weight = by_rows_of(live.d_mix, live.out_rows, True, turned=True)
    span_ends = live.cum.reshape(2, spans, SPAN, NS)[:, :, SPAN - 1]
    before = jnp.cumsum(span_ends, axis=1) - span_ends
    live.before = jnp.broadcast_to(before[:, :, None], (2, spans, 8, NS))
    part, bc, cum, before, state_in, local, gate, gain_out = (
        live.part, live.bc, live.cum, live.before, live.state_in, live.local, live.gate, live.gain_out
    )
    ssm_out, sums = call(
        finish_kernel,
        (2, spans),
        [
            in_span(EC), in_span(2 * NS), in_span(NS), before_spec, state_spec, local_span, in_span(EC), in_span(EC),
            fixed(8, EC),
        ],
        [in_span(EC), in_span(NS)],
        [shape(2, rows, EC), shape(2, rows, NS)],
    )(part, bc, cum, before, state_in, local, gate, d_mixer_in, gain_out)
    sums = sums + swapped(sums, "core")
    rev = lambda *dims: pl.BlockSpec((1, SPAN) + dims, lambda s, c: (s, spans - 1 - c) + (0,) * len(dims))
    rev_local = pl.BlockSpec((1, 1, NS, EC), lambda s, c: (s, spans - 1 - c, 0, 0))
    mixer_in, d_ssm, d_gate, g_gain_out, back_part, back_local = call(
        functools.partial(gate_kernel, spans, nz),
        (2, spans),
        [rev(EC), rev(EC), rev(EC), rev(NS), fixed(8, EC), rev(2 * NS), rev(NS)],
        [rev(EC), rev(EC), rev(EC), fixed(8, EC), state_spec, rev_local],
        [
            shape(2, rows, EC, dtype=BF16), shape(2, rows, EC), shape(2, rows, EC, dtype=BF16), shape(8, EC),
            shape(nz, 2, NS // nz, EC, dtype=BF16), shape(2, spans, NS, EC, dtype=BF16),
        ],
        [pltpu.VMEM((NS, EC), F32)],
    )(ssm_out, gate, d_mixer_in, sums, gain_out, bc, cum)
    live.mixer_in, live.d_ssm, live.d_gate, live.back_part, live.back_local = mixer_in, d_ssm, d_gate, back_part, back_local
    live.g_gain_out = g_gain_out
    del live.part, live.gate, live.out_rows, live.gain_out
    settle(live)

    live.tails = exchange(live.back_part)
    live.out_sums = outer(live.mixer_in, live.d_mix)
    live.gate_sums = outer(live.normed, live.d_gate, HALO)
    live.mixer_own, live.mixer_part = two_slots(core, live.mixer_in, live.back_weight)
    del live.back_part, live.d_mix, live.mixer_in, live.back_weight
    settle(live)

    tails = live.tails.astype(F32)
    running = jnp.zeros_like(tails[0])
    backs = [None] * nz
    for k in reversed(range(nz)):
        backs[k] = running.astype(BF16)
        running = running * live.decays[k] + tails[k]
    live.backs = jnp.stack(backs)
    live.out_sums = cut_first(live.out_sums.reshape(nx, nz, ny, 2, thin // 2, features), True)
    live.gate_sums = cut_first(live.gate_sums.reshape(nx, 2, nz, ny, deep, EC), False)
    del live.tails, live.decays
    settle(live)
    live.back_in = exchange(live.backs)
    live.out_sums = move_first(live.out_sums)

    def back_call(slot, kept):
        one = lambda *dims: pl.BlockSpec((1, SPAN) + dims, lambda c: (slot, c) + (0,) * len(dims))
        anywhere = [pl.BlockSpec(memory_space=pl.ANY)] * len(kept)
        return call(
            functools.partial(back_kernel, len(kept)),
            (spans,),
            [
                one(EC), one(2 * NS), one(NS), one(NS), pl.BlockSpec((1, 1, 8, NS), lambda c: (slot, c, 0, 0)), one(EC),
                pl.BlockSpec((nz, 1, NS // nz, EC), lambda c: (0, slot, 0, 0)),
                pl.BlockSpec((1, 1, NS, EC), lambda c: (slot, c, 0, 0)),
            ]
            + anywhere,
            [one(EC), one(2 * NS), one(NS), one(NS)],
            [shape(2, rows, EC), shape(2, rows, 2 * NS), shape(2, rows, NS), shape(2, rows, NS)],
            [
                pltpu.VMEM((SPAN, SPAN), F32), pltpu.VMEM((SPAN, SPAN), F32), pltpu.VMEM((NS, SPAN), F32),
                pltpu.VMEM((NS, SPAN), F32),
            ],
            input_output_aliases={8 + i: i for i in range(len(kept))},
        )(live.x, live.bc, live.step, live.cum, live.before, live.d_ssm, live.state_in, live.local, *kept)

    live.first_slot = back_call(0, ())
    del live.backs
    settle(live)

    live.gate_sums = move_first(live.gate_sums)
    live.mixer_part = swapped(live.mixer_part, "core")
    live.dxs, live.d_bc, live.d_cum, live.d_step = back_call(1, live.first_slot)
    del live.first_slot, live.before
    settle(live)

    live.out_sums = cut_second(live.out_sums)
    live.gate_sums = cut_second(live.gate_sums)
    settle(live)
    live.out_sums = move_second(live.out_sums)
    live.gate_sums = move_second(live.gate_sums)
    slot_state = pl.BlockSpec((nz, 1, NS // nz, EC), lambda s: (0, s, 0, 0))
    d_proj, mine, theirs, g_taps, g_heads = call(
        functools.partial(close_kernel, rows, nz),
        (2,),
        [
            whole_row(rows, EC), whole_row(rows, 2 * NS), whole_row(rows, NS), whole_row(rows, NS), whole_row(rows, EC),
            whole_row(tall, WIDE), fixed(8, WIDE), fixed(8, NS), whole_row(rows, EC), whole_row(rows, 2 * NS),
            whole_row(rows, NS), whole_row(rows, NS), slot_state, whole_row(spans, NS, EC), slot_state,
            whole_row(spans, NS, EC),
        ],
        [whole_row(tall, BACK), whole_row(rows, NS), whole_row(rows, NS), whole_row(8, EC), whole_row(8, NS)],
        [shape(2, tall, BACK, dtype=BF16), shape(2, rows, NS), shape(2, rows, NS), shape(2, 8, EC), shape(2, 8, NS)],
        [pltpu.VMEM((HALO + rows + HALO, EC), F32)],
    )(live.x, live.bc, live.step, live.cum, live.d_ssm, live.proj, live.taps, live.heads_par, live.dxs, live.d_bc, live.d_cum, live.d_step, live.state_in, live.local, live.back_in, live.back_local)

    live.d_proj, live.bc_mine, live.bc_theirs, live.g_taps, live.g_heads = d_proj, mine, theirs, g_taps, g_heads
    del live.x, live.bc, live.step, live.cum, live.d_ssm, live.taps, live.heads_par, live.dxs, live.d_bc, live.d_cum
    live.block_out, live.stats = block_rows(bounds, live.own_in, live.mixer_own, live.mixer_part)
    del live.d_step, live.state_in, live.local, live.back_in, live.back_local, live.mixer_own, live.mixer_part
    settle(live)

    live.out_sums = cut_line(live.out_sums)
    live.block_keep, live.block_send = by_slots(live.block_out)
    del live.block_out
    settle(live)
    live.out_sums = move(live.out_sums, "z")
    live.block_send = swapped(live.block_send, "y")
    mine, theirs, d_proj, proj, own_taps = (
        live.bc_mine, swapped(live.bc_theirs, "core"), live.d_proj, live.proj, live.own_taps
    )
    column = pl.BlockSpec((1, tall, NS), lambda s: (s, 0, OWN // NS))
    d_proj, g_own = call(
        functools.partial(own_kernel, rows),
        (2,),
        [pl.BlockSpec(memory_space=pl.ANY), whole_row(rows, NS), whole_row(rows, NS), column, fixed(8, NS)],
        [column, whole_row(8, NS)],
        [shape(2, tall, BACK, dtype=BF16), shape(2, 8, NS)],
        [pltpu.VMEM((HALO + rows + HALO, NS), F32)],
        input_output_aliases={0: 0},
    )(d_proj, mine, theirs, proj, own_taps)

    live.d_proj, live.g_own = d_proj, g_own
    live.scan_sums = outer(live.normed, d_proj)
    del live.bc_mine, live.bc_theirs, live.proj, live.own_taps, live.normed
    settle(live)

    live.scan_sums = cut_first(live.scan_sums.reshape(nx, 2, nz, ny, deep, BACK), False)
    live.gate_sums = cut_line(live.gate_sums)
    settle(live)
    live.scan_sums = move_first(live.scan_sums)
    live.gate_sums = move(live.gate_sums, "z")
    live.d_own, live.d_came = to_normed(core, live.d_proj, live.d_gate, live.scan_weight, live.gate_weight)
    del live.d_proj, live.d_gate, live.scan_weight, live.gate_weight
    settle(live)

    live.scan_sums = cut_second(live.scan_sums)
    halo_own, halo_came = live.d_own[:HALO], live.d_came[:HALO]
    settle(live)
    live.scan_sums = move_second(live.scan_sums)
    live.back_own = lax.ppermute(halo_own, "z", [(i + 1, i) for i in range(nz - 1)])
    across = [(c * nz + i + 1, (1 - c) * nz + i) for c in range(2) for i in range(nz - 1)]
    live.back_came = lax.ppermute(halo_came, ("core", "z"), across)
    live.d_came = swapped(live.d_came, "core")
    live.out_sums = add_up(live.out_sums)
    live.gate_sums = add_up(live.gate_sums)
    settle(live)

    live.scan_sums = cut_line(live.scan_sums)
    settle(live)
    live.scan_sums = move(live.scan_sums, "z")
    live.grad_in, g_gain_in = input_rows(
        bounds, live.own_in, live.own_grad, live.d_own, live.d_came, live.back_own, live.back_came, live.gain_in
    )

    def spread_half(value, width):
        parts = value.reshape(value.shape[:-1] + (nx, 1, width // (2 * nx)))
        zero = jnp.zeros_like(parts)
        first = core == 0
        both = jnp.concatenate([jnp.where(first, parts, zero), jnp.where(first, zero, parts)], axis=-2)
        return both.reshape(value.shape[:-1] + (width,))

    taps_sum = jnp.sum(live.g_taps, axis=0)
    own_sum = jnp.sum(live.g_own, axis=0)
    nothing = jnp.zeros_like(own_sum)
    taps_sum = jnp.concatenate(
        [
            spread_half(taps_sum, E),
            jnp.where(core == 0, own_sum, nothing),
            jnp.where(core == 0, nothing, own_sum),
        ],
        axis=1,
    )
    head_sum = spread_half(jnp.sum(live.g_heads, axis=0)[:3, :HC], H)
    packed = jnp.concatenate(
        [
            taps_sum[: CONV + 1].reshape(-1),
            spread_half(live.g_gain_out[0], E),
            g_gain_in[0],
            head_sum.reshape(-1),
            live.stats[0, :3],
        ]
    )
    live.packed = jnp.pad(packed, (0, -packed.shape[0] % 1024)).reshape(-1, NS)
    live.grad_keep, live.grad_send = by_slots(live.grad_in)
    del live.own_in, live.own_grad, live.d_own, live.d_came, live.g_taps, live.g_own, live.g_heads, live.grad_in
    del live.g_gain_out, live.gain_in, live.back_own, live.back_came, live.stats
    settle(live)

    packed = sum_everywhere(live.packed).reshape(-1)
    grad_in = by_index("y", live.grad_keep, swapped(live.grad_send, "y"))
    block_out = by_index("y", live.block_keep, live.block_send)
    g_out = live.out_sums.reshape(thin, features)

    def row_share(value):
        return take(value, core, 0), swapped(take(value, 1 - core, 0), "core")

    gate_mine, gate_came = row_share(live.gate_sums)
    scan_mine, scan_came = row_share(add_up(live.scan_sums))
    place_at = [0]
    for size in ((CONV + 1) * CH, E, features, 3 * H, 3):
        place_at.append(place_at[-1] + size)
    device = ((ix * 2 + core) * nz + iz) * ny + iy
    taps_total = packed[: place_at[1]].reshape(CONV + 1, CH)
    taps_mine = lax.dynamic_slice_in_dim(taps_total, device * chan, chan, 1)
    gain_out_mine = lax.dynamic_slice_in_dim(packed[place_at[1] : place_at[2]], device * thin, thin)
    gain_in_mine = lax.dynamic_slice_in_dim(packed[place_at[2] : place_at[3]], device * deep, deep)
    head_total = packed[place_at[3] : place_at[4]].reshape(3, H)
    valid_sums = packed[place_at[4] : place_at[5]]

    def both_halves(mine_part, came_part):
        pair = by_index("core", mine_part, came_part)
        width = mine_part.shape[-1]
        return pair.reshape(2, deep, nx, width // nx).transpose(1, 2, 0, 3).reshape(deep, 2 * width)

    own_pair = by_index("core", scan_mine[:, OWN:STEP], scan_came[:, OWN:STEP])
    g_in_weight = jnp.concatenate(
        [
            both_halves(gate_mine, gate_came),
            both_halves(scan_mine[:, :EC], scan_came[:, :EC]),
            own_pair[0],
            own_pair[1],
            both_halves(scan_mine[:, STEP : STEP + HC], scan_came[:, STEP : STEP + HC]),
        ],
        axis=1,
    )
    token_total = jnp.sum(lengths).astype(F32) * features
    rms_stats = jnp.sqrt(valid_sums / token_total)
    return (
        block_out,
        grad_in,
        gain_in_mine,
        g_in_weight,
        taps_mine[:CONV],
        taps_mine[CONV],
        head_total[0],
        head_total[1],
        head_total[2],
        gain_out_mine,
        g_out,
        rms_stats,
    )


def solution(mesh):
    nb, ns = mesh.shape["batch"], mesh.shape["seq"]
    fine = Mesh(mesh.devices.reshape(nb // 2, 2, ns // 2, 2), ("x", "core", "z", "y"))
    batch, seq = ("x", "core"), ("z", "y")
    every = batch + seq
    act = P(batch, seq, None)
    return jax.shard_map(
        shards,
        mesh=fine,
        in_specs=(
            act, P(), P(every), P(every, None), P(None, every), P(every), P(), P(), P(), P(every), P(every, None), act,
        ),
        out_specs=(
            act, act, P(every), P(every, None), P(None, every), P(every), P(), P(), P(), P(every), P(every, None), P(),
        ),
        check_vma=False,
    )
```

time: 836 us -> 655 us (0.78)
  waiting for transfers between devices: 275 us -> 112 us
  Pallas kernels: 148 us -> 276 us
  matrix products: 71.3 us -> 0 us
  starting transfers between devices: 146 us -> 115 us
  other arithmetic: 80.6 us -> 58 us
  local copies, waits for them, and re-layouts: 102 us -> 82.4 us
    pallas_call x1 -> x18, Pallas kernels: 38.7 us -> 170 us  [the longest x2 51.4 us: back_call(): call(functools.partial(back_kernel, len(kept)), (spans,), [one(EC), one(2...]
    ppermute x36 -> x21, waiting for transfers between devices: 172 us -> 43 us  [others(): lax.ppermute(piece, axis, route)]
    dot_general x9 -> x0, matrix products: 71.3 us -> none  [the longest x3 27 us: dot(): return jnp.dot(a, b, preferred_element_type=F32)]
    ppermute x32 -> x25, waiting for transfers between devices: 72 us -> 37.5 us  [the longest x21 30.6 us: move(): lax.ppermute(piece, axis, [(i, (i + step) % size) for i in range(size)])]
    ppermute x36 -> x21, starting transfers between devices: 51 us -> 28.4 us  [others(): lax.ppermute(piece, axis, route)]
    ppermute x32 -> x25, starting transfers between devices: 64.7 us -> 45.1 us  [the longest x21 37.6 us: move(): lax.ppermute(piece, axis, [(i, (i + step) % size) for i in range(size)])]
    convert_element_type x21 -> x9, other arithmetic: 27.8 us -> 12.4 us  [the longest x6 8.57 us: cut_second(): add_up(one).astype(BF16)]
    dot_general x3 -> x0, local copies, waits for them, and re-layouts: 13.4 us -> none  [the longest x1 4.82 us: shards(): lax.dot_general(flat_mix, flat_dmix, (((0,), (0,)), ((), ())), preferred_...]
  transfers between devices with their start and end apart: 91 -> 69, of which waited for: 41 -> 26; matrix products, arithmetic and copies ran while one was open for 24% -> 8% of each run, Pallas kernels for 12% -> 34%
where the time goes in v2:
time: 655 us; the launch traced here: 646 us
  Pallas kernels  276 us (42%)
  starting transfers between devices  115 us (18%)
  waiting for transfers between devices  112 us (17%)
  local copies, waits for them, and re-layouts  82.4 us (13%)
  other arithmetic  58 us (9%)
    pallas_call x2, Pallas kernels, back_call(): call(functools.partial(back_kernel, len(kept)), (spans,), [one(EC), one(2...  51.4 us
    ppermute x21, waiting for transfers between devices, others(): lax.ppermute(piece, axis, route)  43 us
    ppermute x21, starting transfers between devices, move(): lax.ppermute(piece, axis, [(i, (i + step) % size) for i in range(size)])  37.6 us
    pallas_call x3, Pallas kernels, by_rows_of(): call(kernel, (slots,), [pl.BlockSpec(memory_space=pltpu.SMEM), pl.BlockSp...  35.1 us
    pallas_call x1, Pallas kernels, shards(): call(functools.partial(close_kernel, rows, nz), (2,), [whole_row(rows, EC...  33.9 us
    pallas_call x3, Pallas kernels, outer(): call(functools.partial(outer_kernel, halo), (left // tile,), [pl.BlockSpe...  31.2 us
    ppermute x21, waiting for transfers between devices, move(): lax.ppermute(piece, axis, [(i, (i + step) % size) for i in range(size)])  30.6 us
    ppermute x21, starting transfers between devices, others(): lax.ppermute(piece, axis, route)  28.4 us
  transfers between devices with their start and end apart: 69, of which 26 were waited for; matrix products, arithmetic and copies ran while one was open for 8% of the time, Pallas kernels for 34%

profile of v2, /device:TPU:0, one launch (start us, length us, event | category | flops | bytes accessed | tf_op | source)
XLA Modules:
  0.0 646.4 jit_solution(16975589672373039188)
XLA Ops:
  2.2 4.0 dynamic-slice_reduce_fusion
  10.2 2.6 collective-permute-start.2
  16.3 2.6 collective-permute-start.4
  20.9 2.8 all-to-all-start
  23.7 8.0 %collective-permute-done.2 = bf16[256,1536]{1,0:T(8,128)(2,1)} collective-permute-done((bf16[256,1536]{1,0:T(8,128)(2,1)}, bf16[256,1536]{1,0:T(8,128)(2,1)}, u32[]{:S(2)}, u32[]{:S(2)}) %collective-permute-start.2) | collective-permute-done | bytes 786464 | tf_op jit(solution)/shard_map/ppermute | solution.py:66
  31.6 3.4 maximum_select_fusion.3
  35.0 13.6 %collective-permute-done.1 = bf16[256,1536]{1,0:T(8,128)(2,1)} collective-permute-done((bf16[256,1536]{1,0:T(8,128)(2,1)}, bf16[256,1536]{1,0:T(8,128)(2,1)}, u32[]{:S(2)}, u32[]{:S(2)}) %collective-permute-start.1) | collective-permute-done | bytes 786464 | tf_op jit(solution)/shard_map/ppermute | solution.py:66
  48.6 2.8 maximum_select_fusion.2
  57.5 2.6 collective-permute-start.6
  67.8 13.4 %collective-permute-done.10.refs_3_ = bf16[4,48,1920]{2,1,0:T(8,128)(2,1)S(1)} collective-permute-done((bf16[4,48,1920]{2,1,0:T(8,128)(2,1)S(1)}, bf16[4,48,1920]{2,1,0:T(8,128)(2,1)S(1)}, u32[]{:S(2)}, u32[]{:S(2)}) %collective-permute-start.10) | collective-permute-done | bytes 737312 | tf_op jit(solution)/shard_map/ppermute | solution.py:45
  91.0 2.9 collective-permute-start.13
  96.7 3.4 maximum_select_fusion
  103.0 8.6 %collective-permute-done.12.refs_2_ = bf16[2,48,1536]{2,1,0:T(8,128)(2,1)} collective-permute-done((bf16[2,48,1536]{2,1,0:T(8,128)(2,1)S(1)}, bf16[2,48,1536]{2,1,0:T(8,128)(2,1)}, u32[]{:S(2)}, u32[]{:S(2)}) %collective-permute-start.12) | collective-permute-done | bytes 294944 | tf_op jit(solution)/shard_map/ppermute | solution.py:45
  111.6 14.7 %collective-permute-done.14.refs_1_ = bf16[2,4,48,1920]{3,2,1,0:T(8,128)(2,1)} collective-permute-done((bf16[2,4,48,1920]{3,2,1,0:T(8,128)(2,1)S(1)}, bf16[2,4,48,1920]{3,2,1,0:T(8,128)(2,1)}, u32[]{:S(2)}, u32[]{:S(2)}) %collective-permute-start.14) | collective-permute-done | bytes 1474592 | tf_op jit(solution)/shard_map/ppermute | solution.py:45
  132.9 13.4 %shard_map.214 = (f32[2,528,1920]{2,1,0:T(8,128)}, bf16[2,2,4,2,48,1920]{5,4,3,2,1,0:T(8,128)(2,1)}) custom-call(s32[8]{0:T(128)} %stack.435.table_ref, bf16[2,528,1536]{2,1,0:T(8,128)(2,1)} %fusion.2.a_ref, bf16[2,4,48,1920]{3,2,1,0:T(8,128)(2,1)} %copy-done, bf16[2,4,48,1920]{3,2,1,0:T(8,128)(2,1)} %collective-permute-done.14.refs_1_, ...), custom_call_target="tpu_custom_call" | custom-call | bytes 1024 | tf_op jit(solution)/shard_map/pallas_call | solution.py:685
  156.6 15.3 %shard_map.216 = (f32[2,512,1536]{2,1,0:T(8,128)}, f32[2,512,256]{2,1,0:T(8,128)}, f32[2,512,128]{2,1,0:T(8,128)}, f32[2,512,128]{2,1,0:T(8,128)}, bf16[4,2,32,1...) custom-call(f32[2,528,1920]{2,1,0:T(8,128)} %get-tuple-element.1292.proj.proj_ref, ...), custom_call_target="tpu_custom_call" | custom-call | bytes 1024 | tf_op jit(solution)/shard_map/pallas_call | solution.py:955
  185.0 5.7 all-to-all-start.1
  193.4 24.9 %shard_map.218.part_ref = f32[2,512,1536]{2,1,0:T(8,128)} custom-call(f32[2,512,1536]{2,1,0:T(8,128)} %get-tuple-element.1219.x_ref, f32[2,512,256]{2,1,0:T(8,128)} %get-tuple-element.1220.bc_ref, f32[2,512,128]{2,1,0:T(8,128)} %get-tuple-element.1221.step_ref, f32[2,512,128]{2,1,0:T(8,128)} %get-tuple-element.1222.cum_ref, f32[8,128]{1,0:T(8,128)} %stack.412.heads_par), custom_call_target="tpu_custom_call" | custom-call | bytes 1024 | tf_op jit(solution)/shard_map/pallas_call | solution.py:981
  228.8 5.1 all-to-all-start.2
  237.7 10.9 %shard_map.220 = (f32[2,512,1536]{2,1,0:T(8,128)}, bf16[2,2,4,2,48,1536]{5,4,3,2,1,0:T(8,128)(2,1)}) custom-call(s32[8]{0:T(128)} %stack.462.table_ref, bf16[2,528,1536]{2,1,0:T(8,128)(2,1)} %fusion.2.a_ref, bf16[2,4,48,1536]{3,2,1,0:T(8,128)(2,1)} %copy-done.2, bf16[2,4,48,1536]{3,2,1,0:T(8,128)(2,1)} %collective-permute-done.19.refs_1_, ...), custom_call_target="tpu_custom_call" | custom-call | bytes 1024 | tf_op jit(solution)/shard_map/pallas_call | solution.py:685
  248.6 4.6 fusion.3.a_ref.b_ref
  254.6 10.8 %shard_map.221 = (f32[2,512,1536]{2,1,0:T(8,128)}, bf16[2,4,2,2,48,1536]{5,4,3,2,1,0:T(8,128)(2,1)}) custom-call(s32[8]{0:T(128)} %stack.467.table_ref, bf16[2,512,1536]{2,1,0:T(8,128)(2,1)} %fusion.3.a_ref.b_ref, bf16[2,4,48,1536]{3,2,1,0:T(8,128)(2,1)} %copy-done.4, bf16[2,4,48,1536]{3,2,1,0:T(8,128)(2,1)} %collective-permute-done.26.refs_1_, ...), custom_call_target="tpu_custom_call" | custom-call | bytes 1024 | tf_op jit(solution)/shard_map/pallas_call | solution.py:685
  266.1 12.2 %shard_map.222 = (f32[2,512,1536]{2,1,0:T(8,128)}, f32[2,512,128]{2,1,0:T(8,128)}) custom-call(f32[2,512,1536]{2,1,0:T(8,128)} %shard_map.218.part_ref, f32[2,512,256]{2,1,0:T(8,128)} %get-tuple-element.1220.bc_ref, f32[2,512,128]{2,1,0:T(8,128)} %get-tuple-element.1222.cum_ref, f32[2,2,8,128]{3,2,1,0:T(8,128)} %broadcast_in_dim.70.before_ref, ...), custom_call_target="tpu_custom_call" | custom-call | bytes 1024 | tf_op jit(solution)/shard_map/pallas_call | solution.py:1030
  282.4 17.2 %shard_map.223 = (bf16[2,512,1536]{2,1,0:T(8,128)(2,1)}, f32[2,512,1536]{2,1,0:T(8,128)}, bf16[2,512,1536]{2,1,0:T(8,128)(2,1)}, f32[8,1536]{1,0:T(8,128)}, bf16...) custom-call(f32[2,512,1536]{2,1,0:T(8,128)} %get-tuple-element.1031.y_ref, ...), custom_call_target="tpu_custom_call" | custom-call | bytes 1024 | tf_op jit(solution)/shard_map/pallas_call | solution.py:1043
  299.6 5.3 all-to-all-start.3
  304.9 9.8 %shard_map.226 = bf16[1536,1536]{1,0:T(8,128)(2,1)} custom-call(bf16[2,512,1536]{2,1,0:T(8,128)(2,1)} %get-tuple-element.1066.a_ref, bf16[2,512,1536]{2,1,0:T(8,128)(2,1)} %fusion.3.a_ref.b_ref), custom_call_target="tpu_custom_call" | custom-call | bytes 1024 | tf_op jit(solution)/shard_map/pallas_call | solution.py:631
  314.7 10.2 %shard_map.225 = (f32[512,1536]{1,0:T(8,128)}, f32[512,1536]{1,0:T(8,128)}) custom-call(s32[1]{0:T(128)} %bitcast.66.core_ref, bf16[2,512,1536]{2,1,0:T(8,128)(2,1)} %get-tuple-element.1066.a_ref, bf16[1536,1536]{1,0:T(8,128)(2,1)} %bitcast.271), custom_call_target="tpu_custom_call" | custom-call | bytes 1024 | tf_op jit(solution)/shard_map/pallas_call | solution.py:734
  324.9 9.8 %shard_map.224 = bf16[1536,1536]{1,0:T(8,128)(2,1)} custom-call(bf16[2,528,1536]{2,1,0:T(8,128)(2,1)} %fusion.2.a_ref, bf16[2,512,1536]{2,1,0:T(8,128)(2,1)} %get-tuple-element.1340.b_ref.dgate_ref), custom_call_target="tpu_custom_call" | custom-call | bytes 1024 | tf_op jit(solution)/shard_map/pallas_call | solution.py:631
  334.7 3.2 fusion.51
  349.2 5.1 all-to-all-start.4
  354.3 25.8 %shard_map.227 = (f32[2,512,1536]{2,1,0:T(8,128)}, f32[2,512,256]{2,1,0:T(8,128)}, f32[2,512,128]{2,1,0:T(8,128)}, f32[2,512,128]{2,1,0:T(8,128)}) custom-call(f32[2,512,1536]{2,1,0:T(8,128)} %get-tuple-element.1219.x_ref, f32[2,512,256]{2,1,0:T(8,128)} %get-tuple-element.1220.bc_ref, f32[2,512,128]{2,1,0:T(8,128)} %get-tuple-element.1221.step_ref, ...), custom_call_target="tpu_custom_call" | custom-call | bytes 1024 | tf_op jit(solution)/shard_map/pallas_call | solution.py:1083
  381.7 25.6 %shard_map.228 = (f32[2,512,1536]{2,1,0:T(8,128)}, f32[2,512,256]{2,1,0:T(8,128)}, f32[2,512,128]{2,1,0:T(8,128)}, f32[2,512,128]{2,1,0:T(8,128)}) custom-call(f32[2,512,1536]{2,1,0:T(8,128)} %get-tuple-element.1219.x_ref, f32[2,512,256]{2,1,0:T(8,128)} %get-tuple-element.1220.bc_ref, ...), custom_call_target="tpu_custom_call", output_to_operand_aliasing={{0}: (8, {}), {1}: (9, {}), {2}: (10, {}), {3}: (11, {})} | custom-call | bytes 1024 | tf_op jit(solution)/shard_map/pallas_call | solution.py:1083
  424.2 5.0 shard_map.230
  429.2 33.9 %shard_map.229 = (bf16[2,528,1792]{2,1,0:T(8,128)(2,1)}, f32[2,512,128]{2,1,0:T(8,128)}, f32[2,512,128]{2,1,0:T(8,128)}, f32[2,8,1536]{2,1,0:T(8,128)}, f32[2,8,128]{2,1,0:T(8,128)}) custom-call(f32[2,512,1536]{2,1,0:T(8,128)} %get-tuple-element.1219.x_ref, f32[2,512,256]{2,1,0:T(8,128)} %get-tuple-element.1220.bc_ref, ...), custom_call_target="tpu_custom_call" | custom-call | bytes 1024 | tf_op jit(solution)/shard_map/pallas_call | solution.py:1117
  478.7 11.7 %shard_map.232 = bf16[1536,1792]{1,0:T(8,128)(2,1)} custom-call(bf16[2,528,1536]{2,1,0:T(8,128)(2,1)} %fusion.2.a_ref, bf16[2,528,1792]{2,1,0:T(8,128)(2,1)} %get-tuple-element.1339.b_ref.dproj_ref), custom_call_target="tpu_custom_call" | custom-call | bytes 1024 | tf_op jit(solution)/shard_map/pallas_call | solution.py:631
  490.3 3.6 collective-permute-done.41
  494.0 3.4 fusion.50
  504.8 6.8 %collective-permute-start.43 = (bf16[2,48,1536]{2,1,0:T(8,128)(2,1)}, bf16[2,48,1536]{2,1,0:T(8,128)(2,1)}, u32[]{:S(2)}, u32[]{:S(2)}) collective-permute-start(bf16[2,48,1536]{2,1,0:T(8,128)(2,1)} %get-tuple-element.1351), channel_id=1, source_target_pairs={{0,2},{2,4},{4,6},{6,0},{1,3},{3,5},{5,7},{7,1},{8,10},{10,12},{12... | collective-permute-start | bytes 884744 | tf_op jit(solution)/shard_map/ppermute | solution.py:175
  514.0 19.1 %shard_map.233 = (f32[528,1536]{1,0:T(8,128)}, f32[528,1536]{1,0:T(8,128)}) custom-call(s32[1]{0:T(128)} %bitcast.66.core_ref, bf16[2,528,1792]{2,1,0:T(8,128)(2,1)} %get-tuple-element.1339.b_ref.dproj_ref, bf16[2,512,1536]{2,1,0:T(8,128)(2,1)} %get-tuple-element.1340.b_ref.dgate_ref, bf16[1536,1920]{1,0:T(8,128)(2,1)} %bitcast.270, bf16[1536,1536]{1,0:T(8,128)(2,1)} %bitcast.272), custom_call_target="tpu_custom_call" | custom-call | bytes 1024 | tf_op jit(solution)/shard_map/pallas_call | solution.py:712
  552.2 4.1 collective-permute-done.48.across_ref
  556.2 2.8 collective-permute-done.49.later_ref
  566.8 6.3 shard_map.234
  574.7 6.9 %collective-permute-start.53 = (bf16[2,48,1792]{2,1,0:T(8,128)(2,1)S(1)}, bf16[2,48,1792]{2,1,0:T(8,128)(2,1)}, u32[]{:S(2)}, u32[]{:S(2)}) collective-permute-start(bf16[2,48,1792]{2,1,0:T(8,128)(2,1)S(1)} %copy-done.57), channel_id=1, source_target_pairs={{0,2},{2,4},{4,6},{6,0},{1,3},{3,5},{5,7},{7,1},{8,10},{10,12},{12... | collective-permute-start | bytes 1032200 | tf_op jit(solution)/shard_map/ppermute | solution.py:175
  585.7 5.8 collective-permute-done.53
  591.6 13.4 %collective-permute-done.54 = bf16[2,48,1792]{2,1,0:T(8,128)(2,1)} collective-permute-done((bf16[2,48,1792]{2,1,0:T(8,128)(2,1)S(1)}, bf16[2,48,1792]{2,1,0:T(8,128)(2,1)}, u32[]{:S(2)}, u32[]{:S(2)}) %collective-permute-start.54) | collective-permute-done | bytes 344096 | tf_op jit(solution)/shard_map/ppermute | solution.py:175
  610.1 2.8 maximum_select_fusion.4
  614.0 7.9 %collective-permute-start.59 = (f32[168,128]{1,0:T(8,128)S(1)}, f32[168,128]{1,0:T(8,128)S(1)}, u32[]{:S(2)}, u32[]{:S(2)}) collective-permute-start(f32[168,128]{1,0:T(8,128)S(1)} %add.409), channel_id=1, source_target_pairs={{0,2},{2,0},{4,6},{6,4},{1,3},{3,1},{5,7},{7,5},{8,10},{10,8},{12,... | collective-permute-start | bytes 258056 | tf_op jit(solution)/shard_map/ppermute | solution.py:216
  643.5 2.8 maximum_select_fusion.5
  (509 shorter events, 207.0 us)
Async XLA Ops:
  10.2 21.4 %collective-permute-start.2 = (bf16[256,1536]{1,0:T(8,128)(2,1)}, bf16[256,1536]{1,0:T(8,128)(2,1)}, u32[]{:S(2)}, u32[]{:S(2)}) collective-permute-start(bf16[256,1536]{1,0:T(8,128)(2,1)} %get-tuple-element.1499), channel_id=1, source_target_pairs={{0,1},{1,0},{2,3},{3,2},{4,5},{5,4},{6,7},{7,6},{8,9},{9,8},{10,11... | collective-permute-start | bytes 2359304 | tf_op jit(solution)/shard_map/ppermute | solution.py:66
  13.8 34.8 %collective-permute-start.1 = (bf16[256,1536]{1,0:T(8,128)(2,1)}, bf16[256,1536]{1,0:T(8,128)(2,1)}, u32[]{:S(2)}, u32[]{:S(2)}) collective-permute-start(bf16[256,1536]{1,0:T(8,128)(2,1)} %get-tuple-element.1501), channel_id=1, source_target_pairs={{0,1},{1,0},{2,3},{3,2},{4,5},{5,4},{6,7},{7,6},{8,9},{9,8},{10,11... | collective-permute-start | bytes 2359304 | tf_op jit(solution)/shard_map/ppermute | solution.py:66
  14.6 39.1 %collective-permute-start.3 = (bf16[2,48,1920]{2,1,0:T(8,128)(2,1)S(1)}, bf16[2,48,1920]{2,1,0:T(8,128)(2,1)S(1)}, u32[]{:S(2)}, u32[]{:S(2)}) collective-permute-start(bf16[2,48,1920]{2,1,0:T(8,128)(2,1)S(1)} %slice.282.refs_0_), channel_id=1, source_target_pairs={{0,2},{2,4},{4,6},{6,0},{1,3},{3,5},{5,7},{7,1},{8,10},{10,12},{12... | collective-permute-start | bytes 1105928 | tf_op jit(solution)/shard_map/ppermute | solution.py:45
  16.3 37.5 %collective-permute-start.4 = (bf16[2,48,1920]{2,1,0:T(8,128)(2,1)S(1)}, bf16[2,48,1920]{2,1,0:T(8,128)(2,1)S(1)}, u32[]{:S(2)}, u32[]{:S(2)}) collective-permute-start(bf16[2,48,1920]{2,1,0:T(8,128)(2,1)S(1)} %slice.282.refs_0_), channel_id=1, source_target_pairs={{0,4},{2,6},{4,0},{6,2},{1,5},{3,7},{5,1},{7,3},{8,12},{10,14},{12... | collective-permute-start | bytes 1105928 | tf_op jit(solution)/shard_map/ppermute | solution.py:45
  18.9 34.9 %collective-permute-start.5 = (bf16[2,48,1920]{2,1,0:T(8,128)(2,1)S(1)}, bf16[2,48,1920]{2,1,0:T(8,128)(2,1)S(1)}, u32[]{:S(2)}, u32[]{:S(2)}) collective-permute-start(bf16[2,48,1920]{2,1,0:T(8,128)(2,1)S(1)} %slice.282.refs_0_), channel_id=1, source_target_pairs={{0,6},{2,0},{4,2},{6,4},{1,7},{3,1},{5,3},{7,5},{8,14},{10,8},{12,... | collective-permute-start | bytes 1105928 | tf_op jit(solution)/shard_map/ppermute | solution.py:45
  20.9 32.9 %all-to-all-start = ((bf16[32,8,128]{2,1,0:T(8,128)(2,1)}), bf16[32,8,128]{2,1,0:T(8,128)(2,1)S(1)}, u32[]{:S(2)}, u32[]{:S(2)}) async-start(bf16[32,8,128]{2,1,0:T(8,128)(2,1)} %broadcast_in_dim.58), calls=%async_computation | async-start | bytes 131072 | tf_op jit(solution)/shard_map/all_to_all | solution.py:57
  56.6 26.6 %collective-permute-start.8 = (bf16[512,1536]{1,0:T(8,128)(2,1)}, bf16[512,1536]{1,0:T(8,128)(2,1)}, u32[]{:S(2)}, u32[]{:S(2)}) collective-permute-start(bf16[512,1536]{1,0:T(8,128)(2,1)} %bitcast.258), channel_id=1, source_target_pairs={{0,8},{8,0},{1,9},{9,1},{2,10},{10,2},{3,11},{11,3},{4,12},{12,4},... | collective-permute-start | bytes 4718600 | tf_op jit(solution)/shard_map/ppermute | solution.py:66
  62.9 18.3 %collective-permute-start.10 = (bf16[4,48,1920]{2,1,0:T(8,128)(2,1)S(1)}, bf16[4,48,1920]{2,1,0:T(8,128)(2,1)S(1)}, u32[]{:S(2)}, u32[]{:S(2)}) collective-permute-start(bf16[4,48,1920]{2,1,0:T(8,128)(2,1)S(1)} %get-tuple-element.780.refs_2_), channel_id=1, source_target_pairs={{0,16},{16,0},{1,17},{17,1},{2,18},{18,2},{3,19},{19,3},{4,20},{20... | collective-permute-start | bytes 2211848 | tf_op jit(solution)/shard_map/ppermute | solution.py:45
  91.0 20.6 %collective-permute-start.12 = (bf16[2,48,1536]{2,1,0:T(8,128)(2,1)S(1)}, bf16[2,48,1536]{2,1,0:T(8,128)(2,1)}, u32[]{:S(2)}, u32[]{:S(2)}) collective-permute-start(bf16[2,48,1536]{2,1,0:T(8,128)(2,1)S(1)} %slice.281.refs_0_), channel_id=1, source_target_pairs={{0,4},{2,6},{4,0},{6,2},{1,5},{3,7},{5,1},{7,3},{8,12},{10,14},{12... | collective-permute-start | bytes 884744 | tf_op jit(solution)/shard_map/ppermute | solution.py:45
  91.0 20.6 %collective-permute-start.13 = (bf16[2,48,1536]{2,1,0:T(8,128)(2,1)S(1)}, bf16[2,48,1536]{2,1,0:T(8,128)(2,1)}, u32[]{:S(2)}, u32[]{:S(2)}) collective-permute-start(bf16[2,48,1536]{2,1,0:T(8,128)(2,1)S(1)} %slice.281.refs_0_), channel_id=1, source_target_pairs={{0,6},{2,0},{4,2},{6,4},{1,7},{3,1},{5,3},{7,5},{8,14},{10,8},{12,... | collective-permute-start | bytes 884744 | tf_op jit(solution)/shard_map/ppermute | solution.py:45
  93.9 32.4 %collective-permute-start.14 = (bf16[2,4,48,1920]{3,2,1,0:T(8,128)(2,1)S(1)}, bf16[2,4,48,1920]{3,2,1,0:T(8,128)(2,1)}, u32[]{:S(2)}, u32[]{:S(2)}) collective-permute-start(bf16[2,4,48,1920]{3,2,1,0:T(8,128)(2,1)S(1)} %get-tuple-element.837.refs_0_), channel_id=1, source_target_pairs={{0,16},{16,0},{1,17},{17,1},{2,18},{18,2},{3,19},{19,3},{4,20},{20... | collective-permute-start | bytes 4423688 | tf_op jit(solution)/shard_map/ppermute | solution.py:45
  94.4 32.2 %collective-permute-start.15 = (bf16[2,4,48,1920]{3,2,1,0:T(8,128)(2,1)S(1)}, bf16[2,4,48,1920]{3,2,1,0:T(8,128)(2,1)}, u32[]{:S(2)}, u32[]{:S(2)}) collective-permute-start(bf16[2,4,48,1920]{3,2,1,0:T(8,128)(2,1)S(1)} %get-tuple-element.839.refs_2_), channel_id=1, source_target_pairs={{0,1},{1,0},{2,3},{3,2},{4,5},{5,4},{6,7},{7,6},{8,9},{9,8},{10,11... | collective-permute-start | bytes 4423688 | tf_op jit(solution)/shard_map/ppermute | solution.py:45
  150.5 27.9 %collective-permute-start.19 = (bf16[2,4,48,1536]{3,2,1,0:T(8,128)(2,1)S(1)}, bf16[2,4,48,1536]{3,2,1,0:T(8,128)(2,1)}, u32[]{:S(2)}, u32[]{:S(2)}) collective-permute-start(bf16[2,4,48,1536]{3,2,1,0:T(8,128)(2,1)S(1)} %get-tuple-element.995.refs_0_), channel_id=1, source_target_pairs={{0,16},{16,0},{1,17},{17,1},{2,18},{18,2},{3,19},{19,3},{4,20},{20... | collective-permute-start | bytes 3538952 | tf_op jit(solution)/shard_map/ppermute | solution.py:45
  151.9 27.0 %collective-permute-start.20 = (bf16[2,4,48,1536]{3,2,1,0:T(8,128)(2,1)S(1)}, bf16[2,4,48,1536]{3,2,1,0:T(8,128)(2,1)}, u32[]{:S(2)}, u32[]{:S(2)}) collective-permute-start(bf16[2,4,48,1536]{3,2,1,0:T(8,128)(2,1)S(1)} %get-tuple-element.997.refs_2_), channel_id=1, source_target_pairs={{0,1},{1,0},{2,3},{3,2},{4,5},{5,4},{6,7},{7,6},{8,9},{9,8},{10,11... | collective-permute-start | bytes 3538952 | tf_op jit(solution)/shard_map/ppermute | solution.py:45
  152.4 19.5 %collective-permute-start.21 = (bf16[2,48,1536]{2,1,0:T(8,128)(2,1)S(1)}, bf16[2,48,1536]{2,1,0:T(8,128)(2,1)S(1)}, u32[]{:S(2)}, u32[]{:S(2)}) collective-permute-start(bf16[2,48,1536]{2,1,0:T(8,128)(2,1)S(1)} %bitcast.254), channel_id=1, source_target_pairs={{0,2},{2,4},{4,6},{6,0},{1,3},{3,5},{5,7},{7,1},{8,10},{10,12},{12... | collective-permute-start | bytes 884744 | tf_op jit(solution)/shard_map/ppermute | solution.py:45
  152.6 22.2 %collective-permute-start.22 = (bf16[2,48,1536]{2,1,0:T(8,128)(2,1)S(1)}, bf16[2,48,1536]{2,1,0:T(8,128)(2,1)S(1)}, u32[]{:S(2)}, u32[]{:S(2)}) collective-permute-start(bf16[2,48,1536]{2,1,0:T(8,128)(2,1)S(1)} %bitcast.255), channel_id=1, source_target_pairs={{0,4},{2,6},{4,0},{6,2},{1,5},{3,7},{5,1},{7,3},{8,12},{10,14},{12... | collective-permute-start | bytes 884744 | tf_op jit(solution)/shard_map/ppermute | solution.py:45
  154.4 21.2 %collective-permute-start.23 = (bf16[2,48,1536]{2,1,0:T(8,128)(2,1)S(1)}, bf16[2,48,1536]{2,1,0:T(8,128)(2,1)S(1)}, u32[]{:S(2)}, u32[]{:S(2)}) collective-permute-start(bf16[2,48,1536]{2,1,0:T(8,128)(2,1)S(1)} %bitcast.256), channel_id=1, source_target_pairs={{0,6},{2,0},{4,2},{6,4},{1,7},{3,1},{5,3},{7,5},{8,14},{10,8},{12,... | collective-permute-start | bytes 884744 | tf_op jit(solution)/shard_map/ppermute | solution.py:45
  185.0 34.2 %all-to-all-start.1 = ((bf16[4,2,32,1664]{3,2,1,0:T(8,128)(2,1)}), bf16[4,2,32,1664]{3,2,1,0:T(8,128)(2,1)}, u32[]{:S(2)}, u32[]{:S(2)}) async-start(bf16[4,2,32,1664]{3,2,1,0:T(8,128)(2,1)} %get-tuple-element.922), calls=%async_computation.1 | async-start | bytes 1703936 | tf_op jit(solution)/shard_map/all_to_all | solution.py:852
  190.7 27.7 %collective-permute-start.24 = (bf16[4,48,1536]{2,1,0:T(8,128)(2,1)S(1)}, bf16[4,48,1536]{2,1,0:T(8,128)(2,1)S(1)}, u32[]{:S(2)}, u32[]{:S(2)}) collective-permute-start(bf16[4,48,1536]{2,1,0:T(8,128)(2,1)S(1)} %get-tuple-element.968.refs_0_), channel_id=1, source_target_pairs={{0,1},{1,0},{2,3},{3,2},{4,5},{5,4},{6,7},{7,6},{8,9},{9,8},{10,11... | collective-permute-start | bytes 1769480 | tf_op jit(solution)/shard_map/ppermute | solution.py:45
  192.2 27.0 %collective-permute-start.25 = (bf16[4,48,1536]{2,1,0:T(8,128)(2,1)S(1)}, bf16[4,48,1536]{2,1,0:T(8,128)(2,1)S(1)}, u32[]{:S(2)}, u32[]{:S(2)}) collective-permute-start(bf16[4,48,1536]{2,1,0:T(8,128)(2,1)S(1)} %get-tuple-element.970.refs_2_), channel_id=1, source_target_pairs={{0,16},{16,0},{1,17},{17,1},{2,18},{18,2},{3,19},{19,3},{4,20},{20... | collective-permute-start | bytes 1769480 | tf_op jit(solution)/shard_map/ppermute | solution.py:45
  227.3 25.8 %collective-permute-start.26 = (bf16[2,4,48,1536]{3,2,1,0:T(8,128)(2,1)S(1)}, bf16[2,4,48,1536]{3,2,1,0:T(8,128)(2,1)}, u32[]{:S(2)}, u32[]{:S(2)}) collective-permute-start(bf16[2,4,48,1536]{3,2,1,0:T(8,128)(2,1)S(1)} %get-tuple-element.1025.refs_0_), channel_id=1, source_target_pairs={{0,16},{16,0},{1,17},{17,1},{2,18},{18,2},{3,19},{19,3},{4,20},{20... | collective-permute-start | bytes 3538952 | tf_op jit(solution)/shard_map/ppermute | solution.py:45
  228.2 25.0 %collective-permute-start.27 = (bf16[2,4,48,1536]{3,2,1,0:T(8,128)(2,1)S(1)}, bf16[2,4,48,1536]{3,2,1,0:T(8,128)(2,1)}, u32[]{:S(2)}, u32[]{:S(2)}) collective-permute-start(bf16[2,4,48,1536]{3,2,1,0:T(8,128)(2,1)S(1)} %get-tuple-element.1027.refs_2_), channel_id=1, source_target_pairs={{0,1},{1,0},{2,3},{3,2},{4,5},{5,4},{6,7},{7,6},{8,9},{9,8},{10,11... | collective-permute-start | bytes 3538952 | tf_op jit(solution)/shard_map/ppermute | solution.py:45
  228.8 24.4 %all-to-all-start.2 = ((bf16[4,2,32,1536]{3,2,1,0:T(8,128)(2,1)}), bf16[4,2,32,1536]{3,2,1,0:T(8,128)(2,1)S(1)}, u32[]{:S(2)}, u32[]{:S(2)}) async-start(bf16[4,2,32,1536]{3,2,1,0:T(8,128)(2,1)} %pad_maximum_fusion.1), calls=%async_computation.2 | async-start | bytes 1572864 | tf_op jit(solution)/shard_map/all_to_all | solution.py:852
  299.6 35.1 %all-to-all-start.3 = ((bf16[4,2,32,1536]{3,2,1,0:T(8,128)(2,1)}), bf16[4,2,32,1536]{3,2,1,0:T(8,128)(2,1)S(1)}, u32[]{:S(2)}, u32[]{:S(2)}) async-start(bf16[4,2,32,1536]{3,2,1,0:T(8,128)(2,1)} %get-tuple-element.1078), calls=%async_computation.3 | async-start | bytes 1572864 | tf_op jit(solution)/shard_map/all_to_all | solution.py:852
  346.5 33.6 %collective-permute-start.29 = (bf16[4,2,48,1536]{3,2,1,0:T(8,128)(2,1)}, bf16[4,2,48,1536]{3,2,1,0:T(8,128)(2,1)}, u32[]{:S(2)}, u32[]{:S(2)}) collective-permute-start(bf16[4,2,48,1536]{3,2,1,0:T(8,128)(2,1)} %get-tuple-element.1135), channel_id=1, source_target_pairs={{0,16},{16,0},{1,17},{17,1},{2,18},{18,2},{3,19},{19,3},{4,20},{20... | collective-permute-start | bytes 3538952 | tf_op jit(solution)/shard_map/ppermute | solution.py:175
  347.7 32.4 %collective-permute-start.30 = (bf16[2,4,48,1536]{3,2,1,0:T(8,128)(2,1)}, bf16[2,4,48,1536]{3,2,1,0:T(8,128)(2,1)}, u32[]{:S(2)}, u32[]{:S(2)}) collective-permute-start(bf16[2,4,48,1536]{3,2,1,0:T(8,128)(2,1)} %get-tuple-element.1137), channel_id=1, source_target_pairs={{0,1},{1,0},{2,3},{3,2},{4,5},{5,4},{6,7},{7,6},{8,9},{9,8},{10,11... | collective-permute-start | bytes 3538952 | tf_op jit(solution)/shard_map/ppermute | solution.py:175
  349.2 30.9 %all-to-all-start.4 = ((bf16[4,2,32,1536]{3,2,1,0:T(8,128)(2,1)}), bf16[4,2,32,1536]{3,2,1,0:T(8,128)(2,1)}, u32[]{:S(2)}, u32[]{:S(2)}) async-start(bf16[4,2,32,1536]{3,2,1,0:T(8,128)(2,1)} %pad_maximum_fusion.2), calls=%async_computation.4 | async-start | bytes 1572864 | tf_op jit(solution)/shard_map/all_to_all | solution.py:852
  380.1 29.3 %collective-permute-start.33 = (f32[512,1536]{1,0:T(8,128)}, f32[512,1536]{1,0:T(8,128)}, u32[]{:S(2)}, u32[]{:S(2)}) collective-permute-start(f32[512,1536]{1,0:T(8,128)} %get-tuple-element.1172), channel_id=1, source_target_pairs={{0,8},{8,0},{1,9},{9,1},{2,10},{10,2},{3,11},{11,3},{4,12},{12,4},... | collective-permute-start | bytes 9437192 | tf_op jit(solution)/shard_map/ppermute | solution.py:66
  380.2 28.7 %collective-permute-start.31 = (bf16[4,2,48,1536]{3,2,1,0:T(8,128)(2,1)}, bf16[4,2,48,1536]{3,2,1,0:T(8,128)(2,1)}, u32[]{:S(2)}, u32[]{:S(2)}) collective-permute-start(bf16[4,2,48,1536]{3,2,1,0:T(8,128)(2,1)} %get-tuple-element.1166), channel_id=1, source_target_pairs={{0,16},{16,0},{1,17},{17,1},{2,18},{18,2},{3,19},{19,3},{4,20},{20... | collective-permute-start | bytes 3538952 | tf_op jit(solution)/shard_map/ppermute | solution.py:175
  381.0 28.4 %collective-permute-start.32 = (bf16[2,4,48,1536]{3,2,1,0:T(8,128)(2,1)}, bf16[2,4,48,1536]{3,2,1,0:T(8,128)(2,1)}, u32[]{:S(2)}, u32[]{:S(2)}) collective-permute-start(bf16[2,4,48,1536]{3,2,1,0:T(8,128)(2,1)} %get-tuple-element.1168), channel_id=1, source_target_pairs={{0,1},{1,0},{2,3},{3,2},{4,5},{5,4},{6,7},{7,6},{8,9},{9,8},{10,11... | collective-permute-start | bytes 3538952 | tf_op jit(solution)/shard_map/ppermute | solution.py:175
  420.1 42.9 %collective-permute-start.34 = (bf16[4,48,1536]{2,1,0:T(8,128)(2,1)}, bf16[4,48,1536]{2,1,0:T(8,128)(2,1)S(1)}, u32[]{:S(2)}, u32[]{:S(2)}) collective-permute-start(bf16[4,48,1536]{2,1,0:T(8,128)(2,1)} %get-tuple-element.1248), channel_id=1, source_target_pairs={{0,1},{1,0},{2,3},{3,2},{4,5},{5,4},{6,7},{7,6},{8,9},{9,8},{10,11... | collective-permute-start | bytes 1769480 | tf_op jit(solution)/shard_map/ppermute | solution.py:175
  420.7 42.3 %collective-permute-start.35 = (bf16[4,48,1536]{2,1,0:T(8,128)(2,1)}, bf16[4,48,1536]{2,1,0:T(8,128)(2,1)S(1)}, u32[]{:S(2)}, u32[]{:S(2)}) collective-permute-start(bf16[4,48,1536]{2,1,0:T(8,128)(2,1)} %get-tuple-element.1250), channel_id=1, source_target_pairs={{0,16},{16,0},{1,17},{17,1},{2,18},{18,2},{3,19},{19,3},{4,20},{20... | collective-permute-start | bytes 1769480 | tf_op jit(solution)/shard_map/ppermute | solution.py:175
  421.9 41.1 %collective-permute-start.36 = (bf16[4,48,1536]{2,1,0:T(8,128)(2,1)}, bf16[4,48,1536]{2,1,0:T(8,128)(2,1)}, u32[]{:S(2)}, u32[]{:S(2)}) collective-permute-start(bf16[4,48,1536]{2,1,0:T(8,128)(2,1)} %get-tuple-element.1254), channel_id=1, source_target_pairs={{0,1},{1,0},{2,3},{3,2},{4,5},{5,4},{6,7},{7,6},{8,9},{9,8},{10,11... | collective-permute-start | bytes 1769480 | tf_op jit(solution)/shard_map/ppermute | solution.py:175
  423.4 39.7 %collective-permute-start.37 = (bf16[4,48,1536]{2,1,0:T(8,128)(2,1)}, bf16[4,48,1536]{2,1,0:T(8,128)(2,1)}, u32[]{:S(2)}, u32[]{:S(2)}) collective-permute-start(bf16[4,48,1536]{2,1,0:T(8,128)(2,1)} %get-tuple-element.1256), channel_id=1, source_target_pairs={{0,16},{16,0},{1,17},{17,1},{2,18},{18,2},{3,19},{19,3},{4,20},{20... | collective-permute-start | bytes 1769480 | tf_op jit(solution)/shard_map/ppermute | solution.py:175
  468.9 25.1 %collective-permute-start.38 = (bf16[256,1536]{1,0:T(8,128)(2,1)S(1)}, bf16[256,1536]{1,0:T(8,128)(2,1)S(1)}, u32[]{:S(2)}, u32[]{:S(2)}) collective-permute-start(bf16[256,1536]{1,0:T(8,128)(2,1)S(1)} %get-tuple-element.1287), channel_id=1, source_target_pairs={{0,1},{1,0},{2,3},{3,2},{4,5},{5,4},{6,7},{7,6},{8,9},{9,8},{10,11... | collective-permute-start | bytes 2359304 | tf_op jit(solution)/shard_map/ppermute | solution.py:66
  469.5 20.9 %collective-permute-start.40 = (bf16[2,48,1536]{2,1,0:T(8,128)(2,1)}, bf16[2,48,1536]{2,1,0:T(8,128)(2,1)S(1)}, u32[]{:S(2)}, u32[]{:S(2)}) collective-permute-start(bf16[2,48,1536]{2,1,0:T(8,128)(2,1)} %get-tuple-element.1306), channel_id=1, source_target_pairs={{0,2},{2,4},{4,6},{6,0},{1,3},{3,5},{5,7},{7,1},{8,10},{10,12},{12... | collective-permute-start | bytes 884744 | tf_op jit(solution)/shard_map/ppermute | solution.py:175
  471.5 22.4 %collective-permute-start.41 = (bf16[2,48,1536]{2,1,0:T(8,128)(2,1)}, bf16[2,48,1536]{2,1,0:T(8,128)(2,1)S(1)}, u32[]{:S(2)}, u32[]{:S(2)}) collective-permute-start(bf16[2,48,1536]{2,1,0:T(8,128)(2,1)} %get-tuple-element.1307), channel_id=1, source_target_pairs={{0,4},{2,6},{4,0},{6,2},{1,5},{3,7},{5,1},{7,3},{8,12},{10,14},{12... | collective-permute-start | bytes 884744 | tf_op jit(solution)/shard_map/ppermute | solution.py:175
  473.9 20.1 %collective-permute-start.42 = (bf16[2,48,1536]{2,1,0:T(8,128)(2,1)}, bf16[2,48,1536]{2,1,0:T(8,128)(2,1)}, u32[]{:S(2)}, u32[]{:S(2)}) collective-permute-start(bf16[2,48,1536]{2,1,0:T(8,128)(2,1)} %get-tuple-element.1308), channel_id=1, source_target_pairs={{0,6},{2,0},{4,2},{6,4},{1,7},{3,1},{5,3},{7,5},{8,14},{10,8},{12,... | collective-permute-start | bytes 884744 | tf_op jit(solution)/shard_map/ppermute | solution.py:175
  502.1 32.3 %collective-permute-start.46 = (bf16[4,2,48,1792]{3,2,1,0:T(8,128)(2,1)}, bf16[4,2,48,1792]{3,2,1,0:T(8,128)(2,1)S(1)}, u32[]{:S(2)}, u32[]{:S(2)}) collective-permute-start(bf16[4,2,48,1792]{3,2,1,0:T(8,128)(2,1)} %get-tuple-element.1361), channel_id=1, source_target_pairs={{0,16},{16,0},{1,17},{17,1},{2,18},{18,2},{3,19},{19,3},{4,20},{20... | collective-permute-start | bytes 4128776 | tf_op jit(solution)/shard_map/ppermute | solution.py:175
  503.3 32.1 %collective-permute-start.47 = (bf16[2,4,48,1792]{3,2,1,0:T(8,128)(2,1)}, bf16[2,4,48,1792]{3,2,1,0:T(8,128)(2,1)}, u32[]{:S(2)}, u32[]{:S(2)}) collective-permute-start(bf16[2,4,48,1792]{3,2,1,0:T(8,128)(2,1)} %get-tuple-element.1363), channel_id=1, source_target_pairs={{0,1},{1,0},{2,3},{3,2},{4,5},{5,4},{6,7},{7,6},{8,9},{9,8},{10,11... | collective-permute-start | bytes 4128776 | tf_op jit(solution)/shard_map/ppermute | solution.py:175
  504.8 28.3 %collective-permute-start.43 = (bf16[2,48,1536]{2,1,0:T(8,128)(2,1)}, bf16[2,48,1536]{2,1,0:T(8,128)(2,1)}, u32[]{:S(2)}, u32[]{:S(2)}) collective-permute-start(bf16[2,48,1536]{2,1,0:T(8,128)(2,1)} %get-tuple-element.1351), channel_id=1, source_target_pairs={{0,2},{2,4},{4,6},{6,0},{1,3},{3,5},{5,7},{7,1},{8,10},{10,12},{12... | collective-permute-start | bytes 884744 | tf_op jit(solution)/shard_map/ppermute | solution.py:175
  511.6 21.5 %collective-permute-start.44 = (bf16[2,48,1536]{2,1,0:T(8,128)(2,1)}, bf16[2,48,1536]{2,1,0:T(8,128)(2,1)}, u32[]{:S(2)}, u32[]{:S(2)}) collective-permute-start(bf16[2,48,1536]{2,1,0:T(8,128)(2,1)} %get-tuple-element.1352), channel_id=1, source_target_pairs={{0,4},{2,6},{4,0},{6,2},{1,5},{3,7},{5,1},{7,3},{8,12},{10,14},{12... | collective-permute-start | bytes 884744 | tf_op jit(solution)/shard_map/ppermute | solution.py:175
  513.3 19.7 %collective-permute-start.45 = (bf16[2,48,1536]{2,1,0:T(8,128)(2,1)}, bf16[2,48,1536]{2,1,0:T(8,128)(2,1)}, u32[]{:S(2)}, u32[]{:S(2)}) collective-permute-start(bf16[2,48,1536]{2,1,0:T(8,128)(2,1)} %get-tuple-element.1353), channel_id=1, source_target_pairs={{0,6},{2,0},{4,2},{6,4},{1,7},{3,1},{5,3},{7,5},{8,14},{10,8},{12,... | collective-permute-start | bytes 884744 | tf_op jit(solution)/shard_map/ppermute | solution.py:175
  539.8 22.5 %collective-permute-start.50 = (f32[528,1536]{1,0:T(8,128)}, f32[528,1536]{1,0:T(8,128)S(1)}, u32[]{:S(2)}, u32[]{:S(2)}) collective-permute-start(f32[528,1536]{1,0:T(8,128)} %get-tuple-element.1391), channel_id=1, source_target_pairs={{0,8},{8,0},{1,9},{9,1},{2,10},{10,2},{3,11},{11,3},{4,12},{12,4},... | collective-permute-start | bytes 9732104 | tf_op jit(solution)/shard_map/ppermute | solution.py:66
  581.5 23.4 %collective-permute-start.54 = (bf16[2,48,1792]{2,1,0:T(8,128)(2,1)S(1)}, bf16[2,48,1792]{2,1,0:T(8,128)(2,1)}, u32[]{:S(2)}, u32[]{:S(2)}) collective-permute-start(bf16[2,48,1792]{2,1,0:T(8,128)(2,1)S(1)} %copy-done.56), channel_id=1, source_target_pairs={{0,4},{2,6},{4,0},{6,2},{1,5},{3,7},{5,1},{7,3},{8,12},{10,14},{12... | collective-permute-start | bytes 1032200 | tf_op jit(solution)/shard_map/ppermute | solution.py:175
  582.9 22.1 %collective-permute-start.55 = (bf16[2,48,1792]{2,1,0:T(8,128)(2,1)S(1)}, bf16[2,48,1792]{2,1,0:T(8,128)(2,1)}, u32[]{:S(2)}, u32[]{:S(2)}) collective-permute-start(bf16[2,48,1792]{2,1,0:T(8,128)(2,1)S(1)} %copy-done.55), channel_id=1, source_target_pairs={{0,6},{2,0},{4,2},{6,4},{1,7},{3,1},{5,3},{7,5},{8,14},{10,8},{12,... | collective-permute-start | bytes 1032200 | tf_op jit(solution)/shard_map/ppermute | solution.py:175
  607.2 21.9 %collective-permute-start.63 = (f32[48,1792]{1,0:T(8,128)}, f32[48,1792]{1,0:T(8,128)}, u32[]{:S(2)}, u32[]{:S(2)}) collective-permute-start(f32[48,1792]{1,0:T(8,128)} %get-tuple-element.1527), channel_id=1, source_target_pairs={{0,8},{8,0},{1,9},{9,1},{2,10},{10,2},{3,11},{11,3},{4,12},{12,4},... | collective-permute-start | bytes 1032200 | tf_op jit(solution)/shard_map/ppermute | solution.py:66
  608.6 34.9 %collective-permute-start.56 = (bf16[256,1536]{1,0:T(8,128)(2,1)S(1)}, bf16[256,1536]{1,0:T(8,128)(2,1)}, u32[]{:S(2)}, u32[]{:S(2)}) collective-permute-start(bf16[256,1536]{1,0:T(8,128)(2,1)S(1)} %get-tuple-element.1458), channel_id=1, source_target_pairs={{0,1},{1,0},{2,3},{3,2},{4,5},{5,4},{6,7},{7,6},{8,9},{9,8},{10,11... | collective-permute-start | bytes 2359304 | tf_op jit(solution)/shard_map/ppermute | solution.py:66
  (104 other events, 791.5 us)

commit v3 on v2

--- a/solution.py
+++ b/solution.py
@@ -29,6 +29,7 @@
 EPSILON = 1e-05
 BF16 = jnp.bfloat16
 VM = 60
+UNROLL = 6
 F32 = jnp.float32
 
 
@@ -396,7 +397,7 @@
         out_ref[0, :, lanes] += jnp.where(low, made[0], made[1])
         return carry
 
-    lax.fori_loop(0, HC // 2, pair, 0)
+    lax.fori_loop(0, HC // 2, pair, 0, unroll=UNROLL)
 
 
 def span_state(state_ref, local_ref, before, heads):
@@ -637,6 +638,71 @@
     )(a, b)
 
 
+def outer_cut(a, b, inner, halo=0):
+    nx, nz, ny = lax.axis_size("x"), lax.axis_size("z"), lax.axis_size("y")
+    slots, tall, left = a.shape
+    rows, right = b.shape[1:]
+    deep = left // (2 * nx * nz * ny)
+    if nx != 2 or nz % 2 or deep % 16:
+        dims = (nx, nz, ny, 2, deep, right) if inner else (nx, 2, nz, ny, deep, right)
+        return cut_first(outer(a, b, halo).reshape(dims), inner)
+    tile = left // 4
+    few = nz // 2
+
+    def kernel(place_ref, a_ref, b_ref, stay0, go0, stay1, go1):
+        at = pl.program_id(0)
+        x = at // 2
+        here = place_ref[0] == x
+        low = place_ref[1] == 0
+        part = a_ref[...][:, halo:].reshape(-1, tile)
+        made = tn(part, b_ref[...].reshape(part.shape[0], -1)).astype(BF16)
+
+        def split(value):
+            return jnp.where(low, value[:, 0], value[:, 1]), jnp.where(low, value[:, 1], value[:, 0])
+
+        if inner:
+            made = made.reshape(few, ny, 2, deep, right)
+            group = pl.ds((at % 2) * few, few)
+
+            @pl.when(here)
+            def _():
+                stay0[group] = made[:, :, 0]
+
+            @pl.when(jnp.logical_not(here))
+            def _():
+                go0[group] = made[:, :, 0]
+
+            stay1[x, group], go1[x, group] = split(made[:, :, 1])
+        else:
+            made = made.reshape(nz, ny, deep, right)
+            first = at % 2 == 0
+
+            @pl.when(first & here)
+            def _():
+                stay0[...] = made
+
+            @pl.when(first & jnp.logical_not(here))
+            def _():
+                go0[...] = made
+
+            @pl.when(jnp.logical_not(first))
+            def _():
+                stay1[x], go1[x] = split(made)
+
+    half0, half1 = (nz, ny, deep, right), (nx, nz, deep, right)
+    stay0, go0, stay1, go1 = call(
+        kernel,
+        (4,),
+        [
+            pl.BlockSpec(memory_space=pltpu.SMEM), pl.BlockSpec((slots, tall, tile), lambda i: (0, 0, i)),
+            fixed(slots, rows, right),
+        ],
+        [fixed(*half0), fixed(*half0), fixed(*half1), fixed(*half1)],
+        [shape(*d, dtype=BF16) for d in (half0, half0, half1, half1)],
+    )(jnp.stack([lax.axis_index("x"), lax.axis_index("y")]), a, b)
+    return [(stay0, [go0]), (stay1, [go1])]
+
+
 def rows_kernel(turned, halo, a_ref, b_ref, out_ref):
     value = a_ref[0, halo:]
     out_ref[0] = (nt if turned else nn)(value, b_ref[...])
@@ -811,6 +877,48 @@
         [tile, fixed(8, features)],
         [shape(rows, features, dtype=BF16), shape(8, features)],
     )(bounds, own_in, own_grad, d_own, d_came, back_own, back_came, gain)
+
+
+def start_kernel(ends_ref, starts_out, decays_out):
+    heads = head_map()
+    nz, slots, depth, _ = starts_out.shape
+    for slot in range(slots):
+        running = jnp.zeros((depth, EC), F32)
+        for k in range(nz):
+            starts_out[k, slot] = running.astype(BF16)
+            pieces = ends_ref[k, slot, :, EC:].astype(F32)
+            total = pieces[0:1] + pieces[1:2] + pieces[2:3]
+            decay = spread(jnp.broadcast_to(jnp.exp(total), (8, NS)), heads)
+            decays_out[k, slot] = decay
+            running = running * decay[0:1] + ends_ref[k, slot, :, :EC].astype(F32)
+
+
+def start_states(ends):
+    nz, slots, depth, _ = ends.shape
+    return pl.pallas_call(
+        start_kernel,
+        out_shape=[shape(nz, slots, depth, EC, dtype=BF16), shape(nz, slots, 8, EC)],
+        compiler_params=pltpu.CompilerParams(vmem_limit_bytes=VM * 1024 * 1024),
+        cost_estimate=NO_COST,
+    )(ends)
+
+
+def later_kernel(tails_ref, decays_ref, backs_out):
+    nz, slots, depth, _ = backs_out.shape
+    for slot in range(slots):
+        running = jnp.zeros((depth, EC), F32)
+        for k in reversed(range(nz)):
+            backs_out[k, slot] = running.astype(BF16)
+            running = running * decays_ref[k, slot, 0:1] + tails_ref[k, slot].astype(F32)
+
+
+def later_states(tails, decays):
+    return pl.pallas_call(
+        later_kernel,
+        out_shape=shape(*tails.shape, dtype=BF16),
+        compiler_params=pltpu.CompilerParams(vmem_limit_bytes=VM * 1024 * 1024),
+        cost_estimate=NO_COST,
+    )(tails, decays)
 
 
 def shards(
@@ -993,15 +1101,7 @@
     del live.state_part
     settle(live)
 
-    decays = jnp.exp(jnp.sum(live.ends[:, :, :3, EC : EC + HC].astype(F32), axis=2))
-    live.decays = jnp.broadcast_to(decays[..., None], decays.shape + (P_SIZE,)).reshape(nz, 2, 1, EC)
-    ends = live.ends[..., :EC].astype(F32)
-    running = jnp.zeros_like(ends[0])
-    starts = []
-    for k in range(nz):
-        starts.append(running.astype(BF16))
-        running = running * live.decays[k] + ends[k]
-    live.starts = jnp.stack(starts)
+    live.starts, live.decays = start_states(live.ends)
     live.out_rows = plane_stack(live.out_rows)
     del live.ends
     settle(live)
@@ -1057,21 +1157,13 @@
     settle(live)
 
     live.tails = exchange(live.back_part)
-    live.out_sums = outer(live.mixer_in, live.d_mix)
-    live.gate_sums = outer(live.normed, live.d_gate, HALO)
+    live.out_sums = outer_cut(live.mixer_in, live.d_mix, True)
+    live.gate_sums = outer_cut(live.normed, live.d_gate, False, HALO)
     live.mixer_own, live.mixer_part = two_slots(core, live.mixer_in, live.back_weight)
     del live.back_part, live.d_mix, live.mixer_in, live.back_weight
     settle(live)
 
-    tails = live.tails.astype(F32)
-    running = jnp.zeros_like(tails[0])
-    backs = [None] * nz
-    for k in reversed(range(nz)):
-        backs[k] = running.astype(BF16)
-        running = running * live.decays[k] + tails[k]
-    live.backs = jnp.stack(backs)
-    live.out_sums = cut_first(live.out_sums.reshape(nx, nz, ny, 2, thin // 2, features), True)
-    live.gate_sums = cut_first(live.gate_sums.reshape(nx, 2, nz, ny, deep, EC), False)
+    live.backs = later_states(live.tails, live.decays)
     del live.tails, live.decays
     settle(live)
     live.back_in = exchange(live.backs)
@@ -1155,11 +1247,10 @@
     )(d_proj, mine, theirs, proj, own_taps)
 
     live.d_proj, live.g_own = d_proj, g_own
-    live.scan_sums = outer(live.normed, d_proj)
+    live.scan_sums = outer_cut(live.normed, d_proj, False)
     del live.bc_mine, live.bc_theirs, live.proj, live.own_taps, live.normed
     settle(live)
 
-    live.scan_sums = cut_first(live.scan_sums.reshape(nx, 2, nz, ny, deep, BACK), False)
     live.gate_sums = cut_line(live.gate_sums)
     settle(live)
     live.scan_sums = move_first(live.scan_sums)
@@ -1183,10 +1274,9 @@
     live.scan_sums = cut_line(live.scan_sums)
     settle(live)
     live.scan_sums = move(live.scan_sums, "z")
-    live.grad_in, g_gain_in = input_rows(
+    live.grad_in, live.g_gain_in = input_rows(
         bounds, live.own_in, live.own_grad, live.d_own, live.d_came, live.back_own, live.back_came, live.gain_in
     )
-
     def spread_half(value, width):
         parts = value.reshape(value.shape[:-1] + (nx, 1, width // (2 * nx)))
         zero = jnp.zeros_like(parts)
@@ -1206,23 +1296,17 @@
         axis=1,
     )
     head_sum = spread_half(jnp.sum(live.g_heads, axis=0)[:3, :HC], H)
-    packed = jnp.concatenate(
-        [
-            taps_sum[: CONV + 1].reshape(-1),
-            spread_half(live.g_gain_out[0], E),
-            g_gain_in[0],
-            head_sum.reshape(-1),
-            live.stats[0, :3],
-        ]
+    live.known = jnp.concatenate(
+        [taps_sum[: CONV + 1].reshape(-1), spread_half(live.g_gain_out[0], E), head_sum.reshape(-1), live.stats[0, :3]]
     )
-    live.packed = jnp.pad(packed, (0, -packed.shape[0] % 1024)).reshape(-1, NS)
-    live.grad_keep, live.grad_send = by_slots(live.grad_in)
-    del live.own_in, live.own_grad, live.d_own, live.d_came, live.g_taps, live.g_own, live.g_heads, live.grad_in
-    del live.g_gain_out, live.gain_in, live.back_own, live.back_came, live.stats
-    settle(live)
-
-    packed = sum_everywhere(live.packed).reshape(-1)
-    grad_in = by_index("y", live.grad_keep, swapped(live.grad_send, "y"))
+    del live.g_taps, live.g_own, live.g_heads, live.g_gain_out, live.stats
+
+    settle(live)
+
+    packed = jnp.concatenate([live.known, live.g_gain_in[0]])
+    packed = sum_everywhere(jnp.pad(packed, (0, -packed.shape[0] % 1024)).reshape(-1, NS)).reshape(-1)
+    grad_keep, grad_send = by_slots(live.grad_in)
+    grad_in = by_index("y", grad_keep, swapped(grad_send, "y"))
     block_out = by_index("y", live.block_keep, live.block_send)
     g_out = live.out_sums.reshape(thin, features)
 
@@ -1232,15 +1316,15 @@
     gate_mine, gate_came = row_share(live.gate_sums)
     scan_mine, scan_came = row_share(add_up(live.scan_sums))
     place_at = [0]
-    for size in ((CONV + 1) * CH, E, features, 3 * H, 3):
+    for size in ((CONV + 1) * CH, E, 3 * H, 3, features):
         place_at.append(place_at[-1] + size)
     device = ((ix * 2 + core) * nz + iz) * ny + iy
     taps_total = packed[: place_at[1]].reshape(CONV + 1, CH)
     taps_mine = lax.dynamic_slice_in_dim(taps_total, device * chan, chan, 1)
     gain_out_mine = lax.dynamic_slice_in_dim(packed[place_at[1] : place_at[2]], device * thin, thin)
-    gain_in_mine = lax.dynamic_slice_in_dim(packed[place_at[2] : place_at[3]], device * deep, deep)
-    head_total = packed[place_at[3] : place_at[4]].reshape(3, H)
-    valid_sums = packed[place_at[4] : place_at[5]]
+    gain_in_mine = lax.dynamic_slice_in_dim(packed[place_at[4] : place_at[5]], device * deep, deep)
+    head_total = packed[place_at[2] : place_at[3]].reshape(3, H)
+    valid_sums = packed[place_at[3] : place_at[4]]
 
     def both_halves(mine_part, came_part):
         pair = by_index("core", mine_part, came_part)

time: 655 us -> 628 us (0.959)
  local copies, waits for them, and re-layouts: 82.4 us -> 67.7 us
  other arithmetic: 58 us -> 50.8 us
    pallas_call x3 -> x5, Pallas kernels: 31.2 us -> 39.6 us  [the longest x3 34.4 us: outer_cut(): call(kernel, (4,), [pl.BlockSpec(memory_space=pltpu.SMEM), pl.BlockSpec((...]
    squeeze x15 -> x8, local copies, waits for them, and re-layouts: 17.6 us -> 9.22 us  [take(): return lax.dynamic_index_in_dim(value, index, axis, keepdims=False)]
    ppermute x21, waiting for transfers between devices: 30.6 us -> 23.2 us  [move(): lax.ppermute(piece, axis, [(i, (i + step) % size) for i in range(size)])]
    pallas_call x1, Pallas kernels: 24.9 us -> 17.7 us  [shards(): call(intra_kernel, (2, spans), [in_span(EC), in_span(2 * NS), in_span(NS)...]
    slice x5 -> x2, local copies, waits for them, and re-layouts: 7.81 us -> 0.89 us  [the longest x1 0.82 us: shards(): packed = jnp.concatenate([live.known, live.g_gain_in[0]])]
    unnamed x177 -> x179, local copies, waits for them, and re-layouts: 24.3 us -> 28.9 us
  transfers between devices with their start and end apart: 69 -> 69, of which waited for: 26 -> 27; matrix products, arithmetic and copies ran while one was open for 8% -> 8% of each run, Pallas kernels for 34% -> 36%
where the time goes in v3:
time: 628 us; the launch traced here: 620 us
  Pallas kernels  277 us (44%)
  starting transfers between devices  114 us (18%)
  waiting for transfers between devices  107 us (17%)
  local copies, waits for them, and re-layouts  67.7 us (11%)
  other arithmetic  50.8 us (8%)
    pallas_call x2, Pallas kernels, back_call(): call(functools.partial(back_kernel, len(kept)), (spans,), [one(EC), one(2...  51.4 us
    ppermute x21, waiting for transfers between devices, others(): lax.ppermute(piece, axis, route)  43.7 us
    ppermute x21, starting transfers between devices, move(): lax.ppermute(piece, axis, [(i, (i + step) % size) for i in range(size)])  37.5 us
    pallas_call x3, Pallas kernels, by_rows_of(): call(kernel, (slots,), [pl.BlockSpec(memory_space=pltpu.SMEM), pl.BlockSp...  35.1 us
    pallas_call x3, Pallas kernels, outer_cut(): call(kernel, (4,), [pl.BlockSpec(memory_space=pltpu.SMEM), pl.BlockSpec((...  34.4 us
    pallas_call x1, Pallas kernels, shards(): call(functools.partial(close_kernel, rows, nz), (2,), [whole_row(rows, EC...  33.8 us
    unnamed x179, local copies, waits for them, and re-layouts  28.9 us
    ppermute x21, starting transfers between devices, others(): lax.ppermute(piece, axis, route)  28.8 us
  transfers between devices with their start and end apart: 69, of which 27 were waited for; matrix products, arithmetic and copies ran while one was open for 8% of the time, Pallas kernels for 36%

profile of v3, /device:TPU:0, one launch (start us, length us, event | category | flops | bytes accessed | tf_op | source)
XLA Modules:
  0.0 619.6 jit_solution(3660176724208448861)
XLA Ops:
  2.2 4.0 dynamic-slice_reduce_fusion
  10.2 2.6 collective-permute-start.2
  16.3 2.6 collective-permute-start.4
  20.9 2.8 all-to-all-start
  23.7 8.0 %collective-permute-done.2 = bf16[256,1536]{1,0:T(8,128)(2,1)} collective-permute-done((bf16[256,1536]{1,0:T(8,128)(2,1)}, bf16[256,1536]{1,0:T(8,128)(2,1)}, u32[]{:S(2)}, u32[]{:S(2)}) %collective-permute-start.2) | collective-permute-done | bytes 786464 | tf_op jit(solution)/shard_map/ppermute | solution.py:67
  31.6 3.4 maximum_select_fusion.3
  35.0 13.6 %collective-permute-done.1 = bf16[256,1536]{1,0:T(8,128)(2,1)} collective-permute-done((bf16[256,1536]{1,0:T(8,128)(2,1)}, bf16[256,1536]{1,0:T(8,128)(2,1)}, u32[]{:S(2)}, u32[]{:S(2)}) %collective-permute-start.1) | collective-permute-done | bytes 786464 | tf_op jit(solution)/shard_map/ppermute | solution.py:67
  48.6 2.8 maximum_select_fusion.2
  53.9 2.5 shard_map.211
  57.5 2.6 collective-permute-start.6
  67.7 13.5 %collective-permute-done.10.refs_3_ = bf16[4,48,1920]{2,1,0:T(8,128)(2,1)S(1)} collective-permute-done((bf16[4,48,1920]{2,1,0:T(8,128)(2,1)S(1)}, bf16[4,48,1920]{2,1,0:T(8,128)(2,1)S(1)}, u32[]{:S(2)}, u32[]{:S(2)}) %collective-permute-start.10) | collective-permute-done | bytes 737312 | tf_op jit(solution)/shard_map/ppermute | solution.py:46
  90.9 3.2 collective-permute-start.13
  96.8 3.5 maximum_select_fusion
  103.3 8.3 %collective-permute-done.12.refs_2_ = bf16[2,48,1536]{2,1,0:T(8,128)(2,1)} collective-permute-done((bf16[2,48,1536]{2,1,0:T(8,128)(2,1)S(1)}, bf16[2,48,1536]{2,1,0:T(8,128)(2,1)}, u32[]{:S(2)}, u32[]{:S(2)}) %collective-permute-start.12) | collective-permute-done | bytes 294944 | tf_op jit(solution)/shard_map/ppermute | solution.py:46
  111.6 14.9 %collective-permute-done.14.refs_1_ = bf16[2,4,48,1920]{3,2,1,0:T(8,128)(2,1)} collective-permute-done((bf16[2,4,48,1920]{3,2,1,0:T(8,128)(2,1)S(1)}, bf16[2,4,48,1920]{3,2,1,0:T(8,128)(2,1)}, u32[]{:S(2)}, u32[]{:S(2)}) %collective-permute-start.14) | collective-permute-done | bytes 1474592 | tf_op jit(solution)/shard_map/ppermute | solution.py:46
  133.1 13.4 %shard_map.214 = (f32[2,528,1920]{2,1,0:T(8,128)}, bf16[2,2,4,2,48,1920]{5,4,3,2,1,0:T(8,128)(2,1)}) custom-call(s32[8]{0:T(128)} %stack.432.table_ref, bf16[2,528,1536]{2,1,0:T(8,128)(2,1)} %fusion.2.a_ref, bf16[2,4,48,1920]{3,2,1,0:T(8,128)(2,1)} %copy-done, bf16[2,4,48,1920]{3,2,1,0:T(8,128)(2,1)} %collective-permute-done.14.refs_1_, ...), custom_call_target="tpu_custom_call" | custom-call | bytes 1024 | tf_op jit(solution)/shard_map/pallas_call | solution.py:751
  156.8 15.3 %shard_map.216 = (f32[2,512,1536]{2,1,0:T(8,128)}, f32[2,512,256]{2,1,0:T(8,128)}, f32[2,512,128]{2,1,0:T(8,128)}, f32[2,512,128]{2,1,0:T(8,128)}, bf16[4,2,32,1...) custom-call(f32[2,528,1920]{2,1,0:T(8,128)} %get-tuple-element.1331.proj.proj_ref, ...), custom_call_target="tpu_custom_call" | custom-call | bytes 1024 | tf_op jit(solution)/shard_map/pallas_call | solution.py:1063
  185.2 5.3 all-to-all-start.1
  193.3 17.7 %shard_map.218.part_ref = f32[2,512,1536]{2,1,0:T(8,128)} custom-call(f32[2,512,1536]{2,1,0:T(8,128)} %get-tuple-element.1258.x_ref, f32[2,512,256]{2,1,0:T(8,128)} %get-tuple-element.1259.bc_ref, f32[2,512,128]{2,1,0:T(8,128)} %get-tuple-element.1260.step_ref, f32[2,512,128]{2,1,0:T(8,128)} %get-tuple-element.1261.cum_ref, f32[8,128]{1,0:T(8,128)} %stack.409.heads_par), custom_call_target="tpu_custom_call" | custom-call | bytes 1024 | tf_op jit(solution)/shard_map/pallas_call | solution.py:1089
  212.7 2.9 shard_map.219
  220.5 4.9 all-to-all-start.2
  226.0 2.6 pad_add_fusion.3
  229.2 10.8 %shard_map.221 = (f32[2,512,1536]{2,1,0:T(8,128)}, bf16[2,2,4,2,48,1536]{5,4,3,2,1,0:T(8,128)(2,1)}) custom-call(s32[8]{0:T(128)} %stack.457.table_ref, bf16[2,528,1536]{2,1,0:T(8,128)(2,1)} %fusion.2.a_ref, bf16[2,4,48,1536]{3,2,1,0:T(8,128)(2,1)} %copy-done.2, bf16[2,4,48,1536]{3,2,1,0:T(8,128)(2,1)} %collective-permute-done.19.refs_1_, ...), custom_call_target="tpu_custom_call" | custom-call | bytes 1024 | tf_op jit(solution)/shard_map/pallas_call | solution.py:751
  240.1 4.7 fusion.3.a_ref.b_ref
  246.9 10.9 %shard_map.222 = (f32[2,512,1536]{2,1,0:T(8,128)}, bf16[2,4,2,2,48,1536]{5,4,3,2,1,0:T(8,128)(2,1)}) custom-call(s32[8]{0:T(128)} %stack.462.table_ref, bf16[2,512,1536]{2,1,0:T(8,128)(2,1)} %fusion.3.a_ref.b_ref, bf16[2,4,48,1536]{3,2,1,0:T(8,128)(2,1)} %copy-done.4, bf16[2,4,48,1536]{3,2,1,0:T(8,128)(2,1)} %collective-permute-done.26.refs_1_, ...), custom_call_target="tpu_custom_call" | custom-call | bytes 1024 | tf_op jit(solution)/shard_map/pallas_call | solution.py:751
  258.4 12.2 %shard_map.223 = (f32[2,512,1536]{2,1,0:T(8,128)}, f32[2,512,128]{2,1,0:T(8,128)}) custom-call(f32[2,512,1536]{2,1,0:T(8,128)} %shard_map.218.part_ref, f32[2,512,256]{2,1,0:T(8,128)} %get-tuple-element.1259.bc_ref, f32[2,512,128]{2,1,0:T(8,128)} %get-tuple-element.1261.cum_ref, f32[2,2,8,128]{3,2,1,0:T(8,128)} %broadcast_in_dim.48.before_ref, ...), custom_call_target="tpu_custom_call" | custom-call | bytes 1024 | tf_op jit(solution)/shard_map/pallas_call | solution.py:1130
  274.8 17.3 %shard_map.224 = (bf16[2,512,1536]{2,1,0:T(8,128)(2,1)}, f32[2,512,1536]{2,1,0:T(8,128)}, bf16[2,512,1536]{2,1,0:T(8,128)(2,1)}, f32[8,1536]{1,0:T(8,128)}, bf16...) custom-call(f32[2,512,1536]{2,1,0:T(8,128)} %get-tuple-element.1056.y_ref, ...), custom_call_target="tpu_custom_call" | custom-call | bytes 1024 | tf_op jit(solution)/shard_map/pallas_call | solution.py:1143
  292.1 4.6 all-to-all-start.3
  297.3 10.4 %shard_map.227 = (bf16[4,2,48,1536]{3,2,1,0:T(8,128)(2,1)}, bf16[4,2,48,1536]{3,2,1,0:T(8,128)(2,1)}, bf16[2,4,48,1536]{3,2,1,0:T(8,128)(2,1)}, bf16[2,4,48,1536]{3,2,1,0:T(8,128)(2,1)}) custom-call(s32[2]{0:T(128)} %pad_add_fusion.4.place_ref, bf16[2,512,1536]{2,1,0:T(8,128)(2,1)} %get-tuple-element.1095.a_ref, bf16[2,512,1536]{2,1,0:T(8,128)(2,1)} %fusion.3.a_ref.b_ref), custom_call_target="tpu_custom_call" | custom-call | bytes 1024 | tf_op jit(solution)/shard_map/pallas_call | solution.py:693
  307.7 10.3 %shard_map.226 = (f32[512,1536]{1,0:T(8,128)}, f32[512,1536]{1,0:T(8,128)}) custom-call(s32[1]{0:T(128)} %bitcast.65.core_ref, bf16[2,512,1536]{2,1,0:T(8,128)(2,1)} %get-tuple-element.1095.a_ref, bf16[1536,1536]{1,0:T(8,128)(2,1)} %bitcast.226), custom_call_target="tpu_custom_call" | custom-call | bytes 1024 | tf_op jit(solution)/shard_map/pallas_call | solution.py:800
  318.0 10.6 %shard_map.225 = (bf16[4,2,48,1536]{3,2,1,0:T(8,128)(2,1)}, bf16[4,2,48,1536]{3,2,1,0:T(8,128)(2,1)}, bf16[2,4,48,1536]{3,2,1,0:T(8,128)(2,1)}, bf16[2,4,48,1536]{3,2,1,0:T(8,128)(2,1)}) custom-call(s32[2]{0:T(128)} %pad_add_fusion.4.place_ref, bf16[2,528,1536]{2,1,0:T(8,128)(2,1)} %fusion.2.a_ref, bf16[2,512,1536]{2,1,0:T(8,128)(2,1)} %get-tuple-element.1386.b_ref.dgate_ref), custom_call_target="tpu_custom_call" | custom-call | bytes 1024 | tf_op jit(solution)/shard_map/pallas_call | solution.py:693
  334.4 5.1 all-to-all-start.4
  339.5 25.8 %shard_map.229 = (f32[2,512,1536]{2,1,0:T(8,128)}, f32[2,512,256]{2,1,0:T(8,128)}, f32[2,512,128]{2,1,0:T(8,128)}, f32[2,512,128]{2,1,0:T(8,128)}) custom-call(f32[2,512,1536]{2,1,0:T(8,128)} %get-tuple-element.1258.x_ref, f32[2,512,256]{2,1,0:T(8,128)} %get-tuple-element.1259.bc_ref, f32[2,512,128]{2,1,0:T(8,128)} %get-tuple-element.1260.step_ref, ...), custom_call_target="tpu_custom_call" | custom-call | bytes 1024 | tf_op jit(solution)/shard_map/pallas_call | solution.py:1175
  368.4 25.6 %shard_map.230 = (f32[2,512,1536]{2,1,0:T(8,128)}, f32[2,512,256]{2,1,0:T(8,128)}, f32[2,512,128]{2,1,0:T(8,128)}, f32[2,512,128]{2,1,0:T(8,128)}) custom-call(f32[2,512,1536]{2,1,0:T(8,128)} %get-tuple-element.1258.x_ref, f32[2,512,256]{2,1,0:T(8,128)} %get-tuple-element.1259.bc_ref, ...), custom_call_target="tpu_custom_call", output_to_operand_aliasing={{0}: (8, {}), {1}: (9, {}), {2}: (10, {}), {3}: (11, {})} | custom-call | bytes 1024 | tf_op jit(solution)/shard_map/pallas_call | solution.py:1175
  396.2 3.1 add_convert_fusion.2
  412.0 5.0 shard_map.232
  417.0 33.8 %shard_map.231 = (bf16[2,528,1792]{2,1,0:T(8,128)(2,1)}, f32[2,512,128]{2,1,0:T(8,128)}, f32[2,512,128]{2,1,0:T(8,128)}, f32[2,8,1536]{2,1,0:T(8,128)}, f32[2,8,128]{2,1,0:T(8,128)}) custom-call(f32[2,512,1536]{2,1,0:T(8,128)} %get-tuple-element.1258.x_ref, f32[2,512,256]{2,1,0:T(8,128)} %get-tuple-element.1259.bc_ref, ...), custom_call_target="tpu_custom_call" | custom-call | bytes 1024 | tf_op jit(solution)/shard_map/pallas_call | solution.py:1209
  465.0 2.6 shard_map.233
  467.6 13.4 %shard_map.234 = (bf16[4,2,48,1792]{3,2,1,0:T(8,128)(2,1)}, bf16[4,2,48,1792]{3,2,1,0:T(8,128)(2,1)}, bf16[2,4,48,1792]{3,2,1,0:T(8,128)(2,1)}, bf16[2,4,48,1792]{3,2,1,0:T(8,128)(2,1)}) custom-call(s32[2]{0:T(128)} %pad_add_fusion.4.place_ref, bf16[2,528,1536]{2,1,0:T(8,128)(2,1)} %fusion.2.a_ref, bf16[2,528,1792]{2,1,0:T(8,128)(2,1)} %get-tuple-element.1385.b_ref.dproj_ref), custom_call_target="tpu_custom_call" | custom-call | bytes 1024 | tf_op jit(solution)/shard_map/pallas_call | solution.py:693
  488.3 6.8 %collective-permute-start.43 = (bf16[2,48,1536]{2,1,0:T(8,128)(2,1)}, bf16[2,48,1536]{2,1,0:T(8,128)(2,1)}, u32[]{:S(2)}, u32[]{:S(2)}) collective-permute-start(bf16[2,48,1536]{2,1,0:T(8,128)(2,1)} %get-tuple-element.1397), channel_id=1, source_target_pairs={{0,2},{2,4},{4,6},{6,0},{1,3},{3,5},{5,7},{7,1},{8,10},{10,12},{12... | collective-permute-start | bytes 884744 | tf_op jit(solution)/shard_map/ppermute | solution.py:176
  497.5 19.1 %shard_map.235 = (f32[528,1536]{1,0:T(8,128)}, f32[528,1536]{1,0:T(8,128)}) custom-call(s32[1]{0:T(128)} %bitcast.65.core_ref, bf16[2,528,1792]{2,1,0:T(8,128)(2,1)} %get-tuple-element.1385.b_ref.dproj_ref, bf16[2,512,1536]{2,1,0:T(8,128)(2,1)} %get-tuple-element.1386.b_ref.dgate_ref, bf16[1536,1920]{1,0:T(8,128)(2,1)} %bitcast.225, bf16[1536,1536]{1,0:T(8,128)(2,1)} %bitcast.227), custom_call_target="tpu_custom_call" | custom-call | bytes 1024 | tf_op jit(solution)/shard_map/pallas_call | solution.py:778
  535.0 4.1 collective-permute-done.48.across_ref
  539.1 2.8 collective-permute-done.49.later_ref
  549.4 6.9 %collective-permute-start.53 = (bf16[2,48,1792]{2,1,0:T(8,128)(2,1)}, bf16[2,48,1792]{2,1,0:T(8,128)(2,1)S(1)}, u32[]{:S(2)}, u32[]{:S(2)}) collective-permute-start(bf16[2,48,1792]{2,1,0:T(8,128)(2,1)} %get-tuple-element.1498), channel_id=1, source_target_pairs={{0,2},{2,4},{4,6},{6,0},{1,3},{3,5},{5,7},{7,1},{8,10},{10,12},{12... | collective-permute-start | bytes 1032200 | tf_op jit(solution)/shard_map/ppermute | solution.py:176
  559.7 6.5 %shard_map.236 = (bf16[512,1536]{1,0:T(8,128)(2,1)}, f32[8,1536]{1,0:T(8,128)}) custom-call(s32[2]{0:T(128)} %get-tuple-element.1575.bounds_ref, bf16[512,1536]{1,0:T(8,128)(2,1)} %bitcast.220, bf16[512,1536]{1,0:T(8,128)(2,1)} %bitcast.224, f32[528,1536]{1,0:T(8,128)} %get-tuple-element.1484.own_ref, f32[528,1536]{1,0:T(8,128)} %copy-done.30, ...), custom_call_target="tpu_custom_call" | custom-call | bytes 1024 | tf_op jit(solution)/shard_map/pallas_call | solution.py:870
  566.4 13.4 %collective-permute-done.54 = bf16[2,48,1792]{2,1,0:T(8,128)(2,1)S(1)} collective-permute-done((bf16[2,48,1792]{2,1,0:T(8,128)(2,1)}, bf16[2,48,1792]{2,1,0:T(8,128)(2,1)S(1)}, u32[]{:S(2)}, u32[]{:S(2)}) %collective-permute-start.54) | collective-permute-done | bytes 344096 | tf_op jit(solution)/shard_map/ppermute | solution.py:176
  589.5 7.8 %collective-permute-start.59 = (f32[168,128]{1,0:T(8,128)S(1)}, f32[168,128]{1,0:T(8,128)S(1)}, u32[]{:S(2)}, u32[]{:S(2)}) collective-permute-start(f32[168,128]{1,0:T(8,128)S(1)} %fusion.48), channel_id=1, source_target_pairs={{0,2},{2,0},{4,6},{6,4},{1,3},{3,1},{5,7},{7,5},{8,10},{10,8},{12,... | collective-permute-start | bytes 258056 | tf_op jit(solution)/shard_map/ppermute | solution.py:217
  616.6 2.8 maximum_select_fusion.5
  (486 shorter events, 189.9 us)
Async XLA Ops:
  10.2 21.4 %collective-permute-start.2 = (bf16[256,1536]{1,0:T(8,128)(2,1)}, bf16[256,1536]{1,0:T(8,128)(2,1)}, u32[]{:S(2)}, u32[]{:S(2)}) collective-permute-start(bf16[256,1536]{1,0:T(8,128)(2,1)} %get-tuple-element.1521), channel_id=1, source_target_pairs={{0,1},{1,0},{2,3},{3,2},{4,5},{5,4},{6,7},{7,6},{8,9},{9,8},{10,11... | collective-permute-start | bytes 2359304 | tf_op jit(solution)/shard_map/ppermute | solution.py:67
  13.8 34.8 %collective-permute-start.1 = (bf16[256,1536]{1,0:T(8,128)(2,1)}, bf16[256,1536]{1,0:T(8,128)(2,1)}, u32[]{:S(2)}, u32[]{:S(2)}) collective-permute-start(bf16[256,1536]{1,0:T(8,128)(2,1)} %get-tuple-element.1523), channel_id=1, source_target_pairs={{0,1},{1,0},{2,3},{3,2},{4,5},{5,4},{6,7},{7,6},{8,9},{9,8},{10,11... | collective-permute-start | bytes 2359304 | tf_op jit(solution)/shard_map/ppermute | solution.py:67
  14.6 39.1 %collective-permute-start.3 = (bf16[2,48,1920]{2,1,0:T(8,128)(2,1)S(1)}, bf16[2,48,1920]{2,1,0:T(8,128)(2,1)S(1)}, u32[]{:S(2)}, u32[]{:S(2)}) collective-permute-start(bf16[2,48,1920]{2,1,0:T(8,128)(2,1)S(1)} %slice.180.refs_0_), channel_id=1, source_target_pairs={{0,2},{2,4},{4,6},{6,0},{1,3},{3,5},{5,7},{7,1},{8,10},{10,12},{12... | collective-permute-start | bytes 1105928 | tf_op jit(solution)/shard_map/ppermute | solution.py:46
  16.3 37.5 %collective-permute-start.4 = (bf16[2,48,1920]{2,1,0:T(8,128)(2,1)S(1)}, bf16[2,48,1920]{2,1,0:T(8,128)(2,1)S(1)}, u32[]{:S(2)}, u32[]{:S(2)}) collective-permute-start(bf16[2,48,1920]{2,1,0:T(8,128)(2,1)S(1)} %slice.180.refs_0_), channel_id=1, source_target_pairs={{0,4},{2,6},{4,0},{6,2},{1,5},{3,7},{5,1},{7,3},{8,12},{10,14},{12... | collective-permute-start | bytes 1105928 | tf_op jit(solution)/shard_map/ppermute | solution.py:46
  18.8 34.9 %collective-permute-start.5 = (bf16[2,48,1920]{2,1,0:T(8,128)(2,1)S(1)}, bf16[2,48,1920]{2,1,0:T(8,128)(2,1)S(1)}, u32[]{:S(2)}, u32[]{:S(2)}) collective-permute-start(bf16[2,48,1920]{2,1,0:T(8,128)(2,1)S(1)} %slice.180.refs_0_), channel_id=1, source_target_pairs={{0,6},{2,0},{4,2},{6,4},{1,7},{3,1},{5,3},{7,5},{8,14},{10,8},{12,... | collective-permute-start | bytes 1105928 | tf_op jit(solution)/shard_map/ppermute | solution.py:46
  20.9 32.9 %all-to-all-start = ((bf16[32,8,128]{2,1,0:T(8,128)(2,1)}), bf16[32,8,128]{2,1,0:T(8,128)(2,1)S(1)}, u32[]{:S(2)}, u32[]{:S(2)}) async-start(bf16[32,8,128]{2,1,0:T(8,128)(2,1)} %broadcast_in_dim.42), calls=%async_computation | async-start | bytes 131072 | tf_op jit(solution)/shard_map/all_to_all | solution.py:58
  56.6 26.6 %collective-permute-start.8 = (bf16[512,1536]{1,0:T(8,128)(2,1)}, bf16[512,1536]{1,0:T(8,128)(2,1)}, u32[]{:S(2)}, u32[]{:S(2)}) collective-permute-start(bf16[512,1536]{1,0:T(8,128)(2,1)} %bitcast.216), channel_id=1, source_target_pairs={{0,8},{8,0},{1,9},{9,1},{2,10},{10,2},{3,11},{11,3},{4,12},{12,4},... | collective-permute-start | bytes 4718600 | tf_op jit(solution)/shard_map/ppermute | solution.py:67
  90.9 20.6 %collective-permute-start.12 = (bf16[2,48,1536]{2,1,0:T(8,128)(2,1)S(1)}, bf16[2,48,1536]{2,1,0:T(8,128)(2,1)}, u32[]{:S(2)}, u32[]{:S(2)}) collective-permute-start(bf16[2,48,1536]{2,1,0:T(8,128)(2,1)S(1)} %slice.179.refs_0_), channel_id=1, source_target_pairs={{0,4},{2,6},{4,0},{6,2},{1,5},{3,7},{5,1},{7,3},{8,12},{10,14},{12... | collective-permute-start | bytes 884744 | tf_op jit(solution)/shard_map/ppermute | solution.py:46
  90.9 20.6 %collective-permute-start.13 = (bf16[2,48,1536]{2,1,0:T(8,128)(2,1)S(1)}, bf16[2,48,1536]{2,1,0:T(8,128)(2,1)}, u32[]{:S(2)}, u32[]{:S(2)}) collective-permute-start(bf16[2,48,1536]{2,1,0:T(8,128)(2,1)S(1)} %slice.179.refs_0_), channel_id=1, source_target_pairs={{0,6},{2,0},{4,2},{6,4},{1,7},{3,1},{5,3},{7,5},{8,14},{10,8},{12,... | collective-permute-start | bytes 884744 | tf_op jit(solution)/shard_map/ppermute | solution.py:46
  94.1 32.4 %collective-permute-start.14 = (bf16[2,4,48,1920]{3,2,1,0:T(8,128)(2,1)S(1)}, bf16[2,4,48,1920]{3,2,1,0:T(8,128)(2,1)}, u32[]{:S(2)}, u32[]{:S(2)}) collective-permute-start(bf16[2,4,48,1920]{3,2,1,0:T(8,128)(2,1)S(1)} %get-tuple-element.860.refs_0_), channel_id=1, source_target_pairs={{0,16},{16,0},{1,17},{17,1},{2,18},{18,2},{3,19},{19,3},{4,20},{20... | collective-permute-start | bytes 4423688 | tf_op jit(solution)/shard_map/ppermute | solution.py:46
  94.6 32.2 %collective-permute-start.15 = (bf16[2,4,48,1920]{3,2,1,0:T(8,128)(2,1)S(1)}, bf16[2,4,48,1920]{3,2,1,0:T(8,128)(2,1)}, u32[]{:S(2)}, u32[]{:S(2)}) collective-permute-start(bf16[2,4,48,1920]{3,2,1,0:T(8,128)(2,1)S(1)} %get-tuple-element.862.refs_2_), channel_id=1, source_target_pairs={{0,1},{1,0},{2,3},{3,2},{4,5},{5,4},{6,7},{7,6},{8,9},{9,8},{10,11... | collective-permute-start | bytes 4423688 | tf_op jit(solution)/shard_map/ppermute | solution.py:46
  150.7 27.9 %collective-permute-start.19 = (bf16[2,4,48,1536]{3,2,1,0:T(8,128)(2,1)S(1)}, bf16[2,4,48,1536]{3,2,1,0:T(8,128)(2,1)}, u32[]{:S(2)}, u32[]{:S(2)}) collective-permute-start(bf16[2,4,48,1536]{3,2,1,0:T(8,128)(2,1)S(1)} %get-tuple-element.1020.refs_0_), channel_id=1, source_target_pairs={{0,16},{16,0},{1,17},{17,1},{2,18},{18,2},{3,19},{19,3},{4,20},{20... | collective-permute-start | bytes 3538952 | tf_op jit(solution)/shard_map/ppermute | solution.py:46
  152.1 27.0 %collective-permute-start.20 = (bf16[2,4,48,1536]{3,2,1,0:T(8,128)(2,1)S(1)}, bf16[2,4,48,1536]{3,2,1,0:T(8,128)(2,1)}, u32[]{:S(2)}, u32[]{:S(2)}) collective-permute-start(bf16[2,4,48,1536]{3,2,1,0:T(8,128)(2,1)S(1)} %get-tuple-element.1022.refs_2_), channel_id=1, source_target_pairs={{0,1},{1,0},{2,3},{3,2},{4,5},{5,4},{6,7},{7,6},{8,9},{9,8},{10,11... | collective-permute-start | bytes 3538952 | tf_op jit(solution)/shard_map/ppermute | solution.py:46
  152.6 19.5 %collective-permute-start.21 = (bf16[2,48,1536]{2,1,0:T(8,128)(2,1)S(1)}, bf16[2,48,1536]{2,1,0:T(8,128)(2,1)S(1)}, u32[]{:S(2)}, u32[]{:S(2)}) collective-permute-start(bf16[2,48,1536]{2,1,0:T(8,128)(2,1)S(1)} %bitcast.212), channel_id=1, source_target_pairs={{0,2},{2,4},{4,6},{6,0},{1,3},{3,5},{5,7},{7,1},{8,10},{10,12},{12... | collective-permute-start | bytes 884744 | tf_op jit(solution)/shard_map/ppermute | solution.py:46
  152.8 22.2 %collective-permute-start.22 = (bf16[2,48,1536]{2,1,0:T(8,128)(2,1)S(1)}, bf16[2,48,1536]{2,1,0:T(8,128)(2,1)S(1)}, u32[]{:S(2)}, u32[]{:S(2)}) collective-permute-start(bf16[2,48,1536]{2,1,0:T(8,128)(2,1)S(1)} %bitcast.213), channel_id=1, source_target_pairs={{0,4},{2,6},{4,0},{6,2},{1,5},{3,7},{5,1},{7,3},{8,12},{10,14},{12... | collective-permute-start | bytes 884744 | tf_op jit(solution)/shard_map/ppermute | solution.py:46
  154.6 21.2 %collective-permute-start.23 = (bf16[2,48,1536]{2,1,0:T(8,128)(2,1)S(1)}, bf16[2,48,1536]{2,1,0:T(8,128)(2,1)S(1)}, u32[]{:S(2)}, u32[]{:S(2)}) collective-permute-start(bf16[2,48,1536]{2,1,0:T(8,128)(2,1)S(1)} %bitcast.214), channel_id=1, source_target_pairs={{0,6},{2,0},{4,2},{6,4},{1,7},{3,1},{5,3},{7,5},{8,14},{10,8},{12,... | collective-permute-start | bytes 884744 | tf_op jit(solution)/shard_map/ppermute | solution.py:46
  185.2 26.5 %all-to-all-start.1 = ((bf16[4,2,32,1664]{3,2,1,0:T(8,128)(2,1)}), bf16[4,2,32,1664]{3,2,1,0:T(8,128)(2,1)S(1)}, u32[]{:S(2)}, u32[]{:S(2)}) async-start(bf16[4,2,32,1664]{3,2,1,0:T(8,128)(2,1)} %get-tuple-element.945), calls=%async_computation.1 | async-start | bytes 1703936 | tf_op jit(solution)/shard_map/all_to_all | solution.py:960
  190.5 20.4 %collective-permute-start.24 = (bf16[4,48,1536]{2,1,0:T(8,128)(2,1)S(1)}, bf16[4,48,1536]{2,1,0:T(8,128)(2,1)S(1)}, u32[]{:S(2)}, u32[]{:S(2)}) collective-permute-start(bf16[4,48,1536]{2,1,0:T(8,128)(2,1)S(1)} %get-tuple-element.992.refs_0_), channel_id=1, source_target_pairs={{0,1},{1,0},{2,3},{3,2},{4,5},{5,4},{6,7},{7,6},{8,9},{9,8},{10,11... | collective-permute-start | bytes 1769480 | tf_op jit(solution)/shard_map/ppermute | solution.py:46
  192.0 19.7 %collective-permute-start.25 = (bf16[4,48,1536]{2,1,0:T(8,128)(2,1)S(1)}, bf16[4,48,1536]{2,1,0:T(8,128)(2,1)S(1)}, u32[]{:S(2)}, u32[]{:S(2)}) collective-permute-start(bf16[4,48,1536]{2,1,0:T(8,128)(2,1)S(1)} %get-tuple-element.994.refs_2_), channel_id=1, source_target_pairs={{0,16},{16,0},{1,17},{17,1},{2,18},{18,2},{3,19},{19,3},{4,20},{20... | collective-permute-start | bytes 1769480 | tf_op jit(solution)/shard_map/ppermute | solution.py:46
  218.9 25.9 %collective-permute-start.26 = (bf16[2,4,48,1536]{3,2,1,0:T(8,128)(2,1)S(1)}, bf16[2,4,48,1536]{3,2,1,0:T(8,128)(2,1)}, u32[]{:S(2)}, u32[]{:S(2)}) collective-permute-start(bf16[2,4,48,1536]{3,2,1,0:T(8,128)(2,1)S(1)} %get-tuple-element.1050.refs_0_), channel_id=1, source_target_pairs={{0,16},{16,0},{1,17},{17,1},{2,18},{18,2},{3,19},{19,3},{4,20},{20... | collective-permute-start | bytes 3538952 | tf_op jit(solution)/shard_map/ppermute | solution.py:46
  219.7 25.8 %collective-permute-start.27 = (bf16[2,4,48,1536]{3,2,1,0:T(8,128)(2,1)S(1)}, bf16[2,4,48,1536]{3,2,1,0:T(8,128)(2,1)}, u32[]{:S(2)}, u32[]{:S(2)}) collective-permute-start(bf16[2,4,48,1536]{3,2,1,0:T(8,128)(2,1)S(1)} %get-tuple-element.1052.refs_2_), channel_id=1, source_target_pairs={{0,1},{1,0},{2,3},{3,2},{4,5},{5,4},{6,7},{7,6},{8,9},{9,8},{10,11... | collective-permute-start | bytes 3538952 | tf_op jit(solution)/shard_map/ppermute | solution.py:46
  220.5 25.1 %all-to-all-start.2 = ((bf16[4,2,32,1536]{3,2,1,0:T(8,128)(2,1)}), bf16[4,2,32,1536]{3,2,1,0:T(8,128)(2,1)S(1)}, u32[]{:S(2)}, u32[]{:S(2)}) async-start(bf16[4,2,32,1536]{3,2,1,0:T(8,128)(2,1)} %get-tuple-element.1035), calls=%async_computation.2 | async-start | bytes 1572864 | tf_op jit(solution)/shard_map/all_to_all | solution.py:960
  292.1 36.5 %all-to-all-start.3 = ((bf16[4,2,32,1536]{3,2,1,0:T(8,128)(2,1)}), bf16[4,2,32,1536]{3,2,1,0:T(8,128)(2,1)S(1)}, u32[]{:S(2)}, u32[]{:S(2)}) async-start(bf16[4,2,32,1536]{3,2,1,0:T(8,128)(2,1)} %get-tuple-element.1111), calls=%async_computation.3 | async-start | bytes 1572864 | tf_op jit(solution)/shard_map/all_to_all | solution.py:960
  331.8 33.5 %collective-permute-start.29 = (bf16[4,2,48,1536]{3,2,1,0:T(8,128)(2,1)}, bf16[4,2,48,1536]{3,2,1,0:T(8,128)(2,1)S(1)}, u32[]{:S(2)}, u32[]{:S(2)}) collective-permute-start(bf16[4,2,48,1536]{3,2,1,0:T(8,128)(2,1)} %get-tuple-element.1174), channel_id=1, source_target_pairs={{0,16},{16,0},{1,17},{17,1},{2,18},{18,2},{3,19},{19,3},{4,20},{20... | collective-permute-start | bytes 3538952 | tf_op jit(solution)/shard_map/ppermute | solution.py:176
  332.9 32.4 %collective-permute-start.30 = (bf16[2,4,48,1536]{3,2,1,0:T(8,128)(2,1)}, bf16[2,4,48,1536]{3,2,1,0:T(8,128)(2,1)S(1)}, u32[]{:S(2)}, u32[]{:S(2)}) collective-permute-start(bf16[2,4,48,1536]{3,2,1,0:T(8,128)(2,1)} %get-tuple-element.1176), channel_id=1, source_target_pairs={{0,1},{1,0},{2,3},{3,2},{4,5},{5,4},{6,7},{7,6},{8,9},{9,8},{10,11... | collective-permute-start | bytes 3538952 | tf_op jit(solution)/shard_map/ppermute | solution.py:176
  334.4 30.9 %all-to-all-start.4 = ((bf16[4,2,32,1536]{3,2,1,0:T(8,128)(2,1)}), bf16[4,2,32,1536]{3,2,1,0:T(8,128)(2,1)S(1)}, u32[]{:S(2)}, u32[]{:S(2)}) async-start(bf16[4,2,32,1536]{3,2,1,0:T(8,128)(2,1)} %shard_map.228), calls=%async_computation.4 | async-start | bytes 1572864 | tf_op jit(solution)/shard_map/all_to_all | solution.py:960
  366.9 29.2 %collective-permute-start.33 = (f32[512,1536]{1,0:T(8,128)}, f32[512,1536]{1,0:T(8,128)S(1)}, u32[]{:S(2)}, u32[]{:S(2)}) collective-permute-start(f32[512,1536]{1,0:T(8,128)} %get-tuple-element.1211), channel_id=1, source_target_pairs={{0,8},{8,0},{1,9},{9,1},{2,10},{10,2},{3,11},{11,3},{4,12},{12,4},... | collective-permute-start | bytes 9437192 | tf_op jit(solution)/shard_map/ppermute | solution.py:67
  366.9 28.7 %collective-permute-start.31 = (bf16[4,2,48,1536]{3,2,1,0:T(8,128)(2,1)}, bf16[4,2,48,1536]{3,2,1,0:T(8,128)(2,1)}, u32[]{:S(2)}, u32[]{:S(2)}) collective-permute-start(bf16[4,2,48,1536]{3,2,1,0:T(8,128)(2,1)} %get-tuple-element.1205), channel_id=1, source_target_pairs={{0,16},{16,0},{1,17},{17,1},{2,18},{18,2},{3,19},{19,3},{4,20},{20... | collective-permute-start | bytes 3538952 | tf_op jit(solution)/shard_map/ppermute | solution.py:176
  367.8 28.4 %collective-permute-start.32 = (bf16[2,4,48,1536]{3,2,1,0:T(8,128)(2,1)}, bf16[2,4,48,1536]{3,2,1,0:T(8,128)(2,1)}, u32[]{:S(2)}, u32[]{:S(2)}) collective-permute-start(bf16[2,4,48,1536]{3,2,1,0:T(8,128)(2,1)} %get-tuple-element.1207), channel_id=1, source_target_pairs={{0,1},{1,0},{2,3},{3,2},{4,5},{5,4},{6,7},{7,6},{8,9},{9,8},{10,11... | collective-permute-start | bytes 3538952 | tf_op jit(solution)/shard_map/ppermute | solution.py:176
  408.0 42.9 %collective-permute-start.34 = (bf16[4,48,1536]{2,1,0:T(8,128)(2,1)}, bf16[4,48,1536]{2,1,0:T(8,128)(2,1)S(1)}, u32[]{:S(2)}, u32[]{:S(2)}) collective-permute-start(bf16[4,48,1536]{2,1,0:T(8,128)(2,1)} %get-tuple-element.1287), channel_id=1, source_target_pairs={{0,1},{1,0},{2,3},{3,2},{4,5},{5,4},{6,7},{7,6},{8,9},{9,8},{10,11... | collective-permute-start | bytes 1769480 | tf_op jit(solution)/shard_map/ppermute | solution.py:176
  408.6 42.3 %collective-permute-start.35 = (bf16[4,48,1536]{2,1,0:T(8,128)(2,1)}, bf16[4,48,1536]{2,1,0:T(8,128)(2,1)S(1)}, u32[]{:S(2)}, u32[]{:S(2)}) collective-permute-start(bf16[4,48,1536]{2,1,0:T(8,128)(2,1)} %get-tuple-element.1289), channel_id=1, source_target_pairs={{0,16},{16,0},{1,17},{17,1},{2,18},{18,2},{3,19},{19,3},{4,20},{20... | collective-permute-start | bytes 1769480 | tf_op jit(solution)/shard_map/ppermute | solution.py:176
  409.7 41.2 %collective-permute-start.36 = (bf16[4,48,1536]{2,1,0:T(8,128)(2,1)}, bf16[4,48,1536]{2,1,0:T(8,128)(2,1)}, u32[]{:S(2)}, u32[]{:S(2)}) collective-permute-start(bf16[4,48,1536]{2,1,0:T(8,128)(2,1)} %get-tuple-element.1293), channel_id=1, source_target_pairs={{0,1},{1,0},{2,3},{3,2},{4,5},{5,4},{6,7},{7,6},{8,9},{9,8},{10,11... | collective-permute-start | bytes 1769480 | tf_op jit(solution)/shard_map/ppermute | solution.py:176
  411.2 39.7 %collective-permute-start.37 = (bf16[4,48,1536]{2,1,0:T(8,128)(2,1)}, bf16[4,48,1536]{2,1,0:T(8,128)(2,1)}, u32[]{:S(2)}, u32[]{:S(2)}) collective-permute-start(bf16[4,48,1536]{2,1,0:T(8,128)(2,1)} %get-tuple-element.1295), channel_id=1, source_target_pairs={{0,16},{16,0},{1,17},{17,1},{2,18},{18,2},{3,19},{19,3},{4,20},{20... | collective-permute-start | bytes 1769480 | tf_op jit(solution)/shard_map/ppermute | solution.py:176
  457.8 25.1 %collective-permute-start.38 = (bf16[256,1536]{1,0:T(8,128)(2,1)S(1)}, bf16[256,1536]{1,0:T(8,128)(2,1)S(1)}, u32[]{:S(2)}, u32[]{:S(2)}) collective-permute-start(bf16[256,1536]{1,0:T(8,128)(2,1)S(1)} %get-tuple-element.1326), channel_id=1, source_target_pairs={{0,1},{1,0},{2,3},{3,2},{4,5},{5,4},{6,7},{7,6},{8,9},{9,8},{10,11... | collective-permute-start | bytes 2359304 | tf_op jit(solution)/shard_map/ppermute | solution.py:67
  458.4 22.6 %collective-permute-start.40 = (bf16[2,48,1536]{2,1,0:T(8,128)(2,1)}, bf16[2,48,1536]{2,1,0:T(8,128)(2,1)S(1)}, u32[]{:S(2)}, u32[]{:S(2)}) collective-permute-start(bf16[2,48,1536]{2,1,0:T(8,128)(2,1)} %get-tuple-element.1345), channel_id=1, source_target_pairs={{0,2},{2,4},{4,6},{6,0},{1,3},{3,5},{5,7},{7,1},{8,10},{10,12},{12... | collective-permute-start | bytes 884744 | tf_op jit(solution)/shard_map/ppermute | solution.py:176
  460.4 22.4 %collective-permute-start.41 = (bf16[2,48,1536]{2,1,0:T(8,128)(2,1)}, bf16[2,48,1536]{2,1,0:T(8,128)(2,1)S(1)}, u32[]{:S(2)}, u32[]{:S(2)}) collective-permute-start(bf16[2,48,1536]{2,1,0:T(8,128)(2,1)} %get-tuple-element.1346), channel_id=1, source_target_pairs={{0,4},{2,6},{4,0},{6,2},{1,5},{3,7},{5,1},{7,3},{8,12},{10,14},{12... | collective-permute-start | bytes 884744 | tf_op jit(solution)/shard_map/ppermute | solution.py:176
  462.8 20.1 %collective-permute-start.42 = (bf16[2,48,1536]{2,1,0:T(8,128)(2,1)}, bf16[2,48,1536]{2,1,0:T(8,128)(2,1)}, u32[]{:S(2)}, u32[]{:S(2)}) collective-permute-start(bf16[2,48,1536]{2,1,0:T(8,128)(2,1)} %get-tuple-element.1347), channel_id=1, source_target_pairs={{0,6},{2,0},{4,2},{6,4},{1,7},{3,1},{5,3},{7,5},{8,14},{10,8},{12,... | collective-permute-start | bytes 884744 | tf_op jit(solution)/shard_map/ppermute | solution.py:176
  485.7 32.3 %collective-permute-start.46 = (bf16[4,2,48,1792]{3,2,1,0:T(8,128)(2,1)}, bf16[4,2,48,1792]{3,2,1,0:T(8,128)(2,1)S(1)}, u32[]{:S(2)}, u32[]{:S(2)}) collective-permute-start(bf16[4,2,48,1792]{3,2,1,0:T(8,128)(2,1)} %get-tuple-element.1407), channel_id=1, source_target_pairs={{0,16},{16,0},{1,17},{17,1},{2,18},{18,2},{3,19},{19,3},{4,20},{20... | collective-permute-start | bytes 4128776 | tf_op jit(solution)/shard_map/ppermute | solution.py:176
  486.8 32.0 %collective-permute-start.47 = (bf16[2,4,48,1792]{3,2,1,0:T(8,128)(2,1)}, bf16[2,4,48,1792]{3,2,1,0:T(8,128)(2,1)S(1)}, u32[]{:S(2)}, u32[]{:S(2)}) collective-permute-start(bf16[2,4,48,1792]{3,2,1,0:T(8,128)(2,1)} %get-tuple-element.1409), channel_id=1, source_target_pairs={{0,1},{1,0},{2,3},{3,2},{4,5},{5,4},{6,7},{7,6},{8,9},{9,8},{10,11... | collective-permute-start | bytes 4128776 | tf_op jit(solution)/shard_map/ppermute | solution.py:176
  488.3 28.3 %collective-permute-start.43 = (bf16[2,48,1536]{2,1,0:T(8,128)(2,1)}, bf16[2,48,1536]{2,1,0:T(8,128)(2,1)}, u32[]{:S(2)}, u32[]{:S(2)}) collective-permute-start(bf16[2,48,1536]{2,1,0:T(8,128)(2,1)} %get-tuple-element.1397), channel_id=1, source_target_pairs={{0,2},{2,4},{4,6},{6,0},{1,3},{3,5},{5,7},{7,1},{8,10},{10,12},{12... | collective-permute-start | bytes 884744 | tf_op jit(solution)/shard_map/ppermute | solution.py:176
  495.2 21.5 %collective-permute-start.44 = (bf16[2,48,1536]{2,1,0:T(8,128)(2,1)}, bf16[2,48,1536]{2,1,0:T(8,128)(2,1)}, u32[]{:S(2)}, u32[]{:S(2)}) collective-permute-start(bf16[2,48,1536]{2,1,0:T(8,128)(2,1)} %get-tuple-element.1398), channel_id=1, source_target_pairs={{0,4},{2,6},{4,0},{6,2},{1,5},{3,7},{5,1},{7,3},{8,12},{10,14},{12... | collective-permute-start | bytes 884744 | tf_op jit(solution)/shard_map/ppermute | solution.py:176
  496.9 19.7 %collective-permute-start.45 = (bf16[2,48,1536]{2,1,0:T(8,128)(2,1)}, bf16[2,48,1536]{2,1,0:T(8,128)(2,1)}, u32[]{:S(2)}, u32[]{:S(2)}) collective-permute-start(bf16[2,48,1536]{2,1,0:T(8,128)(2,1)} %get-tuple-element.1399), channel_id=1, source_target_pairs={{0,6},{2,0},{4,2},{6,4},{1,7},{3,1},{5,3},{7,5},{8,14},{10,8},{12,... | collective-permute-start | bytes 884744 | tf_op jit(solution)/shard_map/ppermute | solution.py:176
  522.6 22.5 %collective-permute-start.50 = (f32[528,1536]{1,0:T(8,128)}, f32[528,1536]{1,0:T(8,128)S(1)}, u32[]{:S(2)}, u32[]{:S(2)}) collective-permute-start(f32[528,1536]{1,0:T(8,128)} %get-tuple-element.1437), channel_id=1, source_target_pairs={{0,8},{8,0},{1,9},{9,1},{2,10},{10,2},{3,11},{11,3},{4,12},{12,4},... | collective-permute-start | bytes 9732104 | tf_op jit(solution)/shard_map/ppermute | solution.py:67
  556.3 23.6 %collective-permute-start.54 = (bf16[2,48,1792]{2,1,0:T(8,128)(2,1)}, bf16[2,48,1792]{2,1,0:T(8,128)(2,1)S(1)}, u32[]{:S(2)}, u32[]{:S(2)}) collective-permute-start(bf16[2,48,1792]{2,1,0:T(8,128)(2,1)} %get-tuple-element.1499), channel_id=1, source_target_pairs={{0,4},{2,6},{4,0},{6,2},{1,5},{3,7},{5,1},{7,3},{8,12},{10,14},{12... | collective-permute-start | bytes 1032200 | tf_op jit(solution)/shard_map/ppermute | solution.py:176
  557.7 22.2 %collective-permute-start.55 = (bf16[2,48,1792]{2,1,0:T(8,128)(2,1)}, bf16[2,48,1792]{2,1,0:T(8,128)(2,1)S(1)}, u32[]{:S(2)}, u32[]{:S(2)}) collective-permute-start(bf16[2,48,1792]{2,1,0:T(8,128)(2,1)} %get-tuple-element.1500), channel_id=1, source_target_pairs={{0,6},{2,0},{4,2},{6,4},{1,7},{3,1},{5,3},{7,5},{8,14},{10,8},{12,... | collective-permute-start | bytes 1032200 | tf_op jit(solution)/shard_map/ppermute | solution.py:176
  580.8 23.8 %collective-permute-start.63 = (f32[48,1792]{1,0:T(8,128)}, f32[48,1792]{1,0:T(8,128)S(1)}, u32[]{:S(2)}, u32[]{:S(2)}) collective-permute-start(f32[48,1792]{1,0:T(8,128)} %get-tuple-element.1549), channel_id=1, source_target_pairs={{0,8},{8,0},{1,9},{9,1},{2,10},{10,2},{3,11},{11,3},{4,12},{12,4},... | collective-permute-start | bytes 1032200 | tf_op jit(solution)/shard_map/ppermute | solution.py:67
  581.7 19.7 %collective-permute-start.62 = (f32[48,1536]{1,0:T(8,128)}, f32[48,1536]{1,0:T(8,128)}, u32[]{:S(2)}, u32[]{:S(2)}) collective-permute-start(f32[48,1536]{1,0:T(8,128)} %get-tuple-element.1555), channel_id=1, source_target_pairs={{0,8},{8,0},{1,9},{9,1},{2,10},{10,2},{3,11},{11,3},{4,12},{12,4},... | collective-permute-start | bytes 884744 | tf_op jit(solution)/shard_map/ppermute | solution.py:67
  584.1 32.5 %collective-permute-start.56 = (bf16[256,1536]{1,0:T(8,128)(2,1)}, bf16[256,1536]{1,0:T(8,128)(2,1)}, u32[]{:S(2)}, u32[]{:S(2)}) collective-permute-start(bf16[256,1536]{1,0:T(8,128)(2,1)} %get-tuple-element.1517), channel_id=1, source_target_pairs={{0,1},{1,0},{2,3},{3,2},{4,5},{5,4},{6,7},{7,6},{8,9},{9,8},{10,11... | collective-permute-start | bytes 2359304 | tf_op jit(solution)/shard_map/ppermute | solution.py:67
  (105 other events, 748.8 us)

commit v4 on v3

--- a/solution.py
+++ b/solution.py
@@ -1222,16 +1222,12 @@
 
     live.d_proj, live.bc_mine, live.bc_theirs, live.g_taps, live.g_heads = d_proj, mine, theirs, g_taps, g_heads
     del live.x, live.bc, live.step, live.cum, live.d_ssm, live.taps, live.heads_par, live.dxs, live.d_bc, live.d_cum
-    live.block_out, live.stats = block_rows(bounds, live.own_in, live.mixer_own, live.mixer_part)
-    del live.d_step, live.state_in, live.local, live.back_in, live.back_local, live.mixer_own, live.mixer_part
+    del live.d_step, live.state_in, live.local, live.back_in, live.back_local
     settle(live)
 
     live.out_sums = cut_line(live.out_sums)
-    live.block_keep, live.block_send = by_slots(live.block_out)
-    del live.block_out
     settle(live)
     live.out_sums = move(live.out_sums, "z")
-    live.block_send = swapped(live.block_send, "y")
     mine, theirs, d_proj, proj, own_taps = (
         live.bc_mine, swapped(live.bc_theirs, "core"), live.d_proj, live.proj, live.own_taps
     )
@@ -1263,6 +1259,8 @@
     halo_own, halo_came = live.d_own[:HALO], live.d_came[:HALO]
     settle(live)
     live.scan_sums = move_second(live.scan_sums)
+    live.block_out, live.stats = block_rows(bounds, live.own_in, live.mixer_own, live.mixer_part)
+    del live.mixer_own, live.mixer_part
     live.back_own = lax.ppermute(halo_own, "z", [(i + 1, i) for i in range(nz - 1)])
     across = [(c * nz + i + 1, (1 - c) * nz + i) for c in range(2) for i in range(nz - 1)]
     live.back_came = lax.ppermute(halo_came, ("core", "z"), across)
@@ -1272,8 +1270,11 @@
     settle(live)
 
     live.scan_sums = cut_line(live.scan_sums)
+    live.block_keep, live.block_send = by_slots(live.block_out)
+    del live.block_out
     settle(live)
     live.scan_sums = move(live.scan_sums, "z")
+    live.block_send = swapped(live.block_send, "y")
     live.grad_in, live.g_gain_in = input_rows(
         bounds, live.own_in, live.own_grad, live.d_own, live.d_came, live.back_own, live.back_came, live.gain_in
     )

time: 628 us -> 624 us (level)
    unnamed x179 -> x175, local copies, waits for them, and re-layouts: 28.9 us -> 28.3 us
  transfers between devices with their start and end apart: 69 -> 69, of which waited for: 27 -> 25; matrix products, arithmetic and copies ran while one was open for 8% -> 9% of each run, Pallas kernels for 36% -> 36%
where the time goes in v4:
time: 624 us; the launch traced here: 615 us
  Pallas kernels  277 us (44%)
  starting transfers between devices  113 us (18%)
  waiting for transfers between devices  102 us (16%)
  local copies, waits for them, and re-layouts  68.5 us (11%)
  other arithmetic  51.9 us (8%)
    pallas_call x2, Pallas kernels, back_call(): call(functools.partial(back_kernel, len(kept)), (spans,), [one(EC), one(2...  51.4 us
    ppermute x21, waiting for transfers between devices, others(): lax.ppermute(piece, axis, route)  43.4 us
    ppermute x21, starting transfers between devices, move(): lax.ppermute(piece, axis, [(i, (i + step) % size) for i in range(size)])  35.3 us
    pallas_call x3, Pallas kernels, by_rows_of(): call(kernel, (slots,), [pl.BlockSpec(memory_space=pltpu.SMEM), pl.BlockSp...  35.1 us
    pallas_call x3, Pallas kernels, outer_cut(): call(kernel, (4,), [pl.BlockSpec(memory_space=pltpu.SMEM), pl.BlockSpec((...  34.5 us
    pallas_call x1, Pallas kernels, shards(): call(functools.partial(close_kernel, rows, nz), (2,), [whole_row(rows, EC...  33.8 us
    ppermute x21, starting transfers between devices, others(): lax.ppermute(piece, axis, route)  28.9 us
    unnamed x175, local copies, waits for them, and re-layouts  28.3 us
  transfers between devices with their start and end apart: 69, of which 25 were waited for; matrix products, arithmetic and copies ran while one was open for 9% of the time, Pallas kernels for 36%

profile of v4, /device:TPU:0, one launch (start us, length us, event | category | flops | bytes accessed | tf_op | source)
XLA Modules:
  0.0 615.1 jit_solution(10603469355667733170)
XLA Ops:
  2.2 4.0 dynamic-slice_reduce_fusion
  10.2 2.6 collective-permute-start.2
  16.3 2.6 collective-permute-start.4
  20.9 2.8 all-to-all-start
  23.7 8.0 %collective-permute-done.2 = bf16[256,1536]{1,0:T(8,128)(2,1)} collective-permute-done((bf16[256,1536]{1,0:T(8,128)(2,1)}, bf16[256,1536]{1,0:T(8,128)(2,1)}, u32[]{:S(2)}, u32[]{:S(2)}) %collective-permute-start.2) | collective-permute-done | bytes 786464 | tf_op jit(solution)/shard_map/ppermute | solution.py:67
  31.6 3.4 maximum_select_fusion.3
  35.0 13.6 %collective-permute-done.1 = bf16[256,1536]{1,0:T(8,128)(2,1)} collective-permute-done((bf16[256,1536]{1,0:T(8,128)(2,1)}, bf16[256,1536]{1,0:T(8,128)(2,1)}, u32[]{:S(2)}, u32[]{:S(2)}) %collective-permute-start.1) | collective-permute-done | bytes 786464 | tf_op jit(solution)/shard_map/ppermute | solution.py:67
  48.6 2.8 maximum_select_fusion.2
  53.9 2.5 shard_map.211
  57.5 2.6 collective-permute-start.6
  67.8 13.4 %collective-permute-done.10.refs_3_ = bf16[4,48,1920]{2,1,0:T(8,128)(2,1)S(1)} collective-permute-done((bf16[4,48,1920]{2,1,0:T(8,128)(2,1)S(1)}, bf16[4,48,1920]{2,1,0:T(8,128)(2,1)S(1)}, u32[]{:S(2)}, u32[]{:S(2)}) %collective-permute-start.10) | collective-permute-done | bytes 737312 | tf_op jit(solution)/shard_map/ppermute | solution.py:46
  91.0 3.2 collective-permute-start.13
  96.9 3.5 maximum_select_fusion
  103.4 8.2 %collective-permute-done.12.refs_2_ = bf16[2,48,1536]{2,1,0:T(8,128)(2,1)} collective-permute-done((bf16[2,48,1536]{2,1,0:T(8,128)(2,1)S(1)}, bf16[2,48,1536]{2,1,0:T(8,128)(2,1)}, u32[]{:S(2)}, u32[]{:S(2)}) %collective-permute-start.12) | collective-permute-done | bytes 294944 | tf_op jit(solution)/shard_map/ppermute | solution.py:46
  111.6 14.9 %collective-permute-done.14.refs_1_ = bf16[2,4,48,1920]{3,2,1,0:T(8,128)(2,1)} collective-permute-done((bf16[2,4,48,1920]{3,2,1,0:T(8,128)(2,1)S(1)}, bf16[2,4,48,1920]{3,2,1,0:T(8,128)(2,1)}, u32[]{:S(2)}, u32[]{:S(2)}) %collective-permute-start.14) | collective-permute-done | bytes 1474592 | tf_op jit(solution)/shard_map/ppermute | solution.py:46
  133.1 13.4 %shard_map.214 = (f32[2,528,1920]{2,1,0:T(8,128)}, bf16[2,2,4,2,48,1920]{5,4,3,2,1,0:T(8,128)(2,1)}) custom-call(s32[8]{0:T(128)} %stack.432.table_ref, bf16[2,528,1536]{2,1,0:T(8,128)(2,1)} %fusion.2.a_ref, bf16[2,4,48,1920]{3,2,1,0:T(8,128)(2,1)} %copy-done, bf16[2,4,48,1920]{3,2,1,0:T(8,128)(2,1)} %collective-permute-done.14.refs_1_, ...), custom_call_target="tpu_custom_call" | custom-call | bytes 1024 | tf_op jit(solution)/shard_map/pallas_call | solution.py:751
  156.9 15.3 %shard_map.216 = (f32[2,512,1536]{2,1,0:T(8,128)}, f32[2,512,256]{2,1,0:T(8,128)}, f32[2,512,128]{2,1,0:T(8,128)}, f32[2,512,128]{2,1,0:T(8,128)}, bf16[4,2,32,1...) custom-call(f32[2,528,1920]{2,1,0:T(8,128)} %get-tuple-element.1321.proj.proj_ref, ...), custom_call_target="tpu_custom_call" | custom-call | bytes 1024 | tf_op jit(solution)/shard_map/pallas_call | solution.py:1063
  185.3 5.3 all-to-all-start.1
  193.3 17.7 %shard_map.218.part_ref = f32[2,512,1536]{2,1,0:T(8,128)} custom-call(f32[2,512,1536]{2,1,0:T(8,128)} %get-tuple-element.1252.x_ref, f32[2,512,256]{2,1,0:T(8,128)} %get-tuple-element.1253.bc_ref, f32[2,512,128]{2,1,0:T(8,128)} %get-tuple-element.1254.step_ref, f32[2,512,128]{2,1,0:T(8,128)} %get-tuple-element.1255.cum_ref, f32[8,128]{1,0:T(8,128)} %stack.409.heads_par), custom_call_target="tpu_custom_call" | custom-call | bytes 1024 | tf_op jit(solution)/shard_map/pallas_call | solution.py:1089
  212.7 2.9 shard_map.219
  220.6 4.9 all-to-all-start.2
  226.1 2.5 pad_add_fusion.3
  229.3 10.9 %shard_map.221 = (f32[2,512,1536]{2,1,0:T(8,128)}, bf16[2,2,4,2,48,1536]{5,4,3,2,1,0:T(8,128)(2,1)}) custom-call(s32[8]{0:T(128)} %stack.457.table_ref, bf16[2,528,1536]{2,1,0:T(8,128)(2,1)} %fusion.2.a_ref, bf16[2,4,48,1536]{3,2,1,0:T(8,128)(2,1)} %copy-done.2, bf16[2,4,48,1536]{3,2,1,0:T(8,128)(2,1)} %collective-permute-done.19.refs_1_, ...), custom_call_target="tpu_custom_call" | custom-call | bytes 1024 | tf_op jit(solution)/shard_map/pallas_call | solution.py:751
  240.2 4.9 fusion.3.a_ref.b_ref
  247.0 10.9 %shard_map.222 = (f32[2,512,1536]{2,1,0:T(8,128)}, bf16[2,4,2,2,48,1536]{5,4,3,2,1,0:T(8,128)(2,1)}) custom-call(s32[8]{0:T(128)} %stack.462.table_ref, bf16[2,512,1536]{2,1,0:T(8,128)(2,1)} %fusion.3.a_ref.b_ref, bf16[2,4,48,1536]{3,2,1,0:T(8,128)(2,1)} %copy-done.4, bf16[2,4,48,1536]{3,2,1,0:T(8,128)(2,1)} %collective-permute-done.26.refs_1_, ...), custom_call_target="tpu_custom_call" | custom-call | bytes 1024 | tf_op jit(solution)/shard_map/pallas_call | solution.py:751
  258.5 12.2 %shard_map.223 = (f32[2,512,1536]{2,1,0:T(8,128)}, f32[2,512,128]{2,1,0:T(8,128)}) custom-call(f32[2,512,1536]{2,1,0:T(8,128)} %shard_map.218.part_ref, f32[2,512,256]{2,1,0:T(8,128)} %get-tuple-element.1253.bc_ref, f32[2,512,128]{2,1,0:T(8,128)} %get-tuple-element.1255.cum_ref, f32[2,2,8,128]{3,2,1,0:T(8,128)} %broadcast_in_dim.48.before_ref, ...), custom_call_target="tpu_custom_call" | custom-call | bytes 1024 | tf_op jit(solution)/shard_map/pallas_call | solution.py:1130
  274.8 17.2 %shard_map.224 = (bf16[2,512,1536]{2,1,0:T(8,128)(2,1)}, f32[2,512,1536]{2,1,0:T(8,128)}, bf16[2,512,1536]{2,1,0:T(8,128)(2,1)}, f32[8,1536]{1,0:T(8,128)}, bf16...) custom-call(f32[2,512,1536]{2,1,0:T(8,128)} %get-tuple-element.1050.y_ref, ...), custom_call_target="tpu_custom_call" | custom-call | bytes 1024 | tf_op jit(solution)/shard_map/pallas_call | solution.py:1143
  292.0 4.8 all-to-all-start.3
  297.5 10.5 %shard_map.227 = (bf16[4,2,48,1536]{3,2,1,0:T(8,128)(2,1)}, bf16[4,2,48,1536]{3,2,1,0:T(8,128)(2,1)}, bf16[2,4,48,1536]{3,2,1,0:T(8,128)(2,1)}, bf16[2,4,48,1536]{3,2,1,0:T(8,128)(2,1)}) custom-call(s32[2]{0:T(128)} %pad_add_fusion.4.place_ref, bf16[2,512,1536]{2,1,0:T(8,128)(2,1)} %get-tuple-element.1089.a_ref, bf16[2,512,1536]{2,1,0:T(8,128)(2,1)} %fusion.3.a_ref.b_ref), custom_call_target="tpu_custom_call" | custom-call | bytes 1024 | tf_op jit(solution)/shard_map/pallas_call | solution.py:693
  308.0 10.3 %shard_map.226 = (f32[512,1536]{1,0:T(8,128)}, f32[512,1536]{1,0:T(8,128)}) custom-call(s32[1]{0:T(128)} %bitcast.core_ref, bf16[2,512,1536]{2,1,0:T(8,128)(2,1)} %get-tuple-element.1089.a_ref, bf16[1536,1536]{1,0:T(8,128)(2,1)} %bitcast.226), custom_call_target="tpu_custom_call" | custom-call | bytes 1024 | tf_op jit(solution)/shard_map/pallas_call | solution.py:800
  318.3 10.6 %shard_map.225 = (bf16[4,2,48,1536]{3,2,1,0:T(8,128)(2,1)}, bf16[4,2,48,1536]{3,2,1,0:T(8,128)(2,1)}, bf16[2,4,48,1536]{3,2,1,0:T(8,128)(2,1)}, bf16[2,4,48,1536]{3,2,1,0:T(8,128)(2,1)}) custom-call(s32[2]{0:T(128)} %pad_add_fusion.4.place_ref, bf16[2,528,1536]{2,1,0:T(8,128)(2,1)} %fusion.2.a_ref, bf16[2,512,1536]{2,1,0:T(8,128)(2,1)} %get-tuple-element.1374.b_ref.dgate_ref), custom_call_target="tpu_custom_call" | custom-call | bytes 1024 | tf_op jit(solution)/shard_map/pallas_call | solution.py:693
  334.7 5.1 all-to-all-start.4
  339.8 25.8 %shard_map.229 = (f32[2,512,1536]{2,1,0:T(8,128)}, f32[2,512,256]{2,1,0:T(8,128)}, f32[2,512,128]{2,1,0:T(8,128)}, f32[2,512,128]{2,1,0:T(8,128)}) custom-call(f32[2,512,1536]{2,1,0:T(8,128)} %get-tuple-element.1252.x_ref, f32[2,512,256]{2,1,0:T(8,128)} %get-tuple-element.1253.bc_ref, f32[2,512,128]{2,1,0:T(8,128)} %get-tuple-element.1254.step_ref, ...), custom_call_target="tpu_custom_call" | custom-call | bytes 1024 | tf_op jit(solution)/shard_map/pallas_call | solution.py:1175
  368.6 25.6 %shard_map.230 = (f32[2,512,1536]{2,1,0:T(8,128)}, f32[2,512,256]{2,1,0:T(8,128)}, f32[2,512,128]{2,1,0:T(8,128)}, f32[2,512,128]{2,1,0:T(8,128)}) custom-call(f32[2,512,1536]{2,1,0:T(8,128)} %get-tuple-element.1252.x_ref, f32[2,512,256]{2,1,0:T(8,128)} %get-tuple-element.1253.bc_ref, ...), custom_call_target="tpu_custom_call", output_to_operand_aliasing={{0}: (8, {}), {1}: (9, {}), {2}: (10, {}), {3}: (11, {})} | custom-call | bytes 1024 | tf_op jit(solution)/shard_map/pallas_call | solution.py:1175
  396.5 3.1 add_convert_fusion.2
  412.3 33.8 %shard_map.231 = (bf16[2,528,1792]{2,1,0:T(8,128)(2,1)}, f32[2,512,128]{2,1,0:T(8,128)}, f32[2,512,128]{2,1,0:T(8,128)}, f32[2,8,1536]{2,1,0:T(8,128)}, f32[2,8,128]{2,1,0:T(8,128)}) custom-call(f32[2,512,1536]{2,1,0:T(8,128)} %get-tuple-element.1252.x_ref, f32[2,512,256]{2,1,0:T(8,128)} %get-tuple-element.1253.bc_ref, ...), custom_call_target="tpu_custom_call" | custom-call | bytes 1024 | tf_op jit(solution)/shard_map/pallas_call | solution.py:1209
  456.4 2.5 shard_map.232
  458.9 13.4 %shard_map.233 = (bf16[4,2,48,1792]{3,2,1,0:T(8,128)(2,1)}, bf16[4,2,48,1792]{3,2,1,0:T(8,128)(2,1)}, bf16[2,4,48,1792]{3,2,1,0:T(8,128)(2,1)}, bf16[2,4,48,1792]{3,2,1,0:T(8,128)(2,1)}) custom-call(s32[2]{0:T(128)} %pad_add_fusion.4.place_ref, bf16[2,528,1536]{2,1,0:T(8,128)(2,1)} %fusion.2.a_ref, bf16[2,528,1792]{2,1,0:T(8,128)(2,1)} %get-tuple-element.1373.b_ref.dproj_ref), custom_call_target="tpu_custom_call" | custom-call | bytes 1024 | tf_op jit(solution)/shard_map/pallas_call | solution.py:693
  477.8 6.7 %collective-permute-start.42 = (bf16[2,48,1536]{2,1,0:T(8,128)(2,1)}, bf16[2,48,1536]{2,1,0:T(8,128)(2,1)}, u32[]{:S(2)}, u32[]{:S(2)}) collective-permute-start(bf16[2,48,1536]{2,1,0:T(8,128)(2,1)} %get-tuple-element.1385), channel_id=1, source_target_pairs={{0,2},{2,4},{4,6},{6,0},{1,3},{3,5},{5,7},{7,1},{8,10},{10,12},{12... | collective-permute-start | bytes 884744 | tf_op jit(solution)/shard_map/ppermute | solution.py:176
  486.9 19.1 %shard_map.234 = (f32[528,1536]{1,0:T(8,128)}, f32[528,1536]{1,0:T(8,128)}) custom-call(s32[1]{0:T(128)} %bitcast.core_ref, bf16[2,528,1792]{2,1,0:T(8,128)(2,1)} %get-tuple-element.1373.b_ref.dproj_ref, bf16[2,512,1536]{2,1,0:T(8,128)(2,1)} %get-tuple-element.1374.b_ref.dgate_ref, bf16[1536,1920]{1,0:T(8,128)(2,1)} %bitcast.225, bf16[1536,1536]{1,0:T(8,128)(2,1)} %bitcast.227), custom_call_target="tpu_custom_call" | custom-call | bytes 1024 | tf_op jit(solution)/shard_map/pallas_call | solution.py:778
  524.4 4.9 shard_map.235
  531.3 3.1 collective-permute-done.50
  534.6 3.8 dynamic-slice_bitcast_fusion.1
  544.4 6.8 %collective-permute-start.53 = (bf16[2,48,1792]{2,1,0:T(8,128)(2,1)}, bf16[2,48,1792]{2,1,0:T(8,128)(2,1)S(1)}, u32[]{:S(2)}, u32[]{:S(2)}) collective-permute-start(bf16[2,48,1792]{2,1,0:T(8,128)(2,1)} %get-tuple-element.1486), channel_id=1, source_target_pairs={{0,2},{2,4},{4,6},{6,0},{1,3},{3,5},{5,7},{7,1},{8,10},{10,12},{12... | collective-permute-start | bytes 1032200 | tf_op jit(solution)/shard_map/ppermute | solution.py:176
  555.3 6.5 %shard_map.236 = (bf16[512,1536]{1,0:T(8,128)(2,1)}, f32[8,1536]{1,0:T(8,128)}) custom-call(s32[2]{0:T(128)} %get-tuple-element.1563.bounds_ref, bf16[512,1536]{1,0:T(8,128)(2,1)} %bitcast.220, bf16[512,1536]{1,0:T(8,128)(2,1)} %bitcast.224, f32[528,1536]{1,0:T(8,128)} %get-tuple-element.1472.own_ref, f32[528,1536]{1,0:T(8,128)} %copy-done.30, ...), custom_call_target="tpu_custom_call" | custom-call | bytes 1024 | tf_op jit(solution)/shard_map/pallas_call | solution.py:870
  561.7 12.8 %collective-permute-done.54 = bf16[2,48,1792]{2,1,0:T(8,128)(2,1)S(1)} collective-permute-done((bf16[2,48,1792]{2,1,0:T(8,128)(2,1)}, bf16[2,48,1792]{2,1,0:T(8,128)(2,1)S(1)}, u32[]{:S(2)}, u32[]{:S(2)}) %collective-permute-start.54) | collective-permute-done | bytes 344096 | tf_op jit(solution)/shard_map/ppermute | solution.py:176
  585.1 7.8 %collective-permute-start.59 = (f32[168,128]{1,0:T(8,128)S(1)}, f32[168,128]{1,0:T(8,128)S(1)}, u32[]{:S(2)}, u32[]{:S(2)}) collective-permute-start(f32[168,128]{1,0:T(8,128)S(1)} %fusion.48), channel_id=1, source_target_pairs={{0,2},{2,0},{4,6},{6,4},{1,3},{3,1},{5,7},{7,5},{8,10},{10,8},{12,... | collective-permute-start | bytes 258056 | tf_op jit(solution)/shard_map/ppermute | solution.py:217
  612.1 2.8 maximum_select_fusion.5
  (482 shorter events, 186.2 us)
Async XLA Ops:
  10.2 21.4 %collective-permute-start.2 = (bf16[256,1536]{1,0:T(8,128)(2,1)}, bf16[256,1536]{1,0:T(8,128)(2,1)}, u32[]{:S(2)}, u32[]{:S(2)}) collective-permute-start(bf16[256,1536]{1,0:T(8,128)(2,1)} %get-tuple-element.1509), channel_id=1, source_target_pairs={{0,1},{1,0},{2,3},{3,2},{4,5},{5,4},{6,7},{7,6},{8,9},{9,8},{10,11... | collective-permute-start | bytes 2359304 | tf_op jit(solution)/shard_map/ppermute | solution.py:67
  13.8 34.8 %collective-permute-start.1 = (bf16[256,1536]{1,0:T(8,128)(2,1)}, bf16[256,1536]{1,0:T(8,128)(2,1)}, u32[]{:S(2)}, u32[]{:S(2)}) collective-permute-start(bf16[256,1536]{1,0:T(8,128)(2,1)} %get-tuple-element.1511), channel_id=1, source_target_pairs={{0,1},{1,0},{2,3},{3,2},{4,5},{5,4},{6,7},{7,6},{8,9},{9,8},{10,11... | collective-permute-start | bytes 2359304 | tf_op jit(solution)/shard_map/ppermute | solution.py:67
  14.6 39.1 %collective-permute-start.3 = (bf16[2,48,1920]{2,1,0:T(8,128)(2,1)S(1)}, bf16[2,48,1920]{2,1,0:T(8,128)(2,1)S(1)}, u32[]{:S(2)}, u32[]{:S(2)}) collective-permute-start(bf16[2,48,1920]{2,1,0:T(8,128)(2,1)S(1)} %slice.180.refs_0_), channel_id=1, source_target_pairs={{0,2},{2,4},{4,6},{6,0},{1,3},{3,5},{5,7},{7,1},{8,10},{10,12},{12... | collective-permute-start | bytes 1105928 | tf_op jit(solution)/shard_map/ppermute | solution.py:46
  16.3 37.5 %collective-permute-start.4 = (bf16[2,48,1920]{2,1,0:T(8,128)(2,1)S(1)}, bf16[2,48,1920]{2,1,0:T(8,128)(2,1)S(1)}, u32[]{:S(2)}, u32[]{:S(2)}) collective-permute-start(bf16[2,48,1920]{2,1,0:T(8,128)(2,1)S(1)} %slice.180.refs_0_), channel_id=1, source_target_pairs={{0,4},{2,6},{4,0},{6,2},{1,5},{3,7},{5,1},{7,3},{8,12},{10,14},{12... | collective-permute-start | bytes 1105928 | tf_op jit(solution)/shard_map/ppermute | solution.py:46
  18.8 34.9 %collective-permute-start.5 = (bf16[2,48,1920]{2,1,0:T(8,128)(2,1)S(1)}, bf16[2,48,1920]{2,1,0:T(8,128)(2,1)S(1)}, u32[]{:S(2)}, u32[]{:S(2)}) collective-permute-start(bf16[2,48,1920]{2,1,0:T(8,128)(2,1)S(1)} %slice.180.refs_0_), channel_id=1, source_target_pairs={{0,6},{2,0},{4,2},{6,4},{1,7},{3,1},{5,3},{7,5},{8,14},{10,8},{12,... | collective-permute-start | bytes 1105928 | tf_op jit(solution)/shard_map/ppermute | solution.py:46
  20.9 32.9 %all-to-all-start = ((bf16[32,8,128]{2,1,0:T(8,128)(2,1)}), bf16[32,8,128]{2,1,0:T(8,128)(2,1)S(1)}, u32[]{:S(2)}, u32[]{:S(2)}) async-start(bf16[32,8,128]{2,1,0:T(8,128)(2,1)} %broadcast_in_dim.42), calls=%async_computation | async-start | bytes 131072 | tf_op jit(solution)/shard_map/all_to_all | solution.py:58
  56.6 26.7 %collective-permute-start.8 = (bf16[512,1536]{1,0:T(8,128)(2,1)}, bf16[512,1536]{1,0:T(8,128)(2,1)}, u32[]{:S(2)}, u32[]{:S(2)}) collective-permute-start(bf16[512,1536]{1,0:T(8,128)(2,1)} %bitcast.216), channel_id=1, source_target_pairs={{0,8},{8,0},{1,9},{9,1},{2,10},{10,2},{3,11},{11,3},{4,12},{12,4},... | collective-permute-start | bytes 4718600 | tf_op jit(solution)/shard_map/ppermute | solution.py:67
  91.0 20.6 %collective-permute-start.12 = (bf16[2,48,1536]{2,1,0:T(8,128)(2,1)S(1)}, bf16[2,48,1536]{2,1,0:T(8,128)(2,1)}, u32[]{:S(2)}, u32[]{:S(2)}) collective-permute-start(bf16[2,48,1536]{2,1,0:T(8,128)(2,1)S(1)} %slice.179.refs_0_), channel_id=1, source_target_pairs={{0,4},{2,6},{4,0},{6,2},{1,5},{3,7},{5,1},{7,3},{8,12},{10,14},{12... | collective-permute-start | bytes 884744 | tf_op jit(solution)/shard_map/ppermute | solution.py:46
  91.0 20.6 %collective-permute-start.13 = (bf16[2,48,1536]{2,1,0:T(8,128)(2,1)S(1)}, bf16[2,48,1536]{2,1,0:T(8,128)(2,1)}, u32[]{:S(2)}, u32[]{:S(2)}) collective-permute-start(bf16[2,48,1536]{2,1,0:T(8,128)(2,1)S(1)} %slice.179.refs_0_), channel_id=1, source_target_pairs={{0,6},{2,0},{4,2},{6,4},{1,7},{3,1},{5,3},{7,5},{8,14},{10,8},{12,... | collective-permute-start | bytes 884744 | tf_op jit(solution)/shard_map/ppermute | solution.py:46
  94.1 32.4 %collective-permute-start.14 = (bf16[2,4,48,1920]{3,2,1,0:T(8,128)(2,1)S(1)}, bf16[2,4,48,1920]{3,2,1,0:T(8,128)(2,1)}, u32[]{:S(2)}, u32[]{:S(2)}) collective-permute-start(bf16[2,4,48,1920]{3,2,1,0:T(8,128)(2,1)S(1)} %get-tuple-element.854.refs_0_), channel_id=1, source_target_pairs={{0,16},{16,0},{1,17},{17,1},{2,18},{18,2},{3,19},{19,3},{4,20},{20... | collective-permute-start | bytes 4423688 | tf_op jit(solution)/shard_map/ppermute | solution.py:46
  94.7 32.2 %collective-permute-start.15 = (bf16[2,4,48,1920]{3,2,1,0:T(8,128)(2,1)S(1)}, bf16[2,4,48,1920]{3,2,1,0:T(8,128)(2,1)}, u32[]{:S(2)}, u32[]{:S(2)}) collective-permute-start(bf16[2,4,48,1920]{3,2,1,0:T(8,128)(2,1)S(1)} %get-tuple-element.856.refs_2_), channel_id=1, source_target_pairs={{0,1},{1,0},{2,3},{3,2},{4,5},{5,4},{6,7},{7,6},{8,9},{9,8},{10,11... | collective-permute-start | bytes 4423688 | tf_op jit(solution)/shard_map/ppermute | solution.py:46
  150.7 27.9 %collective-permute-start.19 = (bf16[2,4,48,1536]{3,2,1,0:T(8,128)(2,1)S(1)}, bf16[2,4,48,1536]{3,2,1,0:T(8,128)(2,1)}, u32[]{:S(2)}, u32[]{:S(2)}) collective-permute-start(bf16[2,4,48,1536]{3,2,1,0:T(8,128)(2,1)S(1)} %get-tuple-element.1014.refs_0_), channel_id=1, source_target_pairs={{0,16},{16,0},{1,17},{17,1},{2,18},{18,2},{3,19},{19,3},{4,20},{20... | collective-permute-start | bytes 3538952 | tf_op jit(solution)/shard_map/ppermute | solution.py:46
  152.1 27.0 %collective-permute-start.20 = (bf16[2,4,48,1536]{3,2,1,0:T(8,128)(2,1)S(1)}, bf16[2,4,48,1536]{3,2,1,0:T(8,128)(2,1)}, u32[]{:S(2)}, u32[]{:S(2)}) collective-permute-start(bf16[2,4,48,1536]{3,2,1,0:T(8,128)(2,1)S(1)} %get-tuple-element.1016.refs_2_), channel_id=1, source_target_pairs={{0,1},{1,0},{2,3},{3,2},{4,5},{5,4},{6,7},{7,6},{8,9},{9,8},{10,11... | collective-permute-start | bytes 3538952 | tf_op jit(solution)/shard_map/ppermute | solution.py:46
  152.6 19.5 %collective-permute-start.21 = (bf16[2,48,1536]{2,1,0:T(8,128)(2,1)S(1)}, bf16[2,48,1536]{2,1,0:T(8,128)(2,1)S(1)}, u32[]{:S(2)}, u32[]{:S(2)}) collective-permute-start(bf16[2,48,1536]{2,1,0:T(8,128)(2,1)S(1)} %bitcast.212), channel_id=1, source_target_pairs={{0,2},{2,4},{4,6},{6,0},{1,3},{3,5},{5,7},{7,1},{8,10},{10,12},{12... | collective-permute-start | bytes 884744 | tf_op jit(solution)/shard_map/ppermute | solution.py:46
  152.8 22.2 %collective-permute-start.22 = (bf16[2,48,1536]{2,1,0:T(8,128)(2,1)S(1)}, bf16[2,48,1536]{2,1,0:T(8,128)(2,1)S(1)}, u32[]{:S(2)}, u32[]{:S(2)}) collective-permute-start(bf16[2,48,1536]{2,1,0:T(8,128)(2,1)S(1)} %bitcast.213), channel_id=1, source_target_pairs={{0,4},{2,6},{4,0},{6,2},{1,5},{3,7},{5,1},{7,3},{8,12},{10,14},{12... | collective-permute-start | bytes 884744 | tf_op jit(solution)/shard_map/ppermute | solution.py:46
  154.6 21.2 %collective-permute-start.23 = (bf16[2,48,1536]{2,1,0:T(8,128)(2,1)S(1)}, bf16[2,48,1536]{2,1,0:T(8,128)(2,1)S(1)}, u32[]{:S(2)}, u32[]{:S(2)}) collective-permute-start(bf16[2,48,1536]{2,1,0:T(8,128)(2,1)S(1)} %bitcast.214), channel_id=1, source_target_pairs={{0,6},{2,0},{4,2},{6,4},{1,7},{3,1},{5,3},{7,5},{8,14},{10,8},{12,... | collective-permute-start | bytes 884744 | tf_op jit(solution)/shard_map/ppermute | solution.py:46
  185.3 26.5 %all-to-all-start.1 = ((bf16[4,2,32,1664]{3,2,1,0:T(8,128)(2,1)}), bf16[4,2,32,1664]{3,2,1,0:T(8,128)(2,1)S(1)}, u32[]{:S(2)}, u32[]{:S(2)}) async-start(bf16[4,2,32,1664]{3,2,1,0:T(8,128)(2,1)} %get-tuple-element.939), calls=%async_computation.1 | async-start | bytes 1703936 | tf_op jit(solution)/shard_map/all_to_all | solution.py:960
  190.6 20.4 %collective-permute-start.24 = (bf16[4,48,1536]{2,1,0:T(8,128)(2,1)S(1)}, bf16[4,48,1536]{2,1,0:T(8,128)(2,1)S(1)}, u32[]{:S(2)}, u32[]{:S(2)}) collective-permute-start(bf16[4,48,1536]{2,1,0:T(8,128)(2,1)S(1)} %get-tuple-element.986.refs_0_), channel_id=1, source_target_pairs={{0,1},{1,0},{2,3},{3,2},{4,5},{5,4},{6,7},{7,6},{8,9},{9,8},{10,11... | collective-permute-start | bytes 1769480 | tf_op jit(solution)/shard_map/ppermute | solution.py:46
  192.1 19.7 %collective-permute-start.25 = (bf16[4,48,1536]{2,1,0:T(8,128)(2,1)S(1)}, bf16[4,48,1536]{2,1,0:T(8,128)(2,1)S(1)}, u32[]{:S(2)}, u32[]{:S(2)}) collective-permute-start(bf16[4,48,1536]{2,1,0:T(8,128)(2,1)S(1)} %get-tuple-element.988.refs_2_), channel_id=1, source_target_pairs={{0,16},{16,0},{1,17},{17,1},{2,18},{18,2},{3,19},{19,3},{4,20},{20... | collective-permute-start | bytes 1769480 | tf_op jit(solution)/shard_map/ppermute | solution.py:46
  218.9 26.2 %collective-permute-start.26 = (bf16[2,4,48,1536]{3,2,1,0:T(8,128)(2,1)S(1)}, bf16[2,4,48,1536]{3,2,1,0:T(8,128)(2,1)}, u32[]{:S(2)}, u32[]{:S(2)}) collective-permute-start(bf16[2,4,48,1536]{3,2,1,0:T(8,128)(2,1)S(1)} %get-tuple-element.1044.refs_0_), channel_id=1, source_target_pairs={{0,16},{16,0},{1,17},{17,1},{2,18},{18,2},{3,19},{19,3},{4,20},{20... | collective-permute-start | bytes 3538952 | tf_op jit(solution)/shard_map/ppermute | solution.py:46
  219.8 25.8 %collective-permute-start.27 = (bf16[2,4,48,1536]{3,2,1,0:T(8,128)(2,1)S(1)}, bf16[2,4,48,1536]{3,2,1,0:T(8,128)(2,1)}, u32[]{:S(2)}, u32[]{:S(2)}) collective-permute-start(bf16[2,4,48,1536]{3,2,1,0:T(8,128)(2,1)S(1)} %get-tuple-element.1046.refs_2_), channel_id=1, source_target_pairs={{0,1},{1,0},{2,3},{3,2},{4,5},{5,4},{6,7},{7,6},{8,9},{9,8},{10,11... | collective-permute-start | bytes 3538952 | tf_op jit(solution)/shard_map/ppermute | solution.py:46
  220.6 25.1 %all-to-all-start.2 = ((bf16[4,2,32,1536]{3,2,1,0:T(8,128)(2,1)}), bf16[4,2,32,1536]{3,2,1,0:T(8,128)(2,1)S(1)}, u32[]{:S(2)}, u32[]{:S(2)}) async-start(bf16[4,2,32,1536]{3,2,1,0:T(8,128)(2,1)} %get-tuple-element.1029), calls=%async_computation.2 | async-start | bytes 1572864 | tf_op jit(solution)/shard_map/all_to_all | solution.py:960
  292.0 36.8 %all-to-all-start.3 = ((bf16[4,2,32,1536]{3,2,1,0:T(8,128)(2,1)}), bf16[4,2,32,1536]{3,2,1,0:T(8,128)(2,1)S(1)}, u32[]{:S(2)}, u32[]{:S(2)}) async-start(bf16[4,2,32,1536]{3,2,1,0:T(8,128)(2,1)} %get-tuple-element.1105), calls=%async_computation.3 | async-start | bytes 1572864 | tf_op jit(solution)/shard_map/all_to_all | solution.py:960
  332.1 33.5 %collective-permute-start.29 = (bf16[4,2,48,1536]{3,2,1,0:T(8,128)(2,1)}, bf16[4,2,48,1536]{3,2,1,0:T(8,128)(2,1)S(1)}, u32[]{:S(2)}, u32[]{:S(2)}) collective-permute-start(bf16[4,2,48,1536]{3,2,1,0:T(8,128)(2,1)} %get-tuple-element.1168), channel_id=1, source_target_pairs={{0,16},{16,0},{1,17},{17,1},{2,18},{18,2},{3,19},{19,3},{4,20},{20... | collective-permute-start | bytes 3538952 | tf_op jit(solution)/shard_map/ppermute | solution.py:176
  333.2 32.4 %collective-permute-start.30 = (bf16[2,4,48,1536]{3,2,1,0:T(8,128)(2,1)}, bf16[2,4,48,1536]{3,2,1,0:T(8,128)(2,1)S(1)}, u32[]{:S(2)}, u32[]{:S(2)}) collective-permute-start(bf16[2,4,48,1536]{3,2,1,0:T(8,128)(2,1)} %get-tuple-element.1170), channel_id=1, source_target_pairs={{0,1},{1,0},{2,3},{3,2},{4,5},{5,4},{6,7},{7,6},{8,9},{9,8},{10,11... | collective-permute-start | bytes 3538952 | tf_op jit(solution)/shard_map/ppermute | solution.py:176
  334.7 30.9 %all-to-all-start.4 = ((bf16[4,2,32,1536]{3,2,1,0:T(8,128)(2,1)}), bf16[4,2,32,1536]{3,2,1,0:T(8,128)(2,1)S(1)}, u32[]{:S(2)}, u32[]{:S(2)}) async-start(bf16[4,2,32,1536]{3,2,1,0:T(8,128)(2,1)} %shard_map.228), calls=%async_computation.4 | async-start | bytes 1572864 | tf_op jit(solution)/shard_map/all_to_all | solution.py:960
  367.2 29.2 %collective-permute-start.33 = (f32[512,1536]{1,0:T(8,128)}, f32[512,1536]{1,0:T(8,128)S(1)}, u32[]{:S(2)}, u32[]{:S(2)}) collective-permute-start(f32[512,1536]{1,0:T(8,128)} %get-tuple-element.1205), channel_id=1, source_target_pairs={{0,8},{8,0},{1,9},{9,1},{2,10},{10,2},{3,11},{11,3},{4,12},{12,4},... | collective-permute-start | bytes 9437192 | tf_op jit(solution)/shard_map/ppermute | solution.py:67
  367.2 28.7 %collective-permute-start.31 = (bf16[4,2,48,1536]{3,2,1,0:T(8,128)(2,1)}, bf16[4,2,48,1536]{3,2,1,0:T(8,128)(2,1)}, u32[]{:S(2)}, u32[]{:S(2)}) collective-permute-start(bf16[4,2,48,1536]{3,2,1,0:T(8,128)(2,1)} %get-tuple-element.1199), channel_id=1, source_target_pairs={{0,16},{16,0},{1,17},{17,1},{2,18},{18,2},{3,19},{19,3},{4,20},{20... | collective-permute-start | bytes 3538952 | tf_op jit(solution)/shard_map/ppermute | solution.py:176
  368.0 28.4 %collective-permute-start.32 = (bf16[2,4,48,1536]{3,2,1,0:T(8,128)(2,1)}, bf16[2,4,48,1536]{3,2,1,0:T(8,128)(2,1)}, u32[]{:S(2)}, u32[]{:S(2)}) collective-permute-start(bf16[2,4,48,1536]{3,2,1,0:T(8,128)(2,1)} %get-tuple-element.1201), channel_id=1, source_target_pairs={{0,1},{1,0},{2,3},{3,2},{4,5},{5,4},{6,7},{7,6},{8,9},{9,8},{10,11... | collective-permute-start | bytes 3538952 | tf_op jit(solution)/shard_map/ppermute | solution.py:176
  408.2 37.8 %collective-permute-start.34 = (bf16[4,48,1536]{2,1,0:T(8,128)(2,1)}, bf16[4,48,1536]{2,1,0:T(8,128)(2,1)S(1)}, u32[]{:S(2)}, u32[]{:S(2)}) collective-permute-start(bf16[4,48,1536]{2,1,0:T(8,128)(2,1)} %get-tuple-element.1277), channel_id=1, source_target_pairs={{0,1},{1,0},{2,3},{3,2},{4,5},{5,4},{6,7},{7,6},{8,9},{9,8},{10,11... | collective-permute-start | bytes 1769480 | tf_op jit(solution)/shard_map/ppermute | solution.py:176
  408.8 37.2 %collective-permute-start.35 = (bf16[4,48,1536]{2,1,0:T(8,128)(2,1)}, bf16[4,48,1536]{2,1,0:T(8,128)(2,1)S(1)}, u32[]{:S(2)}, u32[]{:S(2)}) collective-permute-start(bf16[4,48,1536]{2,1,0:T(8,128)(2,1)} %get-tuple-element.1279), channel_id=1, source_target_pairs={{0,16},{16,0},{1,17},{17,1},{2,18},{18,2},{3,19},{19,3},{4,20},{20... | collective-permute-start | bytes 1769480 | tf_op jit(solution)/shard_map/ppermute | solution.py:176
  409.9 36.1 %collective-permute-start.36 = (bf16[4,48,1536]{2,1,0:T(8,128)(2,1)}, bf16[4,48,1536]{2,1,0:T(8,128)(2,1)}, u32[]{:S(2)}, u32[]{:S(2)}) collective-permute-start(bf16[4,48,1536]{2,1,0:T(8,128)(2,1)} %get-tuple-element.1285), channel_id=1, source_target_pairs={{0,1},{1,0},{2,3},{3,2},{4,5},{5,4},{6,7},{7,6},{8,9},{9,8},{10,11... | collective-permute-start | bytes 1769480 | tf_op jit(solution)/shard_map/ppermute | solution.py:176
  411.5 34.6 %collective-permute-start.37 = (bf16[4,48,1536]{2,1,0:T(8,128)(2,1)}, bf16[4,48,1536]{2,1,0:T(8,128)(2,1)}, u32[]{:S(2)}, u32[]{:S(2)}) collective-permute-start(bf16[4,48,1536]{2,1,0:T(8,128)(2,1)} %get-tuple-element.1287), channel_id=1, source_target_pairs={{0,16},{16,0},{1,17},{17,1},{2,18},{18,2},{3,19},{19,3},{4,20},{20... | collective-permute-start | bytes 1769480 | tf_op jit(solution)/shard_map/ppermute | solution.py:176
  449.7 22.6 %collective-permute-start.39 = (bf16[2,48,1536]{2,1,0:T(8,128)(2,1)}, bf16[2,48,1536]{2,1,0:T(8,128)(2,1)S(1)}, u32[]{:S(2)}, u32[]{:S(2)}) collective-permute-start(bf16[2,48,1536]{2,1,0:T(8,128)(2,1)} %get-tuple-element.1337), channel_id=1, source_target_pairs={{0,2},{2,4},{4,6},{6,0},{1,3},{3,5},{5,7},{7,1},{8,10},{10,12},{12... | collective-permute-start | bytes 884744 | tf_op jit(solution)/shard_map/ppermute | solution.py:176
  451.8 22.4 %collective-permute-start.40 = (bf16[2,48,1536]{2,1,0:T(8,128)(2,1)}, bf16[2,48,1536]{2,1,0:T(8,128)(2,1)S(1)}, u32[]{:S(2)}, u32[]{:S(2)}) collective-permute-start(bf16[2,48,1536]{2,1,0:T(8,128)(2,1)} %get-tuple-element.1338), channel_id=1, source_target_pairs={{0,4},{2,6},{4,0},{6,2},{1,5},{3,7},{5,1},{7,3},{8,12},{10,14},{12... | collective-permute-start | bytes 884744 | tf_op jit(solution)/shard_map/ppermute | solution.py:176
  454.1 20.1 %collective-permute-start.41 = (bf16[2,48,1536]{2,1,0:T(8,128)(2,1)S(1)}, bf16[2,48,1536]{2,1,0:T(8,128)(2,1)S(1)}, u32[]{:S(2)}, u32[]{:S(2)}) collective-permute-start(bf16[2,48,1536]{2,1,0:T(8,128)(2,1)S(1)} %get-tuple-element.1339), channel_id=1, source_target_pairs={{0,6},{2,0},{4,2},{6,4},{1,7},{3,1},{5,3},{7,5},{8,14},{10,8},{12,... | collective-permute-start | bytes 884744 | tf_op jit(solution)/shard_map/ppermute | solution.py:176
  476.1 32.3 %collective-permute-start.45 = (bf16[4,2,48,1792]{3,2,1,0:T(8,128)(2,1)}, bf16[4,2,48,1792]{3,2,1,0:T(8,128)(2,1)S(1)}, u32[]{:S(2)}, u32[]{:S(2)}) collective-permute-start(bf16[4,2,48,1792]{3,2,1,0:T(8,128)(2,1)} %get-tuple-element.1397), channel_id=1, source_target_pairs={{0,16},{16,0},{1,17},{17,1},{2,18},{18,2},{3,19},{19,3},{4,20},{20... | collective-permute-start | bytes 4128776 | tf_op jit(solution)/shard_map/ppermute | solution.py:176
  477.3 32.0 %collective-permute-start.46 = (bf16[2,4,48,1792]{3,2,1,0:T(8,128)(2,1)}, bf16[2,4,48,1792]{3,2,1,0:T(8,128)(2,1)S(1)}, u32[]{:S(2)}, u32[]{:S(2)}) collective-permute-start(bf16[2,4,48,1792]{3,2,1,0:T(8,128)(2,1)} %get-tuple-element.1399), channel_id=1, source_target_pairs={{0,1},{1,0},{2,3},{3,2},{4,5},{5,4},{6,7},{7,6},{8,9},{9,8},{10,11... | collective-permute-start | bytes 4128776 | tf_op jit(solution)/shard_map/ppermute | solution.py:176
  477.8 28.1 %collective-permute-start.42 = (bf16[2,48,1536]{2,1,0:T(8,128)(2,1)}, bf16[2,48,1536]{2,1,0:T(8,128)(2,1)}, u32[]{:S(2)}, u32[]{:S(2)}) collective-permute-start(bf16[2,48,1536]{2,1,0:T(8,128)(2,1)} %get-tuple-element.1385), channel_id=1, source_target_pairs={{0,2},{2,4},{4,6},{6,0},{1,3},{3,5},{5,7},{7,1},{8,10},{10,12},{12... | collective-permute-start | bytes 884744 | tf_op jit(solution)/shard_map/ppermute | solution.py:176
  484.5 21.5 %collective-permute-start.43 = (bf16[2,48,1536]{2,1,0:T(8,128)(2,1)}, bf16[2,48,1536]{2,1,0:T(8,128)(2,1)}, u32[]{:S(2)}, u32[]{:S(2)}) collective-permute-start(bf16[2,48,1536]{2,1,0:T(8,128)(2,1)} %get-tuple-element.1386), channel_id=1, source_target_pairs={{0,4},{2,6},{4,0},{6,2},{1,5},{3,7},{5,1},{7,3},{8,12},{10,14},{12... | collective-permute-start | bytes 884744 | tf_op jit(solution)/shard_map/ppermute | solution.py:176
  486.3 19.6 %collective-permute-start.44 = (bf16[2,48,1536]{2,1,0:T(8,128)(2,1)}, bf16[2,48,1536]{2,1,0:T(8,128)(2,1)}, u32[]{:S(2)}, u32[]{:S(2)}) collective-permute-start(bf16[2,48,1536]{2,1,0:T(8,128)(2,1)} %get-tuple-element.1387), channel_id=1, source_target_pairs={{0,6},{2,0},{4,2},{6,4},{1,7},{3,1},{5,3},{7,5},{8,14},{10,8},{12,... | collective-permute-start | bytes 884744 | tf_op jit(solution)/shard_map/ppermute | solution.py:176
  513.0 21.5 %collective-permute-start.49 = (f32[528,1536]{1,0:T(8,128)}, f32[528,1536]{1,0:T(8,128)S(1)}, u32[]{:S(2)}, u32[]{:S(2)}) collective-permute-start(f32[528,1536]{1,0:T(8,128)} %get-tuple-element.1427), channel_id=1, source_target_pairs={{0,8},{8,0},{1,9},{9,1},{2,10},{10,2},{3,11},{11,3},{4,12},{12,4},... | collective-permute-start | bytes 9732104 | tf_op jit(solution)/shard_map/ppermute | solution.py:67
  542.8 31.7 %collective-permute-start.52 = (bf16[256,1536]{1,0:T(8,128)(2,1)}, bf16[256,1536]{1,0:T(8,128)(2,1)S(1)}, u32[]{:S(2)}, u32[]{:S(2)}) collective-permute-start(bf16[256,1536]{1,0:T(8,128)(2,1)} %get-tuple-element.1470), channel_id=1, source_target_pairs={{0,1},{1,0},{2,3},{3,2},{4,5},{5,4},{6,7},{7,6},{8,9},{9,8},{10,11... | collective-permute-start | bytes 2359304 | tf_op jit(solution)/shard_map/ppermute | solution.py:67
  551.1 23.4 %collective-permute-start.54 = (bf16[2,48,1792]{2,1,0:T(8,128)(2,1)}, bf16[2,48,1792]{2,1,0:T(8,128)(2,1)S(1)}, u32[]{:S(2)}, u32[]{:S(2)}) collective-permute-start(bf16[2,48,1792]{2,1,0:T(8,128)(2,1)} %get-tuple-element.1487), channel_id=1, source_target_pairs={{0,4},{2,6},{4,0},{6,2},{1,5},{3,7},{5,1},{7,3},{8,12},{10,14},{12... | collective-permute-start | bytes 1032200 | tf_op jit(solution)/shard_map/ppermute | solution.py:176
  552.6 21.9 %collective-permute-start.55 = (bf16[2,48,1792]{2,1,0:T(8,128)(2,1)}, bf16[2,48,1792]{2,1,0:T(8,128)(2,1)S(1)}, u32[]{:S(2)}, u32[]{:S(2)}) collective-permute-start(bf16[2,48,1792]{2,1,0:T(8,128)(2,1)} %get-tuple-element.1488), channel_id=1, source_target_pairs={{0,6},{2,0},{4,2},{6,4},{1,7},{3,1},{5,3},{7,5},{8,14},{10,8},{12,... | collective-permute-start | bytes 1032200 | tf_op jit(solution)/shard_map/ppermute | solution.py:176
  576.4 23.7 %collective-permute-start.63 = (f32[48,1792]{1,0:T(8,128)}, f32[48,1792]{1,0:T(8,128)S(1)}, u32[]{:S(2)}, u32[]{:S(2)}) collective-permute-start(f32[48,1792]{1,0:T(8,128)} %get-tuple-element.1537), channel_id=1, source_target_pairs={{0,8},{8,0},{1,9},{9,1},{2,10},{10,2},{3,11},{11,3},{4,12},{12,4},... | collective-permute-start | bytes 1032200 | tf_op jit(solution)/shard_map/ppermute | solution.py:67
  577.2 19.6 %collective-permute-start.62 = (f32[48,1536]{1,0:T(8,128)}, f32[48,1536]{1,0:T(8,128)}, u32[]{:S(2)}, u32[]{:S(2)}) collective-permute-start(f32[48,1536]{1,0:T(8,128)} %get-tuple-element.1543), channel_id=1, source_target_pairs={{0,8},{8,0},{1,9},{9,1},{2,10},{10,2},{3,11},{11,3},{4,12},{12,4},... | collective-permute-start | bytes 884744 | tf_op jit(solution)/shard_map/ppermute | solution.py:67
  579.7 32.4 %collective-permute-start.56 = (bf16[256,1536]{1,0:T(8,128)(2,1)}, bf16[256,1536]{1,0:T(8,128)(2,1)}, u32[]{:S(2)}, u32[]{:S(2)}) collective-permute-start(bf16[256,1536]{1,0:T(8,128)(2,1)} %get-tuple-element.1505), channel_id=1, source_target_pairs={{0,1},{1,0},{2,3},{3,2},{4,5},{5,4},{6,7},{7,6},{8,9},{9,8},{10,11... | collective-permute-start | bytes 2359304 | tf_op jit(solution)/shard_map/ppermute | solution.py:67
  (103 other events, 725.0 us)
